TPU v7x, 32 devices: a whole 2x2x4 slice. The times are simulated.
32 devices in a mesh: fsdp: 4 (over z), ctx: 8 (over y, x, core).
Axes of the slice: x: 2, y: 2, z: 4, core: 2. Of those that a mesh axis runs over, the one named last changes fastest.
Arguments:
- inputs: bfloat16 [4096, 2048], P(('fsdp', 'ctx')), may hold values from -6 to 6
- doc_lengths: int32 [4, 8], P('fsdp'), may hold values from 1 to 897, 1024 in all within a row
- gain_attn: bfloat16 [2048], P('fsdp'), may hold values from 0.25 to 1.75
- w_query: bfloat16 [2048, 2048], P('fsdp'), may hold values from -0.0625 to 0.0625
- w_key: bfloat16 [2048, 2048], P('fsdp'), may hold values from -0.0625 to 0.0625
- w_value: bfloat16 [2048, 2048], P('fsdp'), may hold values from -0.125 to 0.125
- w_out: bfloat16 [2048, 2048], P('fsdp'), may hold values from -0.5 to 0.5
- bias_table: bfloat16 [32, 32], replicated, may hold values from -4 to 4
- gain_ff: bfloat16 [2048], P('fsdp'), may hold values from 0.25 to 1.75
- w_gate: bfloat16 [2048, 5120], P('fsdp'), may hold values from -0.125 to 0.125
- w_up: bfloat16 [2048, 5120], P('fsdp'), may hold values from -0.125 to 0.125
- w_down: bfloat16 [5120, 2048], P('fsdp'), may hold values from -0.078125 to 0.078125
- cotangent: bfloat16 [4096, 2048], P(('fsdp', 'ctx')), may hold values from -6 to 6
Outputs:
- output: bfloat16 [4096, 2048], P(('fsdp', 'ctx'))
- input_grad: bfloat16 [4096, 2048], P(('fsdp', 'ctx'))
- attn_gain_grad: float32 [2048], P(('fsdp', 'ctx'))
- ff_gain_grad: float32 [2048], P(('fsdp', 'ctx'))
- query_weight_grad: float32 [2048, 2048], P(('fsdp', 'ctx'))
- key_weight_grad: float32 [2048, 2048], P(('fsdp', 'ctx'))
- value_weight_grad: float32 [2048, 2048], P(('fsdp', 'ctx'))
- out_weight_grad: float32 [2048, 2048], P(('fsdp', 'ctx'))
- bias_grad: float32 [1024], P(('fsdp', 'ctx'))
- gate_weight_grad: float32 [2048, 5120], P(('fsdp', 'ctx'))
- up_weight_grad: float32 [2048, 5120], P(('fsdp', 'ctx'))
- down_weight_grad: float32 [5120, 2048], P(('fsdp', 'ctx'))
Inputs may be any that keep to these rules, and one draw needn't show every extreme that they name: `doc_lengths`: each row lists the lengths of the documents packed in order into one sequence; they sum to 1024, and the longest is exactly 897 tokens.
All inputs are finite; a program needn't handle non-finite values.
Results may differ from a plain program's by a relative error of at most 0.019.
Values may be sent and summed in bfloat16 or wider, within the bound.
No kernel may reach another device: no remote copies, remote signals or barrier semaphores. Data moves between devices by JAX's collectives and lax.ppermute only.
A program may use at most 448 MiB of HBM per device.

v0:
```python
import jax
import jax.numpy as jnp
from jax import lax
from jax.sharding import PartitionSpec as P

H = 32
DH = 64
BUCKETS = 32


epsilon = 1e-06
score_masked_rows = -1000000000.0
bucket_edges = (12, 16, 23, 32, 46, 64, 91)


def passed_along(block, axis, distance):
    devices = range(lax.axis_size(axis))
    route = [((i - distance) % len(devices), i) for i in devices]
    return lax.ppermute(block, axis, route)


def bucket_index(offset):
    distance = jnp.abs(offset)
    far_bucket = BUCKETS // 4 + sum(
        ((distance >= boundary).astype(jnp.int32) for boundary in bucket_edges)
    )
    within = jnp.where(distance < BUCKETS // 4, distance, far_bucket)
    return within + BUCKETS // 2 * (offset > 0).astype(jnp.int32)


def rms_scale(values, gain_row):
    mean_square = jnp.mean(values * values, axis=-1, keepdims=True)
    return values * lax.rsqrt(mean_square + epsilon) * gain_row


def gated_mix(gate_part, up_part):
    return jax.nn.gelu(gate_part, approximate=True) * up_part


def segment_table(doc_row, total_rows):
    doc_ends = jnp.cumsum(doc_row)
    positions = jnp.arange(total_rows, dtype=jnp.int32)
    return jnp.sum((positions[:, None] >= doc_ends[None, :]).astype(jnp.int32), axis=1)


def part_width(total_rows):
    part_rows = total_rows
    while part_rows > 512 and part_rows % 2 == 0:
        part_rows = part_rows // 2
    return part_rows


def part_scores(shared, key_part, key_first):
    query_heads, query_first, bucket_table_entries, query_segment, segment_all = shared
    rows_here = query_heads.shape[0]
    key_count = key_part.shape[0]
    key_heads = key_part.reshape(key_count, H, DH)
    raw_scores = jnp.einsum(
        "qhd,khd->hqk", query_heads, key_heads, preferred_element_type=jnp.float32
    )
    key_index = key_first + jnp.arange(key_count, dtype=jnp.int32)
    query_index = query_first + jnp.arange(rows_here, dtype=jnp.int32)
    buckets = bucket_index(key_index[None, :] - query_index[:, None])
    bucket_indicator = (
        buckets[None, :, :] == jnp.arange(BUCKETS, dtype=jnp.int32)[:, None, None]
    ).astype(jnp.bfloat16)
    bias_portion = jnp.einsum(
        "pli,pa->ali", bucket_indicator, bucket_table_entries, preferred_element_type=jnp.float32
    )
    key_segment = lax.dynamic_slice_in_dim(segment_all, key_first, key_count, 0)
    same_doc = query_segment[:, None] == key_segment[None, :]
    return (
        jnp.where(same_doc[None], raw_scores + bias_portion, score_masked_rows),
        bucket_indicator,
    )


def per_device(
    inputs,
    doc_lengths,
    gain_attn,
    w_query,
    w_key,
    w_value,
    w_out,
    bias_table,
    gain_ff,
    w_gate,
    w_up,
    w_down,
    cotangent,
):
    blk_rows = inputs.shape[0]
    cycle_size = lax.axis_size("ctx")
    own_block = lax.axis_index("ctx")
    query_first = own_block * blk_rows
    segment_all = segment_table(doc_lengths[0], blk_rows * cycle_size)
    query_segment = lax.dynamic_slice_in_dim(segment_all, query_first, blk_rows, 0)
    attention_full = (
        lax.all_gather(gain_attn, "fsdp", axis=0, tiled=True),
        lax.all_gather(w_query, "fsdp", axis=0, tiled=True),
        lax.all_gather(w_key, "fsdp", axis=0, tiled=True),
        lax.all_gather(w_value, "fsdp", axis=0, tiled=True),
        lax.all_gather(w_out, "fsdp", axis=0, tiled=True),
    )
    gain_first, query_full, key_full, value_full, out_full = attention_full
    source = inputs.astype(jnp.float32)
    first_gain_float = gain_first.astype(jnp.float32)
    normed = rms_scale(source, first_gain_float).astype(jnp.bfloat16)
    query_rows = jnp.dot(normed, query_full, preferred_element_type=jnp.float32).astype(
        jnp.bfloat16
    )
    key_rows = jnp.dot(normed, key_full, preferred_element_type=jnp.float32).astype(jnp.bfloat16)
    value_rows = jnp.dot(normed, value_full, preferred_element_type=jnp.float32).astype(
        jnp.bfloat16
    )
    query_heads = query_rows.reshape(blk_rows, H, DH)
    shared = (query_heads, query_first, bias_table, query_segment, segment_all)
    stats_init = (
        jnp.full((H, blk_rows), score_masked_rows, jnp.float32),
        jnp.zeros((H, blk_rows), jnp.float32),
    )
    zero_rows = jnp.zeros((blk_rows, H * DH), jnp.float32)
    key_piece = lax.all_gather(key_rows, "ctx", axis=0, tiled=True)
    part_rows = part_width(key_piece.shape[0])

    def one_part(index_part, loop_state):
        row_max, row_sum = loop_state
        offset_rows = index_part * part_rows
        key_part = lax.dynamic_slice_in_dim(key_piece, offset_rows, part_rows, 0)
        scores = part_scores(shared, key_part, offset_rows)[0]
        new_max = jnp.maximum(row_max, jnp.max(scores, axis=-1))
        new_sum = row_sum * jnp.exp(row_max - new_max) + jnp.sum(
            jnp.exp(scores - new_max[..., None]), axis=-1
        )
        return (new_max, new_sum)

    row_max, row_sum = lax.fori_loop(0, key_piece.shape[0] // part_rows, one_part, stats_init)
    log_total = row_max + jnp.log(row_sum)
    fold_key_piece = lax.all_gather(key_rows, "ctx", axis=0, tiled=True)
    value_piece = lax.all_gather(value_rows, "ctx", axis=0, tiled=True)
    fold_part_rows = part_width(fold_key_piece.shape[0])

    def one_part(index_part, running):
        offset_rows = index_part * fold_part_rows
        key_part = lax.dynamic_slice_in_dim(fold_key_piece, offset_rows, fold_part_rows, 0)
        value_part = lax.dynamic_slice_in_dim(value_piece, offset_rows, fold_part_rows, 0)
        scores = part_scores(shared, key_part, offset_rows)[0]
        probabilities = jnp.exp(scores - log_total[..., None]).astype(jnp.bfloat16)
        value_heads = value_part.reshape(fold_part_rows, H, DH)
        term = jnp.einsum(
            "hqk,khd->qhd", probabilities, value_heads, preferred_element_type=jnp.float32
        )
        return running + term.reshape(blk_rows, H * DH)

    context_sum = lax.fori_loop(0, fold_key_piece.shape[0] // fold_part_rows, one_part, zero_rows)
    context = context_sum.astype(jnp.bfloat16)
    residual = source + jnp.dot(context, out_full, preferred_element_type=jnp.float32)
    feed_full = (
        lax.all_gather(gain_ff, "fsdp", axis=0, tiled=True),
        lax.all_gather(w_gate, "fsdp", axis=0, tiled=True),
        lax.all_gather(w_up, "fsdp", axis=0, tiled=True),
        lax.all_gather(w_down, "fsdp", axis=0, tiled=True),
    )
    gain_second, gate_full, up_full, down_full = feed_full
    gain_second_f = gain_second.astype(jnp.float32)
    normed_ff = rms_scale(residual, gain_second_f).astype(jnp.bfloat16)
    gate_pre = jnp.dot(normed_ff, gate_full, preferred_element_type=jnp.float32)
    up_pre = jnp.dot(normed_ff, up_full, preferred_element_type=jnp.float32)
    active = gated_mix(gate_pre, up_pre).astype(jnp.bfloat16)
    output = (residual + jnp.dot(active, down_full, preferred_element_type=jnp.float32)).astype(
        jnp.bfloat16
    )
    feed_full = (
        lax.all_gather(gain_ff, "fsdp", axis=0, tiled=True),
        lax.all_gather(w_gate, "fsdp", axis=0, tiled=True),
        lax.all_gather(w_up, "fsdp", axis=0, tiled=True),
        lax.all_gather(w_down, "fsdp", axis=0, tiled=True),
    )
    gain_second, gate_full, up_full, down_full = feed_full
    gain_second_f = gain_second.astype(jnp.float32)
    down_grad = jnp.einsum("tf,td->fd", active, cotangent, preferred_element_type=jnp.float32)
    active_grad = jnp.einsum("td,fd->tf", cotangent, down_full, preferred_element_type=jnp.float32)
    mix_back = jax.vjp(gated_mix, gate_pre, up_pre)[1]
    gate_grad, up_grad = mix_back(active_grad)
    gate_grad = gate_grad.astype(jnp.bfloat16)
    up_grad = up_grad.astype(jnp.bfloat16)
    gate_weight_grad = jnp.einsum(
        "td,tf->df", normed_ff, gate_grad, preferred_element_type=jnp.float32
    )
    up_weight_grad = jnp.einsum("td,tf->df", normed_ff, up_grad, preferred_element_type=jnp.float32)
    normed_ff_grad = jnp.einsum(
        "tf,df->td", gate_grad, gate_full, preferred_element_type=jnp.float32
    ) + jnp.einsum("tf,df->td", up_grad, up_full, preferred_element_type=jnp.float32)
    norm_back = jax.vjp(rms_scale, residual, gain_second_f)[1]
    residual_part, ff_gain_grad = norm_back(normed_ff_grad)
    residual_grad = cotangent.astype(jnp.float32) + residual_part
    feed_shards = (
        lax.psum_scatter(ff_gain_grad, ("fsdp", "ctx"), scatter_dimension=0, tiled=True),
        lax.psum_scatter(gate_weight_grad, ("fsdp", "ctx"), scatter_dimension=0, tiled=True),
        lax.psum_scatter(up_weight_grad, ("fsdp", "ctx"), scatter_dimension=0, tiled=True),
        lax.psum_scatter(down_grad, ("fsdp", "ctx"), scatter_dimension=0, tiled=True),
    )
    attention_full = (
        lax.all_gather(gain_attn, "fsdp", axis=0, tiled=True),
        lax.all_gather(w_query, "fsdp", axis=0, tiled=True),
        lax.all_gather(w_key, "fsdp", axis=0, tiled=True),
        lax.all_gather(w_value, "fsdp", axis=0, tiled=True),
        lax.all_gather(w_out, "fsdp", axis=0, tiled=True),
    )
    gain_first, query_full, key_full, value_full, out_full = attention_full
    first_gain_float = gain_first.astype(jnp.float32)
    residual_low = residual_grad.astype(jnp.bfloat16)
    out_weight_grad = jnp.einsum(
        "td,te->de", context, residual_low, preferred_element_type=jnp.float32
    )
    context_grad = jnp.einsum(
        "te,de->td", residual_low, out_full, preferred_element_type=jnp.float32
    ).astype(jnp.bfloat16)
    context_heads = context_grad.reshape(blk_rows, H, DH)
    row_delta = jnp.transpose(
        jnp.sum((context_grad.astype(jnp.float32) * context_sum).reshape(blk_rows, H, DH), axis=-1)
    )

    def back_part(key_part, value_part, key_first):
        key_count = key_part.shape[0]
        scores, bucket_indicator = part_scores(shared, key_part, key_first)
        probabilities = jnp.exp(scores - log_total[..., None])
        key_heads = key_part.reshape(key_count, H, DH)
        value_heads = value_part.reshape(key_count, H, DH)
        prob_grad = jnp.einsum(
            "qhd,khd->hqk", context_heads, value_heads, preferred_element_type=jnp.float32
        )
        score_gradient = (probabilities * (prob_grad - row_delta[..., None])).astype(jnp.bfloat16)
        query_term = jnp.einsum(
            "hqk,khd->qhd", score_gradient, key_heads, preferred_element_type=jnp.float32
        )
        key_term = jnp.einsum(
            "hqk,qhd->khd", score_gradient, query_heads, preferred_element_type=jnp.float32
        )
        value_term = jnp.einsum(
            "hqk,qhd->khd",
            probabilities.astype(jnp.bfloat16),
            context_heads,
            preferred_element_type=jnp.float32,
        )
        bias_term = jnp.einsum(
            "nmz,fmz->nf", bucket_indicator, score_gradient, preferred_element_type=jnp.float32
        )
        return (
            query_term.reshape(blk_rows, H * DH),
            key_term.reshape(key_count, H * DH),
            value_term.reshape(key_count, H * DH),
            bias_term,
        )

    zero_bias = jnp.zeros((BUCKETS, H), jnp.float32)

    def add_block(turn_index, pair_block, grad_block, query_sum, bias_sum):
        key_first = (own_block - turn_index) % cycle_size * blk_rows
        query_term, key_term, value_term, bias_term = back_part(
            pair_block[0], pair_block[1], key_first
        )
        return (
            grad_block + jnp.stack((key_term, value_term)),
            query_sum + query_term,
            bias_sum + bias_term,
        )

    def pass_grads(grad_block):
        return passed_along(grad_block.astype(jnp.bfloat16), "ctx", 1).astype(grad_block.dtype)

    def rotation_step(turn_index, loop_state):
        pair_block, grad_block, query_sum, bias_sum = loop_state
        grad_block, query_sum, bias_sum = add_block(
            turn_index, pair_block, grad_block, query_sum, bias_sum
        )
        pair_block = passed_along(pair_block, "ctx", 1)
        return (pair_block, pass_grads(grad_block), query_sum, bias_sum)

    loop_state = lax.fori_loop(
        0,
        cycle_size - 1,
        rotation_step,
        (
            jnp.stack((key_rows, value_rows)),
            jnp.zeros((2, blk_rows, H * DH), jnp.float32),
            zero_rows,
            zero_bias,
        ),
    )
    pair_block, grad_block, query_sum, bias_sum = loop_state
    grad_block, query_sum, bias_sum = add_block(
        cycle_size - 1, pair_block, grad_block, query_sum, bias_sum
    )
    pair_grads = pass_grads(grad_block)
    query_low = query_sum.astype(jnp.bfloat16)
    key_low = pair_grads[0].astype(jnp.bfloat16)
    value_low = pair_grads[1].astype(jnp.bfloat16)
    query_weight_grad = jnp.einsum(
        "td,te->de", normed, query_low, preferred_element_type=jnp.float32
    )
    key_weight_grad = jnp.einsum("td,te->de", normed, key_low, preferred_element_type=jnp.float32)
    value_weight_grad = jnp.einsum(
        "td,te->de", normed, value_low, preferred_element_type=jnp.float32
    )
    normed_grad = (
        jnp.einsum("te,de->td", query_low, query_full, preferred_element_type=jnp.float32)
        + jnp.einsum("te,de->td", key_low, key_full, preferred_element_type=jnp.float32)
        + jnp.einsum("te,de->td", value_low, value_full, preferred_element_type=jnp.float32)
    )
    first_back = jax.vjp(rms_scale, source, first_gain_float)[1]
    source_part, attn_gain_grad = first_back(normed_grad)
    input_grad = (residual_grad + source_part).astype(jnp.bfloat16)
    attention_shards = (
        lax.psum_scatter(attn_gain_grad, ("fsdp", "ctx"), scatter_dimension=0, tiled=True),
        lax.psum_scatter(query_weight_grad, ("fsdp", "ctx"), scatter_dimension=0, tiled=True),
        lax.psum_scatter(key_weight_grad, ("fsdp", "ctx"), scatter_dimension=0, tiled=True),
        lax.psum_scatter(value_weight_grad, ("fsdp", "ctx"), scatter_dimension=0, tiled=True),
        lax.psum_scatter(out_weight_grad, ("fsdp", "ctx"), scatter_dimension=0, tiled=True),
        lax.psum_scatter(
            bias_sum.reshape(BUCKETS * H), ("fsdp", "ctx"), scatter_dimension=0, tiled=True
        ),
    )
    return (
        output,
        input_grad,
        attention_shards[0],
        feed_shards[0],
        attention_shards[1],
        attention_shards[2],
        attention_shards[3],
        attention_shards[4],
        attention_shards[5],
        feed_shards[1],
        feed_shards[2],
        feed_shards[3],
    )


def solution(mesh):
    placed = (
        P(("fsdp", "ctx"), None),
        P("fsdp", None),
        P("fsdp"),
        P("fsdp", None),
        P("fsdp", None),
        P("fsdp", None),
        P("fsdp", None),
        P(),
        P("fsdp"),
        P("fsdp", None),
        P("fsdp", None),
        P("fsdp", None),
        P(("fsdp", "ctx"), None),
    )
    return jax.shard_map(
        per_device,
        mesh=mesh,
        in_specs=placed,
        out_specs=(
            P(("fsdp", "ctx"), None),
            P(("fsdp", "ctx"), None),
            P(("fsdp", "ctx")),
            P(("fsdp", "ctx")),
            P(("fsdp", "ctx"), None),
            P(("fsdp", "ctx"), None),
            P(("fsdp", "ctx"), None),
            P(("fsdp", "ctx"), None),
            P(("fsdp", "ctx")),
            P(("fsdp", "ctx"), None),
            P(("fsdp", "ctx"), None),
            P(("fsdp", "ctx"), None),
        ),
        check_vma=False,
    )
```

profile of v0, /device:TPU:0, one launch (start us, length us, event | category | flops | bytes accessed | tf_op | source)
XLA Modules:
  0.0 4159.0 jit_solution(6838536795883676030)
XLA Ops:
  9.5 13.5 all-gather
  23.3 138.7 %all-gather.16.cloned.1.call-done = bf16[2048,2048]{1,0:T(8,128)(2,1)} async-done(((bf16[512,2048]{1,0:T(8,128)(2,1)}), bf16[2048,2048]{1,0:T(8,128)(2,1)}) %all-gather.16.cloned.1.call-update) | async-done | bytes 8388624 | tf_op jit(solution)/shard_map/all_gather | solution.py:102
  167.5 143.9 %all-gather.12.cloned.1.call-done = bf16[2048,2048]{1,0:T(8,128)(2,1)} async-done(((bf16[512,2048]{1,0:T(8,128)(2,1)}), bf16[2048,2048]{1,0:T(8,128)(2,1)}) %all-gather.12.cloned.1.call-update) | async-done | bytes 8388624 | tf_op jit(solution)/shard_map/all_gather | solution.py:103
  320.2 15.3 all-gather.1
  339.6 121.5 %all-gather.20.cloned.1.call-done = bf16[2048,2048]{1,0:T(8,128)(2,1)} async-done(((bf16[512,2048]{1,0:T(8,128)(2,1)}), bf16[2048,2048]{1,0:T(8,128)(2,1)}) %all-gather.20.cloned.1.call-update) | async-done | bytes 8388624 | tf_op jit(solution)/shard_map/all_gather | solution.py:101
  469.4 28.8 all-gather.18.cloned.1.call-done
  504.7 62.0 %while.52 = (s32[]{:T(128)}, f32[32,128]{1,0:T(8,128)S(1)}, f32[32,128]{1,0:T(8,128)S(1)}, s32[128]{0:T(128)S(1)}, s32[1024]{0:T(1024)S(1)}, /*index=5*/bf16[102...) while((s32[]{:T(128)}, f32[32,128]{1,0:T(8,128)S(1)}, ...), condition=%wide.region_6.7_spmd.clone, body=%wide.region_3.6_spmd.clone.sunk | while | flops 417157760 | bytes 58029768 | solution.py:138
  566.7 63.8 %while.53 = (s32[]{:T(128)}, f32[128,2048]{0,1:T(8,128)}, bf16[1024,2048]{1,0:T(8,128)(2,1)}, s32[128]{0:T(128)S(1)}, s32[1024]{0:T(1024)S(1)}, /*index=5*/bf16[...) while((s32[]{:T(128)}, f32[128,2048]{0,1:T(8,128)}, ...), condition=%wide.region_8.9_spmd.clone, body=%wide.region_7.8_spmd.clone.sunk | while | flops 683999872 | bytes 64124688 | solution.py:156
  633.2 55.2 %all-gather.22.cloned.1.call-done = bf16[2048,2048]{1,0:T(8,128)(2,1)} async-done(((bf16[512,2048]{1,0:T(8,128)(2,1)}), bf16[2048,2048]{1,0:T(8,128)(2,1)}) %all-gather.22.cloned.1.call-update) | async-done | bytes 8388624 | tf_op jit(solution)/shard_map/all_gather | solution.py:104
  693.4 351.7 %all-gather.24.cloned.1.call-done = bf16[2048,5120]{1,0:T(8,128)(2,1)} async-done(((bf16[512,5120]{1,0:T(8,128)(2,1)}), bf16[2048,5120]{1,0:T(8,128)(2,1)}) %all-gather.24.cloned.1.call-update) | async-done | bytes 20971536 | tf_op jit(solution)/shard_map/all_gather | solution.py:161
  1056.8 345.3 %all-gather.26.cloned.1.call-done = bf16[2048,5120]{1,0:T(8,128)(2,1)} async-done(((bf16[512,5120]{1,0:T(8,128)(2,1)}), bf16[2048,5120]{1,0:T(8,128)(2,1)}) %all-gather.26.cloned.1.call-update) | async-done | bytes 20971536 | tf_op jit(solution)/shard_map/all_gather | solution.py:162
  1413.9 345.3 %all-gather.28.cloned.1.call-done = bf16[5120,2048]{1,0:T(8,128)(2,1)} async-done(((bf16[1280,2048]{1,0:T(8,128)(2,1)}), bf16[5120,2048]{1,0:T(8,128)(2,1)}) %all-gather.28.cloned.1.call-update) | async-done | bytes 20971536 | tf_op jit(solution)/shard_map/all_gather | solution.py:163
  1759.2 14.3 multiply_convert_fusion.1
  1785.8 13.7 multiply_reduce_fusion
  1808.2 221.9 %while.54 = (s32[]{:T(128)}, bf16[2,128,2048]{1,2,0:T(8,128)(2,1)}, f32[2,128,2048]{1,2,0:T(8,128)}, f32[128,2048]{0,1:T(8,128)}, f32[32,32]{1,0:T(8,128)S(1)}, ...) while((s32[]{:T(128)}, bf16[2,128,2048]{1,2,0:T(8,128)(2,1)}, ...), condition=%wide.region_13.14_spmd.clone, body=%wide.region_12.13_spmd.clone.sunk | while | flops 410994944 | bytes 58472980 | solution.py:281
  1823.9 13.4 collective-permute-done.1
  1886.9 13.7 collective-permute-done.1
  1918.6 13.8 collective-permute-done.1
  1950.3 13.8 collective-permute-done.1
  1981.9 13.8 collective-permute-done.1
  2013.6 13.7 collective-permute-done.1
  2060.3 39.1 collective-permute-done.2
  2117.5 16.7 fusion.126
  2135.6 16.7 fusion.127
  2153.7 16.8 fusion.128
  2196.4 40.5 all-reduce.3
  2239.8 187.1 %reduce-scatter.14.cloned.1.call-done = f32[64,2048]{1,0:T(8,128)} async-done(((f32[2048,2048]{1,0:T(8,128)}), f32[64,2048]{1,0:T(8,128)}) %reduce-scatter.14.cloned.1.call-update) | async-done | bytes 524304 | tf_op jit(solution)/shard_map/reduce_scatter | solution.py:320
  2426.9 187.0 %reduce-scatter.10.cloned.1.call-done = f32[64,2048]{1,0:T(8,128)} async-done(((f32[2048,2048]{1,0:T(8,128)}), f32[64,2048]{1,0:T(8,128)}) %reduce-scatter.10.cloned.1.call-update) | async-done | bytes 524304 | tf_op jit(solution)/shard_map/reduce_scatter | solution.py:318
  2613.9 188.1 %reduce-scatter.12.cloned.1.call-done = f32[64,2048]{1,0:T(8,128)} async-done(((f32[2048,2048]{1,0:T(8,128)}), f32[64,2048]{1,0:T(8,128)}) %reduce-scatter.12.cloned.1.call-update) | async-done | bytes 524304 | tf_op jit(solution)/shard_map/reduce_scatter | solution.py:319
  2802.1 445.7 %reduce-scatter.16.cloned.1.call-done = f32[64,5120]{1,0:T(8,128)} async-done(((f32[2048,5120]{1,0:T(8,128)}), f32[64,5120]{1,0:T(8,128)}) %reduce-scatter.16.cloned.1.call-update) | async-done | bytes 1310736 | tf_op jit(solution)/shard_map/reduce_scatter | solution.py:200
  3247.8 452.3 %reduce-scatter.18.cloned.1.call-done = f32[64,5120]{1,0:T(8,128)} async-done(((f32[2048,5120]{1,0:T(8,128)}), f32[64,5120]{1,0:T(8,128)}) %reduce-scatter.18.cloned.1.call-update) | async-done | bytes 1310736 | tf_op jit(solution)/shard_map/reduce_scatter | solution.py:201
  3700.1 452.3 %reduce-scatter.20.cloned.1.call-done = f32[160,2048]{1,0:T(8,128)} async-done(((f32[5120,2048]{1,0:T(8,128)}), f32[160,2048]{1,0:T(8,128)}) %reduce-scatter.20.cloned.1.call-update) | async-done | bytes 1310736 | tf_op jit(solution)/shard_map/reduce_scatter | solution.py:202
  (451 shorter events, 431.0 us)
Async XLA Ops:
  7.2 154.8 %all-gather.16.cloned.1.call-start = ((), (), s32[]{:S(2)}) async-start(), calls=%async_computation.9 | async-start | bytes 10485760 | tf_op jit(solution)/shard_map/all_gather | solution.py:102
  7.9 303.5 %all-gather.12.cloned.1.call-start = ((), (), s32[]{:S(2)}) async-start(), calls=%async_computation.7 | async-start | bytes 10485760 | tf_op jit(solution)/shard_map/all_gather | solution.py:103
  8.7 452.4 %all-gather.20.cloned.1.call-start = ((), (), s32[]{:S(2)}) async-start(), calls=%async_computation.11 | async-start | bytes 10485760 | tf_op jit(solution)/shard_map/all_gather | solution.py:101
  9.4 488.9 %all-gather.18.cloned.1.call-start = ((), (), s32[]{:S(2)}) async-start(), calls=%async_computation.10 | async-start | bytes 4718592 | tf_op jit(solution)/shard_map/all_gather | solution.py:140
  167.5 399.3 %all-gather.14.cloned.1.call-start = ((), (), s32[]{:S(2)}) async-start(), calls=%async_computation.8 | async-start | bytes 4718592 | tf_op jit(solution)/shard_map/all_gather | solution.py:141
  316.9 371.5 %all-gather.22.cloned.1.call-start = ((), (), s32[]{:S(2)}) async-start(), calls=%async_computation.12 | async-start | bytes 10485760 | tf_op jit(solution)/shard_map/all_gather | solution.py:104
  317.5 727.6 %all-gather.24.cloned.1.call-start = ((), (), s32[]{:S(2)}) async-start(), calls=%async_computation.13 | async-start | bytes 26214400 | tf_op jit(solution)/shard_map/all_gather | solution.py:161
  318.3 1083.9 %all-gather.26.cloned.1.call-start = ((), (), s32[]{:S(2)}) async-start(), calls=%async_computation.14 | async-start | bytes 26214400 | tf_op jit(solution)/shard_map/all_gather | solution.py:162
  319.0 1440.2 %all-gather.28.cloned.1.call-start = ((), (), s32[]{:S(2)}) async-start(), calls=%async_computation.15 | async-start | bytes 26214400 | tf_op jit(solution)/shard_map/all_gather | solution.py:163
  319.8 1920.0 %reduce-scatter.8.cloned.1.call-start = ((), (), s32[]{:S(2)}) async-start(), calls=%async_computation.16 | async-start | bytes 17301504 | tf_op jit(solution)/shard_map/reduce_scatter | solution.py:317
  693.4 708.8 %copy-start.18 = (bf16[128,2048]{1,0:T(8,128)(2,1)}, bf16[128,2048]{1,0:T(8,128)(2,1)S(1)}, u32[]{:S(2)}) copy-start(bf16[128,2048]{1,0:T(8,128)(2,1)S(1)} %multiply_convert_fusion.4) | copy-start | bytes 1572868
  1810.7 29.3 collective-permute-start
  1819.5 17.9 collective-permute-start.1
  1842.3 29.3 collective-permute-start
  1851.1 17.9 collective-permute-start.1
  1874.0 29.3 collective-permute-start
  1882.8 17.9 collective-permute-start.1
  1905.7 29.3 collective-permute-start
  1914.5 17.9 collective-permute-start.1
  1937.3 29.3 collective-permute-start
  1946.1 17.9 collective-permute-start.1
  1969.0 29.3 collective-permute-start
  1977.8 17.9 collective-permute-start.1
  2000.7 29.3 collective-permute-start
  2009.5 17.9 collective-permute-start.1
  2045.5 381.4 %reduce-scatter.14.cloned.1.call-start = ((), (), s32[]{:S(2)}) async-start(), calls=%async_computation.19 | async-start | bytes 17301504 | tf_op jit(solution)/shard_map/reduce_scatter | solution.py:320
  2056.1 557.9 %reduce-scatter.10.cloned.1.call-start = ((), (), s32[]{:S(2)}) async-start(), calls=%async_computation.17 | async-start | bytes 17301504 | tf_op jit(solution)/shard_map/reduce_scatter | solution.py:318
  2060.2 39.1 collective-permute-start.2
  2107.6 694.4 %reduce-scatter.12.cloned.1.call-start = ((), (), s32[]{:S(2)}) async-start(), calls=%async_computation.18 | async-start | bytes 17301504 | tf_op jit(solution)/shard_map/reduce_scatter | solution.py:319
  2116.1 1131.7 %reduce-scatter.16.cloned.1.call-start = ((), (), s32[]{:S(2)}) async-start(), calls=%async_computation.20 | async-start | bytes 43253760 | tf_op jit(solution)/shard_map/reduce_scatter | solution.py:200
  2134.3 1565.8 %reduce-scatter.18.cloned.1.call-start = ((), (), s32[]{:S(2)}) async-start(), calls=%async_computation.21 | async-start | bytes 43253760 | tf_op jit(solution)/shard_map/reduce_scatter | solution.py:201
  2152.3 2000.0 %reduce-scatter.20.cloned.1.call-start = ((), (), s32[]{:S(2)}) async-start(), calls=%async_computation.22 | async-start | bytes 43253760 | tf_op jit(solution)/shard_map/reduce_scatter | solution.py:202
  (78 other events, 3141.1 us)
Sparse Core Ops, SparseCore 0:
  9.6 152.3 all-gather.15
  163.5 147.8 all-gather.11
  313.0 148.0 all-gather.19
  463.4 34.8 all-gather.17
  500.6 36.7 all-gather.13
  538.8 149.6 all-gather.21
  690.0 355.0 all-gather.23
  1046.7 355.4 all-gather.25
  1403.8 355.4 all-gather.27
  2045.6 193.3 reduce-scatter.7
  2241.8 185.0 reduce-scatter.13
  2429.6 184.2 reduce-scatter.9
  2616.8 185.2 reduce-scatter.11
  2804.8 442.9 reduce-scatter.15
  3250.5 449.5 reduce-scatter.17
  3702.8 449.4 reduce-scatter.19
where the time goes:
time: 4170 us; the launch traced here: 4160 us
  waiting for transfers between devices  3580 us (86%)
  matrix products  300 us (7%)
  local copies, waits for them, and re-layouts  124 us (3%)
  blocking collectives  69.3 us (2%)
  other arithmetic  64 us (2%)
    reduce_scatter x1, waiting for transfers between devices, per_device(): lax.psum_scatter(up_weight_grad, ('fsdp', 'ctx'), scatter_dimension=0, ti...  452 us
    reduce_scatter x1, waiting for transfers between devices, per_device(): lax.psum_scatter(down_grad, ('fsdp', 'ctx'), scatter_dimension=0, tiled=T...  452 us
    reduce_scatter x1, waiting for transfers between devices, per_device(): lax.psum_scatter(gate_weight_grad, ('fsdp', 'ctx'), scatter_dimension=0,...  446 us
    all_gather x1, waiting for transfers between devices, per_device(): lax.all_gather(w_gate, 'fsdp', axis=0, tiled=True)  352 us
    all_gather x1, waiting for transfers between devices, per_device(): lax.all_gather(w_down, 'fsdp', axis=0, tiled=True)  345 us
    all_gather x1, waiting for transfers between devices, per_device(): lax.all_gather(w_up, 'fsdp', axis=0, tiled=True)  345 us
    reduce_scatter x1, waiting for transfers between devices, per_device(): lax.psum_scatter(value_weight_grad, ('fsdp', 'ctx'), scatter_dimension=0,...  188 us
    reduce_scatter x1, waiting for transfers between devices, per_device(): lax.psum_scatter(out_weight_grad, ('fsdp', 'ctx'), scatter_dimension=0, t...  187 us
  transfers between devices with their start and end apart: 31, of which 22 were waited for; matrix products, arithmetic and copies ran while one was open for 9% of the time, Pallas kernels for 0%

commit v1 on v0

v1 whole, which is shorter than its diff:
```python
import functools

import jax
import jax.numpy as jnp
from jax import lax
from jax.experimental import pallas as pl
from jax.experimental.pallas import tpu as pltpu
from jax.sharding import PartitionSpec as P

H = 32
DH = 64
BUCKETS = 32
TILE = 128
PAIR = 2
CLASSES = 5

epsilon = 1e-06
score_masked_rows = -1000000000.0
bucket_edges = (12, 16, 23, 32, 46, 64, 91)
f32 = jnp.float32
bf16 = jnp.bfloat16
NT = (((1,), (1,)), ((), ()))
VMEM_BYTES = 56 * 1024 * 1024


def bucket_index(offset):
    distance = jnp.abs(offset)
    far_bucket = BUCKETS // 4 + sum(
        ((distance >= boundary).astype(jnp.int32) for boundary in bucket_edges)
    )
    within = jnp.where(distance < BUCKETS // 4, distance, far_bucket)
    return within + BUCKETS // 2 * (offset > 0).astype(jnp.int32)


def rms_scale(values, gain_row):
    mean_square = jnp.mean(values * values, axis=-1, keepdims=True)
    return values * lax.rsqrt(mean_square + epsilon) * gain_row


def gated_mix(gate_part, up_part):
    return jax.nn.gelu(gate_part, approximate=True) * up_part


def segment_table(doc_row, total_rows):
    doc_ends = jnp.cumsum(doc_row)
    positions = jnp.arange(total_rows, dtype=jnp.int32)
    return jnp.sum((positions[:, None] >= doc_ends[None, :]).astype(jnp.int32), axis=1)


def dot(left, right, contract=((1,), (0,))):
    return lax.dot_general(left, right, (contract, ((), ())), preferred_element_type=f32)


def swap(block, mask):
    return lax.ppermute(block, "ctx", [(i, i ^ mask) for i in range(lax.axis_size("ctx"))])


def by_exchange():
    return lax.axis_size("ctx") == 8


def plane_gather(block):
    if not by_exchange():
        return lax.all_gather(block, "ctx", axis=0, tiled=True)
    half = block.shape[0] // 2
    from_x, from_y, from_core = swap(block, 2), swap(block, 4), swap(block, 1)
    diagonal = jnp.concatenate([swap(from_x[:half], 4), swap(from_y[half:], 2)], axis=0)
    x_core, y_core = swap(from_x, 1), swap(from_y, 1)
    return jnp.concatenate(
        [block, from_core, from_x, x_core, from_y, y_core, diagonal, swap(diagonal, 1)], axis=0
    )


def plane_scatter(partial):
    if not by_exchange():
        return lax.psum_scatter(partial, "ctx", scatter_dimension=0, tiled=True).astype(f32)
    rows = partial.shape[0] // 8
    half = rows // 2

    def slot(m):
        return partial[m * rows : (m + 1) * rows]

    def chip(m):
        return slot(m).astype(f32) + swap(slot(m + 1), 1).astype(f32)

    diagonal = chip(6).astype(bf16)
    via_x, via_y = swap(diagonal[:half], 2), swap(diagonal[half:], 4)
    y_sum, x_sum = chip(4), chip(2)
    y_sum = jnp.concatenate([y_sum[:half] + via_x.astype(f32), y_sum[half:]], axis=0)
    x_sum = jnp.concatenate([x_sum[:half], x_sum[half:] + via_y.astype(f32)], axis=0)
    return chip(0) + swap(x_sum.astype(bf16), 2).astype(f32) + swap(y_sum.astype(bf16), 4).astype(f32)


def line_gather(small):
    parts = lax.axis_size("fsdp")
    own = lax.axis_index("fsdp")
    whole = jnp.zeros((parts,) + small.shape, small.dtype)
    for step in range(parts):
        piece = (
            small
            if step == 0
            else lax.ppermute(small, "fsdp", [(i, (i + step) % parts) for i in range(parts)])
        )
        whole = lax.dynamic_update_index_in_dim(whole, piece, (own - step) % parts, 0)
    return jnp.transpose(whole, (1, 0, 2)).reshape(small.shape[0], -1)


def tiles_kernel(table_ref, out_ref):
    heads = out_ref.shape[0]
    row = lax.broadcasted_iota(jnp.int32, (TILE, TILE), 0)
    column = lax.broadcasted_iota(jnp.int32, (TILE, TILE), 1)

    def one_head(h, _):
        for kind in range(CLASSES):
            bucket = bucket_index(row - column + (kind - 2) * TILE)
            first, last = (0, BUCKETS // 2) if kind < 2 else (BUCKETS // 2, BUCKETS)
            if kind == 2:
                first = 0
            tile = jnp.zeros((TILE, TILE), f32)
            for b in range(first, last):
                tile = jnp.where(bucket == b, table_ref[b, h], tile)
            out_ref[h, kind] = tile
        return 0

    lax.fori_loop(0, heads, one_head, 0)


def bias_tiles(table):
    heads = table.shape[1]
    return pl.pallas_call(
        tiles_kernel,
        out_shape=jax.ShapeDtypeStruct((heads, CLASSES, TILE, TILE), f32),
        in_specs=[pl.BlockSpec(memory_space=pltpu.SMEM)],
        out_specs=pl.BlockSpec(memory_space=pltpu.VMEM),
        name="bias_tiles",
    )(table)


def fold(tile, reduce):
    return reduce(tile.reshape(TILE // 8, 8, TILE), axis=0)


def tile_class(base, key_slot, query_slot):
    difference = lax.bitwise_xor(base, key_slot) - lax.bitwise_xor(base, query_slot)
    return jnp.clip(difference, -2, 2) + 2


def score_tile(base, h, a, i, q_i, k_ref, seg_keys, seg_i, tiles_ref):
    s = lax.dot_general(
        k_ref[a * TILE : (a + 1) * TILE, h * DH : (h + 1) * DH], q_i, NT, preferred_element_type=f32
    )
    kind = tile_class(base, jnp.int32(a), i)
    s = s + tiles_ref[h, kind]
    return jnp.where(seg_keys[a * TILE : (a + 1) * TILE, :] == seg_i, s, score_masked_rows), kind


def forward_kernel(base_ref, q_ref, k_ref, v_ref, segk_ref, segq_ref, tiles_ref, ctx_ref, log_ref, s_scr, p_scr):
    blocks = q_ref.shape[0] // TILE
    base = base_ref[0]
    for h in range(PAIR):
        v_t = v_ref[:, h * DH : (h + 1) * DH].astype(f32).T.astype(bf16)

        def one_block(i, _, h=h, v_t=v_t):
            start = pl.multiple_of(i * TILE, TILE)
            q_i = q_ref[pl.ds(start, TILE), h * DH : (h + 1) * DH]
            seg_i = segq_ref[pl.ds(i, 1), :]
            top = jnp.full((8, TILE), -jnp.inf, f32)
            for a in range(blocks):
                s, _ = score_tile(base, h, a, i, q_i, k_ref, segk_ref, seg_i, tiles_ref)
                s_scr[a * TILE : (a + 1) * TILE, :] = s
                top = jnp.maximum(top, fold(s, jnp.max))
            top = jnp.max(top, axis=0, keepdims=True)
            total = jnp.zeros((8, TILE), f32)
            for a in range(blocks):
                e = jnp.exp(s_scr[a * TILE : (a + 1) * TILE, :] - top)
                p_scr[a * TILE : (a + 1) * TILE, :] = e.astype(bf16)
                total = total + fold(e, jnp.sum)
            total = jnp.sum(total, axis=0, keepdims=True)
            context = lax.dot_general(
                v_t, p_scr[...], (((1,), (0,)), ((), ())), preferred_element_type=f32
            )
            ctx_ref[h * DH : (h + 1) * DH, pl.ds(start, TILE)] = (context / total).astype(bf16)
            log_ref[0, h, pl.ds(i, 1), :] = top + jnp.log(total)
            return 0

        lax.fori_loop(0, blocks, one_block, 0)


def attend(base, q, k, v, seg_keys, seg_queries, tiles):
    rows, width = q.shape
    pairs, blocks = width // (PAIR * DH), rows // TILE
    one_pair = pl.BlockSpec((rows, PAIR * DH), lambda j: (0, j))
    return pl.pallas_call(
        forward_kernel,
        grid=(pairs,),
        out_shape=(
            jax.ShapeDtypeStruct((width, rows), bf16),
            jax.ShapeDtypeStruct((pairs, PAIR, blocks, TILE), f32),
        ),
        in_specs=[
            pl.BlockSpec(memory_space=pltpu.SMEM),
            one_pair,
            one_pair,
            one_pair,
            pl.BlockSpec((rows, TILE), lambda j: (0, 0)),
            pl.BlockSpec((blocks, TILE), lambda j: (0, 0)),
            pl.BlockSpec((PAIR, CLASSES, TILE, TILE), lambda j: (j, 0, 0, 0)),
        ],
        out_specs=(
            pl.BlockSpec((PAIR * DH, rows), lambda j: (j, 0)),
            pl.BlockSpec((1, PAIR, blocks, TILE), lambda j: (j, 0, 0, 0)),
        ),
        scratch_shapes=[pltpu.VMEM((rows, TILE), f32), pltpu.VMEM((rows, TILE), bf16)],
        compiler_params=pltpu.CompilerParams(vmem_limit_bytes=VMEM_BYTES),
        name="attend_forward",
    )(base, q, k, v, seg_keys, seg_queries, tiles)


def backward_kernel(
    base_ref, q_ref, k_ref, v_ref, do_ref, log_ref, segk_ref, segq_ref, tiles_ref,
    dq_ref, dk_ref, dv_ref, bias_ref,
    p_scr, dp_scr, p_all, ds_all, near,
):
    rows = q_ref.shape[0]
    blocks = rows // TILE
    base = base_ref[0]
    row = lax.broadcasted_iota(jnp.int32, (TILE, TILE), 0)
    column = lax.broadcasted_iota(jnp.int32, (TILE, TILE), 1)
    for h in range(PAIR):
        lanes = slice(h * DH, (h + 1) * DH)
        near[...] = jnp.zeros_like(near)

        def one_block(i, _, h=h, lanes=lanes):
            start = pl.multiple_of(i * TILE, TILE)
            q_i = q_ref[pl.ds(start, TILE), lanes]
            do_i = do_ref[pl.ds(start, TILE), lanes]
            seg_i = segq_ref[pl.ds(i, 1), :]
            log_i = log_ref[0, h, pl.ds(i, 1), :]
            delta = jnp.zeros((8, TILE), f32)
            for a in range(blocks):
                here = slice(a * TILE, (a + 1) * TILE)
                s, _ = score_tile(base, h, a, i, q_i, k_ref, segk_ref, seg_i, tiles_ref)
                p = jnp.exp(s - log_i)
                dp = lax.dot_general(v_ref[here, lanes], do_i, NT, preferred_element_type=f32)
                delta = delta + fold(p * dp, jnp.sum)
                p_scr[here, :] = p
                dp_scr[here, :] = dp
                p_all[here, pl.ds(start, TILE)] = p.astype(bf16)
            delta = jnp.sum(delta, axis=0, keepdims=True)
            for a in range(blocks):
                here = slice(a * TILE, (a + 1) * TILE)
                ds = (p_scr[here, :] * (dp_scr[here, :] - delta)).astype(bf16)
                ds_all[here, pl.ds(start, TILE)] = ds
                kind = tile_class(base, jnp.int32(a), i)
                near[kind] = near[kind] + ds.astype(f32)
            return 0

        lax.fori_loop(0, blocks, one_block, 0)
        q_h, do_h = q_ref[:, lanes], do_ref[:, lanes]
        k_t = k_ref[:, lanes].astype(f32).T.astype(bf16)

        def products(a, _, lanes=lanes, q_h=q_h, do_h=do_h, k_t=k_t, h=h):
            here = pl.ds(pl.multiple_of(a * 2 * TILE, 2 * TILE), 2 * TILE)
            dv_ref[here, lanes] = jnp.dot(p_all[here, :], do_h, preferred_element_type=f32).astype(bf16)
            dk_ref[here, lanes] = jnp.dot(ds_all[here, :], q_h, preferred_element_type=f32).astype(bf16)
            dq_ref[lanes, here] = jnp.dot(k_t, ds_all[:, here], preferred_element_type=f32).astype(bf16)
            return 0

        lax.fori_loop(0, blocks // 2, products, 0)
        for b in range(BUCKETS):
            part = jnp.zeros((8, TILE), f32)
            low = b < BUCKETS // 2
            for kind in (1, 2) if low else (2, 3):
                bucket = bucket_index(row - column + (kind - 2) * TILE)
                part = part + fold(jnp.where(bucket == b, near[kind], 0.0), jnp.sum)
            if b == BUCKETS // 2 - 1:
                part = part + fold(near[0], jnp.sum)
            if b == BUCKETS - 1:
                part = part + fold(near[4], jnp.sum)
            bias_ref[h, b] = part


def attend_back(base, q, k, v, context_grad, log_total, seg_keys, seg_queries, tiles):
    rows, width = q.shape
    pairs, blocks = width // (PAIR * DH), rows // TILE
    one_pair = pl.BlockSpec((rows, PAIR * DH), lambda j: (0, j))
    return pl.pallas_call(
        backward_kernel,
        grid=(pairs,),
        out_shape=(
            jax.ShapeDtypeStruct((width, rows), bf16),
            jax.ShapeDtypeStruct((rows, width), bf16),
            jax.ShapeDtypeStruct((rows, width), bf16),
            jax.ShapeDtypeStruct((pairs * PAIR, BUCKETS, 8, TILE), f32),
        ),
        in_specs=[
            pl.BlockSpec(memory_space=pltpu.SMEM),
            one_pair,
            one_pair,
            one_pair,
            one_pair,
            pl.BlockSpec((1, PAIR, blocks, TILE), lambda j: (j, 0, 0, 0)),
            pl.BlockSpec((rows, TILE), lambda j: (0, 0)),
            pl.BlockSpec((blocks, TILE), lambda j: (0, 0)),
            pl.BlockSpec((PAIR, CLASSES, TILE, TILE), lambda j: (j, 0, 0, 0)),
        ],
        out_specs=(
            pl.BlockSpec((PAIR * DH, rows), lambda j: (j, 0)),
            one_pair,
            one_pair,
            pl.BlockSpec((PAIR, BUCKETS, 8, TILE), lambda j: (j, 0, 0, 0)),
        ),
        scratch_shapes=[
            pltpu.VMEM((rows, TILE), f32),
            pltpu.VMEM((rows, TILE), f32),
            pltpu.VMEM((rows, rows), bf16),
            pltpu.VMEM((rows, rows), bf16),
            pltpu.VMEM((CLASSES, TILE, TILE), f32),
        ],
        compiler_params=pltpu.CompilerParams(vmem_limit_bytes=VMEM_BYTES),
        name="attend_backward",
    )(base, q, k, v, context_grad, log_total, seg_keys, seg_queries, tiles)


def per_device(
    inputs,
    doc_lengths,
    gain_attn,
    w_query,
    w_key,
    w_value,
    w_out,
    bias_table,
    gain_ff,
    w_gate,
    w_up,
    w_down,
    cotangent,
):
    rows, width = inputs.shape
    planes, members = lax.axis_size("fsdp"), lax.axis_size("ctx")
    me = lax.axis_index("ctx")
    length = rows * members
    heads = H // members
    hidden = w_gate.shape[1] // members
    model = heads * DH
    striped = H % (planes * members) == 0

    def columns(weight, pieces):
        cut = weight.shape[1] // (pieces * members)
        split = weight.reshape(weight.shape[0], pieces, members, cut)
        return lax.dynamic_index_in_dim(split, me, 2, False).reshape(weight.shape[0], pieces * cut)

    def own_rows(weight):
        count = weight.shape[0] // members
        return lax.dynamic_slice_in_dim(weight, me * count, count, 0)

    def over_planes(weight):
        return lax.all_gather(weight, "fsdp", axis=0, tiled=True)

    head_pieces = planes if striped else 1
    w_qkv = over_planes(
        jnp.concatenate([columns(w, head_pieces) for w in (w_query, w_key, w_value)], axis=1)
    )
    if striped:
        out_rows = over_planes(own_rows(w_out))
    else:
        out_rows = lax.dynamic_slice_in_dim(over_planes(w_out), me * model, model, 0)
    w_mix = over_planes(jnp.concatenate([columns(w_gate, planes), columns(w_up, planes)], axis=1))
    down_rows = over_planes(own_rows(w_down))
    gains = line_gather(jnp.stack([gain_attn, gain_ff])).astype(f32)
    gain_first, gain_second = gains[0], gains[1]

    base = me if by_exchange() else jnp.zeros_like(me)
    slots = jnp.arange(members, dtype=jnp.int32)
    segments = segment_table(doc_lengths[0], length).reshape(members, rows)
    seg_queries = jnp.take(segments, lax.bitwise_xor(base, slots), axis=0)
    seg_queries = seg_queries.reshape(length // TILE, TILE)
    seg_keys = jnp.broadcast_to(seg_queries.reshape(length, 1), (length, TILE))
    base_block = jnp.reshape(base, (1,)).astype(jnp.int32)
    if striped:
        unit = H // (planes * members)
        order = jnp.arange(heads, dtype=jnp.int32)
        own_heads = order // unit * (H // planes) + me * unit + order % unit
    else:
        own_heads = me * heads + jnp.arange(heads, dtype=jnp.int32)
    pick = (jnp.arange(H, dtype=jnp.int32)[:, None] == own_heads[None, :]).astype(f32)
    table = jnp.dot(bias_table.astype(f32), pick, precision=lax.Precision.HIGHEST)
    tiles = bias_tiles(table)

    source_all = plane_gather(inputs)
    normed = rms_scale(source_all.astype(f32), gain_first).astype(bf16)
    qkv = dot(normed, w_qkv).astype(bf16)
    q, k, v = qkv[:, :model], qkv[:, model : 2 * model], qkv[:, 2 * model :]
    context_t, log_total = attend(base_block, q, k, v, seg_keys, seg_queries, tiles)
    grad_all = plane_gather(cotangent)
    source = inputs.astype(f32)
    residual = source + plane_scatter(dot(context_t, out_rows, ((0,), (0,))).astype(bf16))

    normed_ff = plane_gather(rms_scale(residual, gain_second).astype(bf16))
    mix = dot(normed_ff, w_mix)
    gate_pre, up_pre = mix[:, :hidden], mix[:, hidden:]
    active_f, mix_back = jax.vjp(gated_mix, gate_pre, up_pre)
    active = active_f.astype(bf16)
    down_grad = dot(active, grad_all, ((0,), (0,))).astype(bf16)
    active_grad = dot(grad_all, down_rows, ((1,), (1,)))
    gate_grad, up_grad = mix_back(active_grad)
    mix_grad = jnp.concatenate([gate_grad.astype(bf16), up_grad.astype(bf16)], axis=1)
    normed_ff_grad = plane_scatter(dot(mix_grad, w_mix, ((1,), (1,))).astype(bf16))
    output_sum = plane_scatter(dot(active, down_rows).astype(bf16))
    output = (residual + output_sum).astype(bf16)
    mix_weight_grad = dot(normed_ff, mix_grad, ((0,), (0,))).astype(bf16)
    norm_back = jax.vjp(rms_scale, residual, gain_second)[1]
    residual_part, ff_gain_grad = norm_back(normed_ff_grad)
    residual_grad = cotangent.astype(f32) + residual_part

    residual_low = plane_gather(residual_grad.astype(bf16))
    context_grad = dot(residual_low, out_rows, ((1,), (1,))).astype(bf16)
    out_weight_grad = dot(context_t, residual_low).astype(bf16)
    query_grad_t, key_grad, value_grad, bias_parts = attend_back(
        base_block, q, k, v, context_grad, log_total, seg_keys, seg_queries, tiles
    )
    w_q, w_kv = w_qkv[:, :model], w_qkv[:, model:]
    kv_grad = jnp.concatenate([key_grad, value_grad], axis=1)
    normed_grad = plane_scatter(
        (dot(query_grad_t, w_q, ((0,), (1,))) + dot(kv_grad, w_kv, ((1,), (1,)))).astype(bf16)
    )
    qkv_weight_grad = jnp.concatenate(
        [dot(normed, query_grad_t, ((0,), (1,))), dot(normed, kv_grad, ((0,), (0,)))], axis=1
    ).astype(bf16)
    first_back = jax.vjp(rms_scale, source, gain_first)[1]
    source_part, attn_gain_grad = first_back(normed_grad)
    input_grad = (residual_grad + source_part).astype(bf16)

    def sum_planes(partial):
        return lax.psum_scatter(partial, "fsdp", scatter_dimension=0, tiled=True)

    def to_rows(partial, kinds, pieces):
        summed = sum_planes(partial)
        cut = summed.shape[1] // (kinds * pieces)
        moved = lax.all_to_all(summed, "ctx", 0, 0, tiled=True)
        moved = moved.reshape(members, summed.shape[0] // members, kinds, pieces, cut)
        moved = jnp.transpose(moved, (2, 1, 3, 0, 4))
        return moved.reshape(kinds, moved.shape[1], pieces * members * cut).astype(f32)

    down_shard = sum_planes(down_grad).astype(f32)
    gate_shard, up_shard = to_rows(mix_weight_grad, 2, planes)
    if striped:
        out_shard = sum_planes(out_weight_grad).astype(f32)
    else:
        placed = jnp.zeros((H * DH, width), f32)
        placed = lax.dynamic_update_slice_in_dim(placed, out_weight_grad.astype(f32), me * model, 0)
        out_shard = lax.psum_scatter(placed, ("fsdp", "ctx"), scatter_dimension=0, tiled=True)
    query_shard, key_shard, value_shard = to_rows(qkv_weight_grad, 3, head_pieces)
    bias_own = jnp.sum(bias_parts, axis=(2, 3))
    bias_rows = jnp.dot(bias_own.T, pick.T, precision=lax.Precision.HIGHEST)
    small = [attn_gain_grad, ff_gain_grad, bias_rows.reshape(BUCKETS * H)]
    small = [lax.psum_scatter(s, ("fsdp", "ctx"), scatter_dimension=0, tiled=True) for s in small]
    return (
        output,
        input_grad,
        small[0],
        small[1],
        query_shard,
        key_shard,
        value_shard,
        out_shard,
        small[2],
        gate_shard,
        up_shard,
        down_shard,
    )


def solution(mesh):
    rows = P(("fsdp", "ctx"), None)
    vector = P(("fsdp", "ctx"))
    weight = P("fsdp", None)
    return jax.shard_map(
        per_device,
        mesh=mesh,
        in_specs=(
            rows,
            P("fsdp", None),
            P("fsdp"),
            weight,
            weight,
            weight,
            weight,
            P(),
            P("fsdp"),
            weight,
            weight,
            weight,
            rows,
        ),
        out_specs=(rows, rows, vector, vector, rows, rows, rows, rows, vector, rows, rows, rows),
        check_vma=False,
    )
```

time: 4170 us -> 701 us (0.17)
  waiting for transfers between devices: 3580 us -> 296 us
  matrix products: 300 us -> 75.4 us
  Pallas kernels: 0 us -> 62.8 us
  starting transfers between devices: 3.38 us -> 60 us
    reduce_scatter x7 -> x4, waiting for transfers between devices: 1910 us -> 112 us  [sum_planes(): return lax.psum_scatter(partial, 'fsdp', scatter_dimension=0, tiled=True)]
    all_gather x9 -> x4, waiting for transfers between devices: 1530 us -> 65.1 us  [over_planes(): return lax.all_gather(weight, 'fsdp', axis=0, tiled=True)]
    dot_general x85 -> x16, matrix products: 300 us -> 75.4 us  [the longest x14 74.5 us: dot(): lax.dot_general(left, right, (contract, ((), ())), preferred_element_type...]
    pallas_call x0 -> x3, Pallas kernels: none -> 62.8 us  [the longest x1 36.4 us: attend_back(): pl.pallas_call(backward_kernel, grid=(pairs,), out_shape=(jax.ShapeDtypeS...]
    ppermute x15 -> x67, starting transfers between devices: 2.34 us -> 51.9 us  [the longest x64 43.9 us: swap(): lax.ppermute(block, 'ctx', [(i, i ^ mask) for i in range(lax.axis_size('c...]
    ppermute x15 -> x67, waiting for transfers between devices: 134 us -> 110 us  [the longest x64 110 us: swap(): lax.ppermute(block, 'ctx', [(i, i ^ mask) for i in range(lax.axis_size('c...]
  transfers between devices with their start and end apart: 31 -> 77, of which waited for: 22 -> 34; matrix products, arithmetic and copies ran while one was open for 9% -> 20% of each run, Pallas kernels for 0% -> 4%
where the time goes in v1:
time: 701 us; the launch traced here: 691 us
  waiting for transfers between devices  296 us (42%)
  local copies, waits for them, and re-layouts  100 us (14%)
  matrix products  75.4 us (11%)
  Pallas kernels  62.8 us (9%)
  starting transfers between devices  60 us (9%)
  blocking collectives  50.8 us (7%)
  other arithmetic  30.9 us (4%)
  between operations  15.7 us (2%)
    reduce_scatter x4, waiting for transfers between devices, sum_planes(): return lax.psum_scatter(partial, 'fsdp', scatter_dimension=0, tiled=True)  112 us
    ppermute x64, waiting for transfers between devices, swap(): lax.ppermute(block, 'ctx', [(i, i ^ mask) for i in range(lax.axis_size('c...  110 us
    dot_general x14, matrix products, dot(): lax.dot_general(left, right, (contract, ((), ())), preferred_element_type...  74.5 us
    all_gather x4, waiting for transfers between devices, over_planes(): return lax.all_gather(weight, 'fsdp', axis=0, tiled=True)  65.1 us
    unnamed x1, blocking collectives  50.8 us
    unnamed x93, local copies, waits for them, and re-layouts  50 us
    ppermute x64, starting transfers between devices, swap(): lax.ppermute(block, 'ctx', [(i, i ^ mask) for i in range(lax.axis_size('c...  43.9 us
    pallas_call x1, Pallas kernels, attend_back(): pl.pallas_call(backward_kernel, grid=(pairs,), out_shape=(jax.ShapeDtypeS...  36.4 us
  transfers between devices with their start and end apart: 77, of which 34 were waited for; matrix products, arithmetic and copies ran while one was open for 20% of the time, Pallas kernels for 4%

profile of v1, /device:TPU:0, one launch (start us, length us, event | category | flops | bytes accessed | tf_op | source)
XLA Modules:
  0.0 691.3 jit_solution(8886074179962524194)
XLA Ops:
  23.0 7.9 %copy.60 = bf16[512,5120]{0,1:T(8,128)(2,1)} copy(bf16[512,5120]{1,0:T(8,128)(2,1)} %param.22) | data formatting | bytes 10485760 | tf_op args[9]
  31.0 8.0 %copy.61 = bf16[512,5120]{0,1:T(8,128)(2,1)} copy(bf16[512,5120]{1,0:T(8,128)(2,1)} %param.23) | data formatting | bytes 10485760 | tf_op args[10]
  61.0 12.9 %collective-permute-done.1 = bf16[128,2048]{1,0:T(8,128)(2,1)S(1)} collective-permute-done((bf16[128,2048]{1,0:T(8,128)(2,1)S(1)}, bf16[128,2048]{1,0:T(8,128)(2,1)S(1)}, u32[]{:S(2)}, u32[]{:S(2)}) %collective-permute-start.1) | collective-permute-done | bytes 524320 | tf_op jit(solution)/shard_map/ppermute | solution.py:55
  91.6 6.6 convolution_convert_fusion.8
  100.4 22.3 %attend_forward.1 = (bf16[256,1024]{1,0:T(8,128)(2,1)}, f32[2,2,8,128]{3,2,1,0:T(8,128)}) custom-call(s32[1]{0:T(128)} %bitcast.base_ref, bf16[1024,256]{1,0:T(8,128)(2,1)} %get-tuple-element.78.q_ref, bf16[1024,256]{1,0:T(8,128)(2,1)} %get-tuple-element.77.k_ref, bf16[1024,256]{1,0:T(8,128)(2,1)} %get-tuple-element.76.v_ref, ...), custom_call_target="tpu_custom_call" | custom-call | tf_op jit(solution)/shard_map/attend_forward/pallas_call | solution.py:193
  142.3 5.0 collective-permute-done.17
  148.9 6.4 collective-permute-done.14
  159.3 8.9 %collective-permute-done.18 = bf16[128,2048]{1,0:T(8,128)(2,1)S(1)} collective-permute-done((bf16[128,2048]{1,0:T(8,128)(2,1)S(1)}, bf16[128,2048]{1,0:T(8,128)(2,1)S(1)}, u32[]{:S(2)}, u32[]{:S(2)}) %collective-permute-start.18) | collective-permute-done | bytes 524320 | tf_op jit(solution)/shard_map/ppermute | solution.py:55
  173.8 10.5 %collective-permute-done.22 = bf16[128,2048]{1,0:T(8,128)(2,1)S(1)} collective-permute-done((bf16[128,2048]{1,0:T(8,128)(2,1)S(1)}, bf16[128,2048]{1,0:T(8,128)(2,1)S(1)}, u32[]{:S(2)}, u32[]{:S(2)}) %collective-permute-start.22) | collective-permute-done | bytes 524320 | tf_op jit(solution)/shard_map/ppermute | solution.py:55
  196.7 20.4 %all-gather.9.cloned.1.call-done = bf16[2048,1280]{0,1:T(8,128)(2,1)} async-done(((bf16[512,1280]{0,1:T(8,128)(2,1)}), bf16[2048,1280]{0,1:T(8,128)(2,1)}) %all-gather.9.cloned.1.call-update) | async-done | bytes 5242896 | tf_op jit(solution)/shard_map/all_gather | solution.py:359
  217.1 10.4 %fusion.52 = f32[1024,1280]{1,0:T(8,128)} fusion(bf16[1024,2048]{1,0:T(8,128)(2,1)} %constant_dynamic-update-slice_fusion.9, bf16[2048,1280]{0,1:T(8,128)(2,1)} %all-gather.9.cloned.1.call-done), kind=kOutput, calls=%fused_computation.192 | convolution fusion | flops 5368709120 | bytes 14680064 | tf_op jit(solution)/shard_map/dot_general | solution.py:51
  227.5 44.7 %all-gather.11.cloned.1.call-done = bf16[640,2048]{1,0:T(8,128)(2,1)} async-done(((bf16[160,2048]{1,0:T(8,128)(2,1)}), bf16[640,2048]{1,0:T(8,128)(2,1)}) %all-gather.11.cloned.1.call-update) | async-done | bytes 2621456 | tf_op jit(solution)/shard_map/all_gather | solution.py:359
  272.3 9.6 %fusion.9 = (bf16[1024,640]{1,0:T(8,128)(2,1)S(1)}, bf16[1024,640]{1,0:T(8,128)(2,1)S(1)}, bf16[1024,640]{1,0:T(8,128)(2,1)S(1)}) fusion(f32[1024,1280]{1,0:T(8,128)} %fusion.52, bf16[1024,2048]{1,0:T(8,128)(2,1)} %copy-done.17, bf16[640,2048]{1,0:T(8,128)(2,1)} %all-gather.11.cloned.1.call-done), kind=kOutput, calls=%fused_computation.23 | convolution fusion | flops 2701393920 | bytes 15990784 | tf_op jit(solution)/shard_map/dot_general | solution.py:51
  287.9 6.2 convolution_convert_fusion.1
  301.5 5.1 collective-permute-done.33
  309.5 4.4 collective-permute-done.49
  317.6 5.5 collective-permute-done.34
  323.1 5.6 collective-permute-done.31
  328.7 4.8 collective-permute-done.50
  343.4 8.1 %collective-permute-done.54 = bf16[128,2048]{1,0:T(8,128)(2,1)S(1)} collective-permute-done((bf16[128,2048]{1,0:T(8,128)(2,1)S(1)}, bf16[128,2048]{1,0:T(8,128)(2,1)S(1)}, u32[]{:S(2)}, u32[]{:S(2)}) %collective-permute-start.54) | collective-permute-done | bytes 524320 | tf_op jit(solution)/shard_map/ppermute | solution.py:55
  366.0 36.4 %attend_backward.1 = (bf16[256,1024]{1,0:T(8,128)(2,1)}, bf16[1024,256]{1,0:T(8,128)(2,1)}, bf16[1024,256]{1,0:T(8,128)(2,1)}, f32[4,32,8,128]{3,2,1,0:T(8,128)}) custom-call(s32[1]{0:T(128)} %bitcast.base_ref, bf16[1024,256]{1,0:T(8,128)(2,1)} %get-tuple-element.78.q_ref, bf16[1024,256]{1,0:T(8,128)(2,1)} %get-tuple-element.77.k_ref, ...), custom_call_target="tpu_custom_call" | custom-call | tf_op jit(solution)/shard_map/attend_backward/pallas_call | solution.py:287
  411.0 9.8 %convolution_convert_fusion = bf16[2048,1280]{1,0:T(8,128)(2,1)} fusion(bf16[1024,2048]{1,0:T(8,128)(2,1)} %constant_dynamic-update-slice_fusion.9, bf16[1024,640]{1,0:T(8,128)(2,1)} %copy-done.26, bf16[1024,640]{1,0:T(8,128)(2,1)} %copy-done.25), kind=kOutput, calls=%fused_computation.7 | convolution fusion | flops 5376573440 | bytes 12058624 | tf_op jit(solution)/shard_map/dot_general | solution.py:51
  421.8 4.5 convolution_convert_fusion.7
  426.6 7.0 %convolution_convert_fusion.4 = bf16[640,2048]{1,0:T(8,128)(2,1)} fusion(bf16[1024,640]{1,0:T(8,128)(2,1)} %copy-done.24, bf16[1024,2048]{1,0:T(8,128)(2,1)} %copy-done.17), kind=kOutput, calls=%fused_computation.14 | convolution fusion | flops 2685665280 | bytes 8126464 | tf_op jit(solution)/shard_map/dot_general | solution.py:51
  446.9 6.8 collective-permute-done.65
  455.7 13.5 %reduce-scatter.5.cloned.1.call-done = bf16[512,768]{0,1:T(8,128)(2,1)} async-done(((bf16[2048,768]{0,1:T(8,128)(2,1)}), bf16[512,768]{0,1:T(8,128)(2,1)}) %reduce-scatter.5.cloned.1.call-update) | async-done | bytes 786448 | tf_op jit(solution)/shard_map/reduce_scatter | solution.py:436
  479.8 8.5 %all-to-all-done = bf16[8,64,768]{2,1,0:T(8,128)(2,1)S(1)} async-done(((bf16[8,64,768]{2,1,0:T(8,128)(2,1)}), bf16[8,64,768]{2,1,0:T(8,128)(2,1)S(1)}, u32[]{:S(2)}, u32[]{:S(2)}) %all-to-all-start) | async-done | bytes 786464 | tf_op jit(solution)/shard_map/all_to_all | solution.py:441
  488.3 76.8 %reduce-scatter.9.cloned.1.call-done = bf16[512,1280]{1,0:T(8,128)(2,1)} async-done(((bf16[2048,1280]{1,0:T(8,128)(2,1)}), bf16[512,1280]{1,0:T(8,128)(2,1)}) %reduce-scatter.9.cloned.1.call-update) | async-done | bytes 1310736 | tf_op jit(solution)/shard_map/reduce_scatter | solution.py:436
  570.8 50.8 %all-reduce.3 = (f32[2048]{0:T(1024)S(1)}, f32[2048]{0:T(1024)S(1)}, f32[1024]{0:T(1024)S(1)}) all-reduce(f32[2048]{0:T(1024)S(1)} %get-tuple-element.26, f32[2048]{0:T(1024)S(1)} %get-tuple-element.24, f32[1024]{0:T(1024)S(1)} %reshape.224), channel_id=2, replica_groups=mesh['fsdp'=4,'ctx'=8] {'fsdp','ctx'}, use_global_device_ids=true, to_apply=%region_8.9.clone | all-reduce | flops 5120 | bytes 40960
  627.8 21.4 %reduce-scatter.11.cloned.1.call-done = bf16[160,2048]{1,0:T(8,128)(2,1)} async-done(((bf16[640,2048]{1,0:T(8,128)(2,1)}), bf16[160,2048]{1,0:T(8,128)(2,1)}) %reduce-scatter.11.cloned.1.call-update) | async-done | bytes 655376 | tf_op jit(solution)/shard_map/reduce_scatter | solution.py:436
  664.8 5.4 reshape.226
  670.2 4.6 copy.72
  (354 shorter events, 216.5 us)
Async XLA Ops:
  7.2 84.4 %all-gather.5.cloned.1.call-start = ((), (), s32[]{:S(2)}) async-start(), calls=%async_computation.6 | async-start | bytes 3932160 | tf_op jit(solution)/shard_map/all_gather | solution.py:359
  22.2 100.5 %all-gather.7.cloned.1.call-start = ((), (), s32[]{:S(2)}) async-start(), calls=%async_computation.7 | async-start | bytes 1310720 | tf_op jit(solution)/shard_map/all_gather | solution.py:359
  23.0 194.1 %all-gather.9.cloned.1.call-start = ((), (), s32[]{:S(2)}) async-start(), calls=%async_computation.8 | async-start | bytes 6553600 | tf_op jit(solution)/shard_map/all_gather | solution.py:359
  41.7 230.6 %all-gather.11.cloned.1.call-start = ((), (), s32[]{:S(2)}) async-start(), calls=%async_computation.9 | async-start | bytes 3276800 | tf_op jit(solution)/shard_map/all_gather | solution.py:359
  41.8 17.2 %collective-permute-start.9 = (bf16[2,512]{1,0:T(2,128)(2,1)S(1)}, bf16[2,512]{1,0:T(2,128)(2,1)S(1)}, u32[]{:S(2)}, u32[]{:S(2)}) collective-permute-start(bf16[2,512]{1,0:T(2,128)(2,1)S(1)} %get-tuple-element.39), channel_id=1, source_target_pairs={{0,16},{8,24},{16,0},{24,8},{1,17},{9,25},{17,1},{25,9},{2,18},{10... | collective-permute-start | bytes 6152 | tf_op jit(solution)/shard_map/ppermute | solution.py:102
  49.8 79.4 %collective-permute-start.36 = (bf16[128,2048]{1,0:T(8,128)(2,1)S(1)}, bf16[128,2048]{1,0:T(8,128)(2,1)S(1)}, u32[]{:S(2)}, u32[]{:S(2)}) collective-permute-start(bf16[128,2048]{1,0:T(8,128)(2,1)S(1)} %copy-done.8), channel_id=1, source_target_pairs={{0,2},{1,3},{2,0},{3,1},{4,6},{5,7},{6,4},{7,5},{8,10},{9,11},{10,... | collective-permute-start | bytes 1572872 | tf_op jit(solution)/shard_map/ppermute | solution.py:55
  51.3 81.8 %collective-permute-start.35 = (bf16[128,2048]{1,0:T(8,128)(2,1)S(1)}, bf16[128,2048]{1,0:T(8,128)(2,1)}, u32[]{:S(2)}, u32[]{:S(2)}) collective-permute-start(bf16[128,2048]{1,0:T(8,128)(2,1)S(1)} %copy-done.8), channel_id=1, source_target_pairs={{0,1},{1,0},{2,3},{3,2},{4,5},{5,4},{6,7},{7,6},{8,9},{9,8},{10,11... | collective-permute-start | bytes 1572872 | tf_op jit(solution)/shard_map/ppermute | solution.py:55
  58.6 15.3 %collective-permute-start.1 = (bf16[128,2048]{1,0:T(8,128)(2,1)S(1)}, bf16[128,2048]{1,0:T(8,128)(2,1)S(1)}, u32[]{:S(2)}, u32[]{:S(2)}) collective-permute-start(bf16[128,2048]{1,0:T(8,128)(2,1)S(1)} %copy-done.4), channel_id=1, source_target_pairs={{0,2},{1,3},{2,0},{3,1},{4,6},{5,7},{6,4},{7,5},{8,10},{9,11},{10,... | collective-permute-start | bytes 1572872 | tf_op jit(solution)/shard_map/ppermute | solution.py:55
  59.1 18.0 %collective-permute-start = (bf16[128,2048]{1,0:T(8,128)(2,1)S(1)}, bf16[128,2048]{1,0:T(8,128)(2,1)S(1)}, u32[]{:S(2)}, u32[]{:S(2)}) collective-permute-start(bf16[128,2048]{1,0:T(8,128)(2,1)S(1)} %copy-done.4), channel_id=1, source_target_pairs={{0,1},{1,0},{2,3},{3,2},{4,5},{5,4},{6,7},{7,6},{8,9},{9,8},{10,11... | collective-permute-start | bytes 1572872 | tf_op jit(solution)/shard_map/ppermute | solution.py:55
  59.4 16.1 %collective-permute-start.3 = (bf16[128,2048]{1,0:T(8,128)(2,1)S(1)}, bf16[128,2048]{1,0:T(8,128)(2,1)S(1)}, u32[]{:S(2)}, u32[]{:S(2)}) collective-permute-start(bf16[128,2048]{1,0:T(8,128)(2,1)S(1)} %copy-done.4), channel_id=1, source_target_pairs={{0,4},{1,5},{2,6},{3,7},{4,0},{5,1},{6,2},{7,3},{8,12},{9,13},{10,... | collective-permute-start | bytes 1572872 | tf_op jit(solution)/shard_map/ppermute | solution.py:55
  81.5 50.1 %collective-permute-start.38 = (bf16[128,2048]{1,0:T(8,128)(2,1)S(1)}, bf16[128,2048]{1,0:T(8,128)(2,1)}, u32[]{:S(2)}, u32[]{:S(2)}) collective-permute-start(bf16[128,2048]{1,0:T(8,128)(2,1)S(1)} %copy-done.8), channel_id=1, source_target_pairs={{0,4},{1,5},{2,6},{3,7},{4,0},{5,1},{6,2},{7,3},{8,12},{9,13},{10,... | collective-permute-start | bytes 1572872 | tf_op jit(solution)/shard_map/ppermute | solution.py:55
  131.2 337.9 %reduce-scatter.5.cloned.1.call-start = ((), (), s32[]{:S(2)}) async-start(), calls=%async_computation.10 | async-start | bytes 3932160 | tf_op jit(solution)/shard_map/reduce_scatter | solution.py:436
  135.3 21.8 %collective-permute-start.37 = (bf16[128,2048]{1,0:T(8,128)(2,1)S(1)}, bf16[128,2048]{1,0:T(8,128)(2,1)S(1)}, u32[]{:S(2)}, u32[]{:S(2)}) collective-permute-start(bf16[128,2048]{1,0:T(8,128)(2,1)S(1)} %collective-permute-done.36), channel_id=1, source_target_pairs={{0,1},{1,0},{2,3},{3,2},{4,5},{5,4},{6,7},{7,6},{8,9},{9,8},{10,11... | collective-permute-start | bytes 1572872 | tf_op jit(solution)/shard_map/ppermute | solution.py:55
  135.4 23.9 %collective-permute-start.39 = (bf16[128,2048]{1,0:T(8,128)(2,1)}, bf16[128,2048]{1,0:T(8,128)(2,1)S(1)}, u32[]{:S(2)}, u32[]{:S(2)}) collective-permute-start(bf16[128,2048]{1,0:T(8,128)(2,1)} %collective-permute-done.38), channel_id=1, source_target_pairs={{0,1},{1,0},{2,3},{3,2},{4,5},{5,4},{6,7},{7,6},{8,9},{9,8},{10,11... | collective-permute-start | bytes 1572872 | tf_op jit(solution)/shard_map/ppermute | solution.py:55
  141.7 32.1 %collective-permute-start.42 = (bf16[128,2048]{1,0:T(8,128)(2,1)S(1)}, bf16[128,2048]{1,0:T(8,128)(2,1)S(1)}, u32[]{:S(2)}, u32[]{:S(2)}) collective-permute-start(bf16[128,2048]{1,0:T(8,128)(2,1)S(1)} %pad_maximum_fusion.12), channel_id=1, source_target_pairs={{0,1},{1,0},{2,3},{3,2},{4,5},{5,4},{6,7},{7,6},{8,9},{9,8},{10,11... | collective-permute-start | bytes 1572872 | tf_op jit(solution)/shard_map/ppermute | solution.py:55
  141.8 17.5 %collective-permute-start.11 = (bf16[128,2048]{1,0:T(8,128)(2,1)S(1)}, bf16[128,2048]{1,0:T(8,128)(2,1)S(1)}, u32[]{:S(2)}, u32[]{:S(2)}) collective-permute-start(bf16[128,2048]{1,0:T(8,128)(2,1)S(1)} %copy-done.13), channel_id=1, source_target_pairs={{0,1},{1,0},{2,3},{3,2},{4,5},{5,4},{6,7},{7,6},{8,9},{9,8},{10,11... | collective-permute-start | bytes 1572872 | tf_op jit(solution)/shard_map/ppermute | solution.py:55
  173.7 14.2 %collective-permute-start.19 = (bf16[128,2048]{1,0:T(8,128)(2,1)S(1)}, bf16[128,2048]{1,0:T(8,128)(2,1)S(1)}, u32[]{:S(2)}, u32[]{:S(2)}) collective-permute-start(bf16[128,2048]{1,0:T(8,128)(2,1)S(1)} %get-tuple-element.35), channel_id=1, source_target_pairs={{0,1},{1,0},{2,3},{3,2},{4,5},{5,4},{6,7},{7,6},{8,9},{9,8},{10,11... | collective-permute-start | bytes 1572872 | tf_op jit(solution)/shard_map/ppermute | solution.py:55
  286.8 30.2 %collective-permute-start.27 = (bf16[128,2048]{1,0:T(8,128)(2,1)S(1)}, bf16[128,2048]{1,0:T(8,128)(2,1)S(1)}, u32[]{:S(2)}, u32[]{:S(2)}) collective-permute-start(bf16[128,2048]{1,0:T(8,128)(2,1)S(1)} %get-tuple-element.59), channel_id=1, source_target_pairs={{0,1},{1,0},{2,3},{3,2},{4,5},{5,4},{6,7},{7,6},{8,9},{9,8},{10,11... | collective-permute-start | bytes 1572872 | tf_op jit(solution)/shard_map/ppermute | solution.py:55
  294.4 23.2 %collective-permute-start.43 = (bf16[128,2048]{1,0:T(8,128)(2,1)S(1)}, bf16[128,2048]{1,0:T(8,128)(2,1)S(1)}, u32[]{:S(2)}, u32[]{:S(2)}) collective-permute-start(bf16[128,2048]{1,0:T(8,128)(2,1)S(1)} %get-tuple-element.52), channel_id=1, source_target_pairs={{0,1},{1,0},{2,3},{3,2},{4,5},{5,4},{6,7},{7,6},{8,9},{9,8},{10,11... | collective-permute-start | bytes 1572872 | tf_op jit(solution)/shard_map/ppermute | solution.py:55
  300.7 14.7 %collective-permute-start.46 = (bf16[64,2048]{1,0:T(8,128)(2,1)S(1)}, bf16[64,2048]{1,0:T(8,128)(2,1)S(1)}, u32[]{:S(2)}, u32[]{:S(2)}) collective-permute-start(bf16[64,2048]{1,0:T(8,128)(2,1)S(1)} %get-tuple-element.83), channel_id=1, source_target_pairs={{0,4},{1,5},{2,6},{3,7},{4,0},{5,1},{6,2},{7,3},{8,12},{9,13},{10,... | collective-permute-start | bytes 786440 | tf_op jit(solution)/shard_map/ppermute | solution.py:55
  308.3 14.9 %collective-permute-start.34 = (bf16[128,2048]{1,0:T(8,128)(2,1)S(1)}, bf16[128,2048]{1,0:T(8,128)(2,1)S(1)}, u32[]{:S(2)}, u32[]{:S(2)}) collective-permute-start(bf16[128,2048]{1,0:T(8,128)(2,1)S(1)} %pad_maximum_fusion.11), channel_id=1, source_target_pairs={{0,4},{1,5},{2,6},{3,7},{4,0},{5,1},{6,2},{7,3},{8,12},{9,13},{10,... | collective-permute-start | bytes 1572872 | tf_op jit(solution)/shard_map/ppermute | solution.py:55
  313.9 14.9 %collective-permute-start.31 = (bf16[128,2048]{1,0:T(8,128)(2,1)S(1)}, bf16[128,2048]{1,0:T(8,128)(2,1)S(1)}, u32[]{:S(2)}, u32[]{:S(2)}) collective-permute-start(bf16[128,2048]{1,0:T(8,128)(2,1)S(1)} %pad_maximum_fusion.10), channel_id=1, source_target_pairs={{0,2},{1,3},{2,0},{3,1},{4,6},{5,7},{6,4},{7,5},{8,10},{9,11},{10,... | collective-permute-start | bytes 1572872 | tf_op jit(solution)/shard_map/ppermute | solution.py:55
  315.5 18.1 %collective-permute-start.50 = (bf16[128,2048]{1,0:T(8,128)(2,1)S(1)}, bf16[128,2048]{1,0:T(8,128)(2,1)S(1)}, u32[]{:S(2)}, u32[]{:S(2)}) collective-permute-start(bf16[128,2048]{1,0:T(8,128)(2,1)S(1)} %pad_maximum_fusion.14), channel_id=1, source_target_pairs={{0,4},{1,5},{2,6},{3,7},{4,0},{5,1},{6,2},{7,3},{8,12},{9,13},{10,... | collective-permute-start | bytes 1572872 | tf_op jit(solution)/shard_map/ppermute | solution.py:55
  317.0 20.0 %collective-permute-start.47 = (bf16[128,2048]{1,0:T(8,128)(2,1)S(1)}, bf16[128,2048]{1,0:T(8,128)(2,1)S(1)}, u32[]{:S(2)}, u32[]{:S(2)}) collective-permute-start(bf16[128,2048]{1,0:T(8,128)(2,1)S(1)} %pad_maximum_fusion.13), channel_id=1, source_target_pairs={{0,2},{1,3},{2,0},{3,1},{4,6},{5,7},{6,4},{7,5},{8,10},{9,11},{10,... | collective-permute-start | bytes 1572872 | tf_op jit(solution)/shard_map/ppermute | solution.py:55
  410.9 154.2 %reduce-scatter.9.cloned.1.call-start = ((), (), s32[]{:S(2)}) async-start(), calls=%async_computation.12 | async-start | bytes 6553600 | tf_op jit(solution)/shard_map/reduce_scatter | solution.py:436
  420.8 205.2 %reduce-scatter.7.cloned.1.call-start = ((), (), s32[]{:S(2)}) async-start(), calls=%async_computation.11 | async-start | bytes 1310720 | tf_op jit(solution)/shard_map/reduce_scatter | solution.py:436
  426.3 222.8 %reduce-scatter.11.cloned.1.call-start = ((), (), s32[]{:S(2)}) async-start(), calls=%async_computation.13 | async-start | bytes 3276800 | tf_op jit(solution)/shard_map/reduce_scatter | solution.py:436
  446.8 122.0 %collective-permute-start.59 = (bf16[128,2048]{1,0:T(8,128)(2,1)}, bf16[128,2048]{1,0:T(8,128)(2,1)S(1)}, u32[]{:S(2)}, u32[]{:S(2)}) collective-permute-start(bf16[128,2048]{1,0:T(8,128)(2,1)} %get-tuple-element.45), channel_id=1, source_target_pairs={{0,1},{1,0},{2,3},{3,2},{4,5},{5,4},{6,7},{7,6},{8,9},{9,8},{10,11... | collective-permute-start | bytes 1572872 | tf_op jit(solution)/shard_map/ppermute | solution.py:55
  454.6 114.1 %collective-permute-start.66 = (bf16[128,2048]{1,0:T(8,128)(2,1)}, bf16[128,2048]{1,0:T(8,128)(2,1)}, u32[]{:S(2)}, u32[]{:S(2)}) collective-permute-start(bf16[128,2048]{1,0:T(8,128)(2,1)} %pad_maximum_fusion.17), channel_id=1, source_target_pairs={{0,4},{1,5},{2,6},{3,7},{4,0},{5,1},{6,2},{7,3},{8,12},{9,13},{10,... | collective-permute-start | bytes 1572872 | tf_op jit(solution)/shard_map/ppermute | solution.py:55
  471.4 16.9 %all-to-all-start = ((bf16[8,64,768]{2,1,0:T(8,128)(2,1)}), bf16[8,64,768]{2,1,0:T(8,128)(2,1)S(1)}, u32[]{:S(2)}, u32[]{:S(2)}) async-start(bf16[8,64,768]{2,1,0:T(8,128)(2,1)} %bitcast.24), calls=%async_computation.1 | async-start | bytes 1572864 | tf_op jit(solution)/shard_map/all_to_all | solution.py:441
  476.1 92.7 %collective-permute-start.63 = (bf16[128,2048]{1,0:T(8,128)(2,1)}, bf16[128,2048]{1,0:T(8,128)(2,1)}, u32[]{:S(2)}, u32[]{:S(2)}) collective-permute-start(bf16[128,2048]{1,0:T(8,128)(2,1)} %pad_maximum_fusion.16), channel_id=1, source_target_pairs={{0,2},{1,3},{2,0},{3,1},{4,6},{5,7},{6,4},{7,5},{8,10},{9,11},{10,... | collective-permute-start | bytes 1572872 | tf_op jit(solution)/shard_map/ppermute | solution.py:55
  565.1 99.6 %all-to-all-start.1 = ((bf16[8,64,1280]{2,1,0:T(8,128)(2,1)}), bf16[8,64,1280]{2,1,0:T(8,128)(2,1)S(1)}, u32[]{:S(2)}, u32[]{:S(2)}) async-start(bf16[8,64,1280]{2,1,0:T(8,128)(2,1)} %bitcast.80), calls=%async_computation.4 | async-start | bytes 2621440 | tf_op jit(solution)/shard_map/all_to_all | solution.py:441
  (72 other events, 766.2 us)
Sparse Core Ops, SparseCore 0:
  22.3 66.2 all-gather.4
  90.8 26.5 all-gather.6
  119.5 97.5 all-gather.8
  219.1 53.1 all-gather.10
  411.1 58.0 reduce-scatter.4
  471.3 93.7 reduce-scatter.8
  568.0 27.6 reduce-scatter.6
  598.1 51.0 reduce-scatter.10

commit v2 on v1

--- a/solution.py
+++ b/solution.py
@@ -71,24 +71,39 @@
     )
 
 
-def plane_scatter(partial):
+def scatter_chips(partial):
     if not by_exchange():
-        return lax.psum_scatter(partial, "ctx", scatter_dimension=0, tiled=True).astype(f32)
+        return partial
     rows = partial.shape[0] // 8
-    half = rows // 2
-
-    def slot(m):
-        return partial[m * rows : (m + 1) * rows]
 
     def chip(m):
-        return slot(m).astype(f32) + swap(slot(m + 1), 1).astype(f32)
+        mine, other = partial[m * rows : (m + 1) * rows], partial[(m + 1) * rows : (m + 2) * rows]
+        return mine.astype(f32) + swap(other, 1).astype(f32)
 
     diagonal = chip(6).astype(bf16)
+    return [chip(0), chip(2), chip(4), diagonal]
+
+
+def scatter_corner(sums):
+    if not by_exchange():
+        return sums
+    own, x_sum, y_sum, diagonal = sums
+    half = own.shape[0] // 2
     via_x, via_y = swap(diagonal[:half], 2), swap(diagonal[half:], 4)
-    y_sum, x_sum = chip(4), chip(2)
     y_sum = jnp.concatenate([y_sum[:half] + via_x.astype(f32), y_sum[half:]], axis=0)
     x_sum = jnp.concatenate([x_sum[:half], x_sum[half:] + via_y.astype(f32)], axis=0)
-    return chip(0) + swap(x_sum.astype(bf16), 2).astype(f32) + swap(y_sum.astype(bf16), 4).astype(f32)
+    return [own, x_sum.astype(bf16), y_sum.astype(bf16)]
+
+
+def scatter_sides(sums):
+    if not by_exchange():
+        return lax.psum_scatter(sums, "ctx", scatter_dimension=0, tiled=True).astype(f32)
+    own, x_sum, y_sum = sums
+    return own + swap(x_sum, 2).astype(f32) + swap(y_sum, 4).astype(f32)
+
+
+def plane_scatter(partial):
+    return scatter_sides(scatter_corner(scatter_chips(partial)))
 
 
 def line_gather(small):
@@ -103,6 +118,116 @@
         )
         whole = lax.dynamic_update_index_in_dim(whole, piece, (own - step) % parts, 0)
     return jnp.transpose(whole, (1, 0, 2)).reshape(small.shape[0], -1)
+
+
+def cut_plan(cut, members):
+    window = max(-(-((cut * p) % TILE + cut) // TILE) for p in range(members))
+    return window, members * cut // TILE - window
+
+
+def cut_kernel(start_ref, *refs, pieces, window, cut, moves, along):
+    out_ref = refs[-1]
+    if along:
+        rows_ref = refs[-2]
+        count, groups = rows_ref.shape[0], rows_ref.shape[1] // along
+        for group in range(groups):
+            part = rows_ref[:, group * along : (group + 1) * along]
+            out_ref[group * count : (group + 1) * count, out_ref.shape[1] - along :] = part
+    shift = start_ref[1]
+    held = {}
+    for source, piece, first, length, target in moves:
+        if (source, piece) not in held:
+            at = (source * pieces + piece) * window
+            span = jnp.concatenate([r[...].astype(f32) for r in refs[at : at + window]], axis=1)
+            held[source, piece] = pltpu.roll(span, shift, 1)
+        part = held[source, piece][:, first : first + length]
+        out_ref[:, target : target + length] = part.astype(bf16)
+
+
+def cut_columns(weights, pieces, me, members, moves, name, along=None):
+    rows, width = weights[0].shape
+    cut = width // (pieces * members)
+    window, most = cut_plan(cut, members)
+    blocks = width // pieces // TILE
+    start = jnp.minimum(cut * me // TILE, most)
+    shift = (window * TILE - (cut * me - start * TILE)) % (window * TILE)
+    step = min(rows, 256)
+    specs = []
+    for _ in weights:
+        for piece in range(pieces):
+            for w in range(window):
+                place = piece * blocks + w
+                specs.append(pl.BlockSpec((step, TILE), lambda r, s, place=place: (r, place + s[0])))
+    columns = sum(move[3] for move in moves)
+    operands = [w for w in weights for _ in range(pieces * window)]
+    extra = 0
+    if along is not None:
+        count = along.shape[0] // members
+        extra = count * along.shape[1] // rows
+        columns += extra
+        specs.append(pl.BlockSpec((count, step // count * extra), lambda r, s: (s[2], r)))
+        operands.append(along)
+    return pl.pallas_call(
+        functools.partial(
+            cut_kernel, pieces=pieces, window=window, cut=cut, moves=moves, along=extra
+        ),
+        grid_spec=pltpu.PrefetchScalarGridSpec(
+            num_scalar_prefetch=1,
+            grid=(rows // step,),
+            in_specs=specs,
+            out_specs=pl.BlockSpec((step, columns), lambda r, s: (r, 0)),
+        ),
+        out_shape=jax.ShapeDtypeStruct((rows, columns), bf16),
+        name=name,
+    )(jnp.stack([start, shift, me]).astype(jnp.int32), *operands)
+
+
+def join_kernel(in_ref, *out_refs, pieces, cut, moves):
+    members = in_ref.shape[0]
+    for kind, piece, first, length, source in moves:
+        for p in range(members):
+            target = (piece * members + p) * cut + first
+            out_refs[kind][:, target : target + length] = in_ref[p, :, source : source + length].astype(f32)
+
+
+def join_columns(moved, kinds, pieces, moves, name):
+    members, rows, columns = moved.shape
+    cut = columns // (kinds * pieces)
+    step = min(rows, 32)
+    width = members * pieces * cut
+    return pl.pallas_call(
+        functools.partial(join_kernel, pieces=pieces, cut=cut, moves=moves),
+        grid=(rows // step,),
+        out_shape=[jax.ShapeDtypeStruct((rows, width), f32)] * kinds,
+        in_specs=[pl.BlockSpec((members, step, columns), lambda r: (0, r, 0))],
+        out_specs=[pl.BlockSpec((step, width), lambda r: (r, 0))] * kinds,
+        name=name,
+    )(moved)
+
+
+def head_moves(pieces, heads):
+    each = heads // pieces
+    return [
+        (kind, t // each, t % each * DH, DH, (t // PAIR * 3 + kind) * PAIR * DH + t % PAIR * DH)
+        for t in range(heads)
+        for kind in range(3)
+    ]
+
+
+def block_moves(kinds, pieces, cut):
+    return [
+        (kind, piece, 0, cut, (kind * pieces + piece) * cut)
+        for kind in range(kinds)
+        for piece in range(pieces)
+    ]
+
+
+def after_all(values, *others):
+    return lax.optimization_barrier((values,) + others)[0]
+
+
+def after(value, *others):
+    return lax.optimization_barrier((value,) + others)[0]
 
 
 def tiles_kernel(table_ref, out_ref):
@@ -186,10 +311,13 @@
         lax.fori_loop(0, blocks, one_block, 0)
 
 
-def attend(base, q, k, v, seg_keys, seg_queries, tiles):
-    rows, width = q.shape
+def of_pair(rows, kind):
+    return pl.BlockSpec((rows, PAIR * DH), lambda j: (0, 3 * j + kind))
+
+
+def attend(base, qkv, seg_keys, seg_queries, tiles):
+    rows, width = qkv.shape[0], qkv.shape[1] // 3
     pairs, blocks = width // (PAIR * DH), rows // TILE
-    one_pair = pl.BlockSpec((rows, PAIR * DH), lambda j: (0, j))
     return pl.pallas_call(
         forward_kernel,
         grid=(pairs,),
@@ -199,9 +327,9 @@
         ),
         in_specs=[
             pl.BlockSpec(memory_space=pltpu.SMEM),
-            one_pair,
-            one_pair,
-            one_pair,
+            of_pair(rows, 0),
+            of_pair(rows, 1),
+            of_pair(rows, 2),
             pl.BlockSpec((rows, TILE), lambda j: (0, 0)),
             pl.BlockSpec((blocks, TILE), lambda j: (0, 0)),
             pl.BlockSpec((PAIR, CLASSES, TILE, TILE), lambda j: (j, 0, 0, 0)),
@@ -213,14 +341,14 @@
         scratch_shapes=[pltpu.VMEM((rows, TILE), f32), pltpu.VMEM((rows, TILE), bf16)],
         compiler_params=pltpu.CompilerParams(vmem_limit_bytes=VMEM_BYTES),
         name="attend_forward",
-    )(base, q, k, v, seg_keys, seg_queries, tiles)
+    )(base, qkv, qkv, qkv, seg_keys, seg_queries, tiles)
 
 
 def backward_kernel(
     base_ref, q_ref, k_ref, v_ref, do_ref, log_ref, segk_ref, segq_ref, tiles_ref,
-    dq_ref, dk_ref, dv_ref, bias_ref,
-    p_scr, dp_scr, p_all, ds_all, near,
+    *rest, kept,
 ):
+    grad_ref, bias_ref, p_scr, dp_scr, p_all, ds_all, near = rest[kept:]
     rows = q_ref.shape[0]
     blocks = rows // TILE
     base = base_ref[0]
@@ -261,9 +389,12 @@
 
         def products(a, _, lanes=lanes, q_h=q_h, do_h=do_h, k_t=k_t, h=h):
             here = pl.ds(pl.multiple_of(a * 2 * TILE, 2 * TILE), 2 * TILE)
-            dv_ref[here, lanes] = jnp.dot(p_all[here, :], do_h, preferred_element_type=f32).astype(bf16)
-            dk_ref[here, lanes] = jnp.dot(ds_all[here, :], q_h, preferred_element_type=f32).astype(bf16)
-            dq_ref[lanes, here] = jnp.dot(k_t, ds_all[:, here], preferred_element_type=f32).astype(bf16)
+            dv = jnp.dot(p_all[here, :], do_h, preferred_element_type=f32)
+            dk = jnp.dot(ds_all[here, :], q_h, preferred_element_type=f32)
+            dq = jnp.dot(k_t, ds_all[:, here], preferred_element_type=f32).T
+            for kind, grad in enumerate((dq, dk, dv)):
+                first = kind * PAIR * DH + h * DH
+                grad_ref[here, first : first + DH] = grad.astype(bf16)
             return 0
 
         lax.fori_loop(0, blocks // 2, products, 0)
@@ -280,35 +411,41 @@
             bias_ref[h, b] = part
 
 
-def attend_back(base, q, k, v, context_grad, log_total, seg_keys, seg_queries, tiles):
-    rows, width = q.shape
-    pairs, blocks = width // (PAIR * DH), rows // TILE
-    one_pair = pl.BlockSpec((rows, PAIR * DH), lambda j: (0, j))
+def attend_back(base, pair, qkv, context_grad, log_total, seg_keys, seg_queries, tiles, earlier=None):
+    rows, width = context_grad.shape
+    blocks = rows // TILE
+
+    def part(kind):
+        return pl.BlockSpec((rows, PAIR * DH), lambda j: (0, 3 * pair + kind))
+
+    specs = [
+        pl.BlockSpec(memory_space=pltpu.SMEM),
+        part(0),
+        part(1),
+        part(2),
+        pl.BlockSpec((rows, PAIR * DH), lambda j: (0, pair)),
+        pl.BlockSpec((1, PAIR, blocks, TILE), lambda j: (pair, 0, 0, 0)),
+        pl.BlockSpec((rows, TILE), lambda j: (0, 0)),
+        pl.BlockSpec((blocks, TILE), lambda j: (0, 0)),
+        pl.BlockSpec((PAIR, CLASSES, TILE, TILE), lambda j: (pair, 0, 0, 0)),
+    ]
+    operands = [base, qkv, qkv, qkv, context_grad, log_total, seg_keys, seg_queries, tiles]
+    aliases = {}
+    if earlier is not None:
+        specs.append(pl.BlockSpec(memory_space=pl.ANY))
+        operands.append(earlier)
+        aliases = {len(operands) - 1: 0}
     return pl.pallas_call(
-        backward_kernel,
-        grid=(pairs,),
+        functools.partial(backward_kernel, kept=len(aliases)),
+        grid=(1,),
         out_shape=(
-            jax.ShapeDtypeStruct((width, rows), bf16),
-            jax.ShapeDtypeStruct((rows, width), bf16),
-            jax.ShapeDtypeStruct((rows, width), bf16),
-            jax.ShapeDtypeStruct((pairs * PAIR, BUCKETS, 8, TILE), f32),
+            jax.ShapeDtypeStruct((rows, 3 * width), bf16),
+            jax.ShapeDtypeStruct((PAIR, BUCKETS, 8, TILE), f32),
         ),
-        in_specs=[
-            pl.BlockSpec(memory_space=pltpu.SMEM),
-            one_pair,
-            one_pair,
-            one_pair,
-            one_pair,
-            pl.BlockSpec((1, PAIR, blocks, TILE), lambda j: (j, 0, 0, 0)),
-            pl.BlockSpec((rows, TILE), lambda j: (0, 0)),
-            pl.BlockSpec((blocks, TILE), lambda j: (0, 0)),
-            pl.BlockSpec((PAIR, CLASSES, TILE, TILE), lambda j: (j, 0, 0, 0)),
-        ],
+        in_specs=specs,
         out_specs=(
-            pl.BlockSpec((PAIR * DH, rows), lambda j: (j, 0)),
-            one_pair,
-            one_pair,
-            pl.BlockSpec((PAIR, BUCKETS, 8, TILE), lambda j: (j, 0, 0, 0)),
+            pl.BlockSpec((rows, 3 * PAIR * DH), lambda j: (0, pair)),
+            pl.BlockSpec((PAIR, BUCKETS, 8, TILE), lambda j: (0, 0, 0, 0)),
         ),
         scratch_shapes=[
             pltpu.VMEM((rows, TILE), f32),
@@ -317,9 +454,10 @@
             pltpu.VMEM((rows, rows), bf16),
             pltpu.VMEM((CLASSES, TILE, TILE), f32),
         ],
+        input_output_aliases=aliases,
         compiler_params=pltpu.CompilerParams(vmem_limit_bytes=VMEM_BYTES),
         name="attend_backward",
-    )(base, q, k, v, context_grad, log_total, seg_keys, seg_queries, tiles)
+    )(*operands)
 
 
 def per_device(
@@ -346,11 +484,6 @@
     model = heads * DH
     striped = H % (planes * members) == 0
 
-    def columns(weight, pieces):
-        cut = weight.shape[1] // (pieces * members)
-        split = weight.reshape(weight.shape[0], pieces, members, cut)
-        return lax.dynamic_index_in_dim(split, me, 2, False).reshape(weight.shape[0], pieces * cut)
-
     def own_rows(weight):
         count = weight.shape[0] // members
         return lax.dynamic_slice_in_dim(weight, me * count, count, 0)
@@ -358,17 +491,32 @@
     def over_planes(weight):
         return lax.all_gather(weight, "fsdp", axis=0, tiled=True)
 
+    def sum_planes(partial):
+        return lax.psum_scatter(partial, "fsdp", scatter_dimension=0, tiled=True)
+
+    def trade(summed):
+        moved = summed.reshape(members, -1, summed.shape[1])
+        return lax.all_to_all(moved, "ctx", 0, 0, tiled=True)
+
     head_pieces = planes if striped else 1
-    w_qkv = over_planes(
-        jnp.concatenate([columns(w, head_pieces) for w in (w_query, w_key, w_value)], axis=1)
+    of_heads = head_moves(head_pieces, heads)
+    of_hidden = block_moves(2, planes, hidden // planes)
+    own_qkv = cut_columns(
+        [w_query, w_key, w_value], head_pieces, me, members, of_heads, "cut_heads",
+        w_out if striped else None,
     )
     if striped:
-        out_rows = over_planes(own_rows(w_out))
+        gathered = over_planes(own_qkv)
+        w_qkv = gathered[:, : 3 * model]
+        lanes = gathered.shape[1] - 3 * model
+        out_rows = gathered[:, 3 * model :].reshape(planes, width // lanes, -1, lanes)
+        out_rows = jnp.transpose(out_rows, (0, 2, 1, 3)).reshape(model, width)
     else:
+        w_qkv = over_planes(own_qkv)
         out_rows = lax.dynamic_slice_in_dim(over_planes(w_out), me * model, model, 0)
-    w_mix = over_planes(jnp.concatenate([columns(w_gate, planes), columns(w_up, planes)], axis=1))
+    w_mix = over_planes(cut_columns([w_gate, w_up], planes, me, members, of_hidden, "cut_hidden"))
     down_rows = over_planes(own_rows(w_down))
-    gains = line_gather(jnp.stack([gain_attn, gain_ff])).astype(f32)
+    gains = line_gather(after(jnp.stack([gain_attn, gain_ff]), own_qkv)).astype(f32)
     gain_first, gain_second = gains[0], gains[1]
 
     base = me if by_exchange() else jnp.zeros_like(me)
@@ -388,12 +536,13 @@
     table = jnp.dot(bias_table.astype(f32), pick, precision=lax.Precision.HIGHEST)
     tiles = bias_tiles(table)
 
+    inputs, cotangent = lax.optimization_barrier((inputs, cotangent, own_qkv))[:2]
     source_all = plane_gather(inputs)
     normed = rms_scale(source_all.astype(f32), gain_first).astype(bf16)
+    grad_all = plane_gather(after(cotangent, source_all))
+    normed = after(normed, grad_all, tiles)
     qkv = dot(normed, w_qkv).astype(bf16)
-    q, k, v = qkv[:, :model], qkv[:, model : 2 * model], qkv[:, 2 * model :]
-    context_t, log_total = attend(base_block, q, k, v, seg_keys, seg_queries, tiles)
-    grad_all = plane_gather(cotangent)
+    context_t, log_total = attend(base_block, qkv, seg_keys, seg_queries, tiles)
     source = inputs.astype(f32)
     residual = source + plane_scatter(dot(context_t, out_rows, ((0,), (0,))).astype(bf16))
 
@@ -403,69 +552,85 @@
     active_f, mix_back = jax.vjp(gated_mix, gate_pre, up_pre)
     active = active_f.astype(bf16)
     down_grad = dot(active, grad_all, ((0,), (0,))).astype(bf16)
-    active_grad = dot(grad_all, down_rows, ((1,), (1,)))
+    down_sum = sum_planes(down_grad)
+    active_grad = dot(after(grad_all, down_grad), down_rows, ((1,), (1,)))
     gate_grad, up_grad = mix_back(active_grad)
     mix_grad = jnp.concatenate([gate_grad.astype(bf16), up_grad.astype(bf16)], axis=1)
-    normed_ff_grad = plane_scatter(dot(mix_grad, w_mix, ((1,), (1,))).astype(bf16))
-    output_sum = plane_scatter(dot(active, down_rows).astype(bf16))
-    output = (residual + output_sum).astype(bf16)
+    normed_ff_part = dot(mix_grad, w_mix, ((1,), (1,))).astype(bf16)
+    normed_ff_grad = plane_scatter(normed_ff_part)
+    mix_grad = after(mix_grad, normed_ff_part)
     mix_weight_grad = dot(normed_ff, mix_grad, ((0,), (0,))).astype(bf16)
-    norm_back = jax.vjp(rms_scale, residual, gain_second)[1]
-    residual_part, ff_gain_grad = norm_back(normed_ff_grad)
-    residual_grad = cotangent.astype(f32) + residual_part
-
-    residual_low = plane_gather(residual_grad.astype(bf16))
-    context_grad = dot(residual_low, out_rows, ((1,), (1,))).astype(bf16)
-    out_weight_grad = dot(context_t, residual_low).astype(bf16)
-    query_grad_t, key_grad, value_grad, bias_parts = attend_back(
-        base_block, q, k, v, context_grad, log_total, seg_keys, seg_queries, tiles
-    )
-    w_q, w_kv = w_qkv[:, :model], w_qkv[:, model:]
-    kv_grad = jnp.concatenate([key_grad, value_grad], axis=1)
-    normed_grad = plane_scatter(
-        (dot(query_grad_t, w_q, ((0,), (1,))) + dot(kv_grad, w_kv, ((1,), (1,)))).astype(bf16)
-    )
-    qkv_weight_grad = jnp.concatenate(
-        [dot(normed, query_grad_t, ((0,), (1,))), dot(normed, kv_grad, ((0,), (0,)))], axis=1
-    ).astype(bf16)
-    first_back = jax.vjp(rms_scale, source, gain_first)[1]
-    source_part, attn_gain_grad = first_back(normed_grad)
-    input_grad = (residual_grad + source_part).astype(bf16)
-
-    def sum_planes(partial):
-        return lax.psum_scatter(partial, "fsdp", scatter_dimension=0, tiled=True)
-
-    def to_rows(partial, kinds, pieces):
-        summed = sum_planes(partial)
-        cut = summed.shape[1] // (kinds * pieces)
-        moved = lax.all_to_all(summed, "ctx", 0, 0, tiled=True)
-        moved = moved.reshape(members, summed.shape[0] // members, kinds, pieces, cut)
-        moved = jnp.transpose(moved, (2, 1, 3, 0, 4))
-        return moved.reshape(kinds, moved.shape[1], pieces * members * cut).astype(f32)
-
-    down_shard = sum_planes(down_grad).astype(f32)
-    gate_shard, up_shard = to_rows(mix_weight_grad, 2, planes)
+    mix_sum = sum_planes(mix_weight_grad)
+    norm_back = jax.vjp(lambda v: rms_scale(v, gain_second), residual)[1]
+    residual_grad = cotangent.astype(f32) + norm_back(normed_ff_grad)[0]
+
+    residual_low = plane_gather(after(residual_grad.astype(bf16), down_sum, mix_weight_grad))
+    output_part = dot(after(active, mix_weight_grad), down_rows).astype(bf16)
+    context_grad = dot(after(residual_low, output_part), out_rows, ((1,), (1,))).astype(bf16)
+    output_sums = scatter_chips(after(output_part, residual_low))
+
+    def back(pair, grad, earlier=None):
+        return attend_back(
+            base_block, pair, qkv, grad, log_total, seg_keys, seg_queries, tiles, earlier
+        )
+
+    qkv_grad, bias_parts = back(0, context_grad)
+    bias_parts = [bias_parts]
+    for pair in range(1, heads // PAIR):
+        context_grad = after(context_grad, qkv_grad, output_sums)
+        qkv_grad, more = back(pair, context_grad, qkv_grad)
+        bias_parts.append(more)
+    bias_parts = jnp.concatenate(bias_parts, axis=0)
+    qkv_weight_grad = dot(normed, qkv_grad, ((0,), (0,))).astype(bf16)
+    qkv_sum = sum_planes(qkv_weight_grad)
+    normed_part = dot(after(qkv_grad, qkv_weight_grad), w_qkv, ((1,), (1,))).astype(bf16)
+    moved_mix = trade(mix_sum)
+    normed_sums, moved_mix = lax.optimization_barrier((scatter_chips(normed_part), moved_mix))
+    out_weight_grad = dot(context_t, after(residual_low, moved_mix)).astype(bf16)
+    bias_own = jnp.sum(after(bias_parts, moved_mix), axis=(2, 3))
+    bias_rows = jnp.dot(bias_own.T, pick.T, precision=lax.Precision.HIGHEST)
+    bias_rows = jnp.transpose(bias_rows.reshape(planes, members, -1), (1, 0, 2))
+    bias_rows = jnp.sum(lax.all_to_all(bias_rows, "ctx", 0, 0, tiled=True), axis=0)
+    normed_sums, bias_rows = lax.optimization_barrier((scatter_corner(normed_sums), bias_rows))
+    bias_shard = jnp.sum(lax.all_to_all(bias_rows, "fsdp", 0, 0, tiled=True), axis=0)
+    gate_shard, up_shard = join_columns(moved_mix, 2, planes, of_hidden, "join_hidden")
+    normed_grad, bias_shard, gate_shard, up_shard, output_sums = lax.optimization_barrier(
+        (scatter_sides(normed_sums), bias_shard, gate_shard, up_shard, output_sums)
+    )
+    moved_qkv = trade(after(qkv_sum, normed_grad))
+    output = (residual + scatter_sides(scatter_corner(output_sums))).astype(bf16)
+    first_back = jax.vjp(lambda v: rms_scale(v, gain_first), source)[1]
+    input_grad = (residual_grad + first_back(normed_grad)[0]).astype(bf16)
+
+    def gain_grad(gain, pairs):
+        return sum(jnp.sum(own_rows(w).astype(f32) * g, axis=1) for w, g in pairs) / own_rows(
+            gain
+        ).astype(f32)
+
+    down_shard = down_sum.astype(f32)
+    ff_gain_shard = gain_grad(gain_ff, ((w_gate, gate_shard), (w_up, up_shard)))
+    query_shard, key_shard, value_shard = join_columns(
+        moved_qkv, 3, head_pieces, of_heads, "join_heads"
+    )
+    attn_gain_shard = gain_grad(
+        gain_attn, ((w_query, query_shard), (w_key, key_shard), (w_value, value_shard))
+    )
     if striped:
-        out_shard = sum_planes(out_weight_grad).astype(f32)
+        out_shard = after(sum_planes(out_weight_grad), attn_gain_shard).astype(f32)
     else:
         placed = jnp.zeros((H * DH, width), f32)
         placed = lax.dynamic_update_slice_in_dim(placed, out_weight_grad.astype(f32), me * model, 0)
         out_shard = lax.psum_scatter(placed, ("fsdp", "ctx"), scatter_dimension=0, tiled=True)
-    query_shard, key_shard, value_shard = to_rows(qkv_weight_grad, 3, head_pieces)
-    bias_own = jnp.sum(bias_parts, axis=(2, 3))
-    bias_rows = jnp.dot(bias_own.T, pick.T, precision=lax.Precision.HIGHEST)
-    small = [attn_gain_grad, ff_gain_grad, bias_rows.reshape(BUCKETS * H)]
-    small = [lax.psum_scatter(s, ("fsdp", "ctx"), scatter_dimension=0, tiled=True) for s in small]
     return (
         output,
         input_grad,
-        small[0],
-        small[1],
+        attn_gain_shard,
+        ff_gain_shard,
         query_shard,
         key_shard,
         value_shard,
         out_shard,
-        small[2],
+        bias_shard,
         gate_shard,
         up_shard,
         down_shard,

time: 701 us -> 513 us (0.73)
  waiting for transfers between devices: 296 us -> 174 us
  local copies, waits for them, and re-layouts: 100 us -> 48.6 us
  blocking collectives: 50.8 us -> 0 us
  Pallas kernels: 62.8 us -> 82.6 us
  other arithmetic: 30.9 us -> 46.9 us
    reduce_scatter x4, waiting for transfers between devices: 112 us -> 3.54 us  [sum_planes(): return lax.psum_scatter(partial, 'fsdp', scatter_dimension=0, tiled=True)]
    unnamed x1 -> x0, blocking collectives: 50.8 us -> none
    unnamed x93 -> x96, local copies, waits for them, and re-layouts: 50 us -> 27.9 us
    pallas_call x1 -> x6, Pallas kernels: 36.4 us -> 55.6 us  [the longest x2 40.6 us: attend_back(): pl.pallas_call(functools.partial(backward_kernel, kept=len(aliases)), gri...]
    another operation x12 -> x2, local copies, waits for them, and re-layouts: 18.8 us -> 0.01 us  [per_device(): jnp.stack([gain_attn, gain_ff])]
    convert_element_type x3 -> x0, local copies, waits for them, and re-layouts: 13.7 us -> none  [to_rows(): moved.reshape(kinds, moved.shape[1], pieces * members * cut).astype(f32)]
    ppermute x64, waiting for transfers between devices: 110 us -> 97.6 us  [swap(): lax.ppermute(block, 'ctx', [(i, i ^ mask) for i in range(lax.axis_size('c...]
    convert_element_type x4 -> x10, other arithmetic: 6.79 us -> 18.9 us  [the longest x2 5.77 us: scatter_chips(): diagonal = chip(6).astype(bf16)]
  transfers between devices with their start and end apart: 77 -> 78, of which waited for: 34 -> 40; matrix products, arithmetic and copies ran while one was open for 20% -> 33% of each run, Pallas kernels for 4% -> 15%
where the time goes in v2:
time: 513 us; the launch traced here: 508 us
  waiting for transfers between devices  174 us (34%)
  Pallas kernels  82.6 us (16%)
  matrix products  77.8 us (15%)
  starting transfers between devices  63.2 us (12%)
  local copies, waits for them, and re-layouts  48.6 us (9%)
  other arithmetic  46.9 us (9%)
  between operations  15.4 us (3%)
    ppermute x64, waiting for transfers between devices, swap(): lax.ppermute(block, 'ctx', [(i, i ^ mask) for i in range(lax.axis_size('c...  97.6 us
    dot_general x12, matrix products, dot(): lax.dot_general(left, right, (contract, ((), ())), preferred_element_type...  76.8 us
    all_gather x3, waiting for transfers between devices, over_planes(): return lax.all_gather(weight, 'fsdp', axis=0, tiled=True)  55.4 us
    ppermute x64, starting transfers between devices, swap(): lax.ppermute(block, 'ctx', [(i, i ^ mask) for i in range(lax.axis_size('c...  41.3 us
    pallas_call x2, Pallas kernels, attend_back(): pl.pallas_call(functools.partial(backward_kernel, kept=len(aliases)), gri...  40.6 us
    unnamed x96, local copies, waits for them, and re-layouts  27.9 us
    pallas_call x1, Pallas kernels, attend(): pl.pallas_call(forward_kernel, grid=(pairs,), out_shape=(jax.ShapeDtypeSt...  22.5 us
    all_to_all x2, waiting for transfers between devices, trade(): return lax.all_to_all(moved, 'ctx', 0, 0, tiled=True)  17 us
  transfers between devices with their start and end apart: 78, of which 40 were waited for; matrix products, arithmetic and copies ran while one was open for 33% of the time, Pallas kernels for 15%

profile of v2, /device:TPU:0, one launch (start us, length us, event | category | flops | bytes accessed | tf_op | source)
XLA Modules:
  0.0 508.4 jit_solution(2386355970251673166)
XLA Ops:
  7.9 4.8 cut_heads.1
  12.8 5.1 %collective-permute-start.10 = (bf16[2,512]{1,0:T(2,128)(2,1)S(1)}, bf16[2,512]{1,0:T(2,128)(2,1)S(1)}, u32[]{:S(2)}, u32[]{:S(2)}) collective-permute-start(bf16[2,512]{1,0:T(2,128)(2,1)S(1)} %pad_maximum_fusion.14), channel_id=1, source_target_pairs={{0,24},{8,0},{16,8},{24,16},{1,25},{9,1},{17,9},{25,17},{2,26},{10... | collective-permute-start | bytes 6152 | tf_op jit(solution)/shard_map/ppermute | solution.py:117
  22.5 5.1 %cut_hidden.1 = bf16[512,1280]{1,0:T(8,128)(2,1)} custom-call(s32[3]{0:T(128)} %add_add_fusion.3.start_ref, bf16[512,5120]{1,0:T(8,128)(2,1)} %refs_7_.3, bf16[512,5120]{1,0:T(8,128)(2,1)} %refs_7_.3, bf16[512,5120]{1,0:T(8,128)(2,1)} %refs_7_.3, bf16[512,5120]{1,0:T(8,128)(2,1)} %refs_7_.3, bf16[512,5120]{1,0:T(8,128)(2,1)} %refs_7_.3, ...), custom_call_target="tpu_custom_call" | custom-call | tf_op jit(solution)/shard_map/cut_hidden/pallas_call | solution.py:170
  31.0 4.6 bias_tiles.1.tiles_ref
  39.2 5.3 %collective-permute-done.6 = bf16[64,2048]{1,0:T(8,128)(2,1)S(1)} collective-permute-done((bf16[64,2048]{1,0:T(8,128)(2,1)S(1)}, bf16[64,2048]{1,0:T(8,128)(2,1)S(1)}, u32[]{:S(2)}, u32[]{:S(2)}) %collective-permute-start.6) | collective-permute-done | bytes 262176 | tf_op jit(solution)/shard_map/ppermute | solution.py:55
  59.1 8.5 %collective-permute-done.14 = bf16[128,2048]{1,0:T(8,128)(2,1)S(1)} collective-permute-done((bf16[128,2048]{1,0:T(8,128)(2,1)S(1)}, bf16[128,2048]{1,0:T(8,128)(2,1)S(1)}, u32[]{:S(2)}, u32[]{:S(2)}) %collective-permute-start.14) | collective-permute-done | bytes 524320 | tf_op jit(solution)/shard_map/ppermute | solution.py:55
  82.0 14.3 %all-gather.4.cloned.1.call-done = bf16[2048,1024]{1,0:T(8,128)(2,1)} async-done(((bf16[512,1024]{1,0:T(8,128)(2,1)}), bf16[2048,1024]{1,0:T(8,128)(2,1)}) %all-gather.4.cloned.1.call-update) | async-done | bytes 4194320 | tf_op jit(solution)/shard_map/all_gather | solution.py:492
  98.8 6.4 %fusion.13.q_ref.k_ref.v_ref = bf16[1024,768]{1,0:T(8,128)(2,1)} fusion(bf16[1024,2048]{1,0:T(8,128)(2,1)S(1)} %copy-done.9, bf16[2048,1024]{1,0:T(8,128)(2,1)} %all-gather.4.cloned.1.call-done), kind=kOutput, calls=%fused_computation.34 | convolution fusion | flops 3222011904 | bytes 8912896 | tf_op jit(solution)/shard_map/dot_general | solution.py:51
  106.2 22.5 %attend_forward.1 = (bf16[256,1024]{1,0:T(8,128)(2,1)}, f32[2,2,8,128]{3,2,1,0:T(8,128)}) custom-call(s32[1]{0:T(128)} %bitcast.2.base_ref, bf16[1024,768]{1,0:T(8,128)(2,1)} %fusion.13.q_ref.k_ref.v_ref, bf16[1024,768]{1,0:T(8,128)(2,1)} %fusion.13.q_ref.k_ref.v_ref, bf16[1024,768]{1,0:T(8,128)(2,1)} %fusion.13.q_ref.k_ref.v_ref, ...), custom_call_target="tpu_custom_call" | custom-call | tf_op jit(solution)/shard_map/attend_forward/pallas_call | solution.py:321
  138.3 5.4 %collective-permute-done.25 = bf16[64,2048]{1,0:T(8,128)(2,1)S(1)} collective-permute-done((bf16[64,2048]{1,0:T(8,128)(2,1)S(1)}, bf16[64,2048]{1,0:T(8,128)(2,1)S(1)}, u32[]{:S(2)}, u32[]{:S(2)}) %collective-permute-start.25) | collective-permute-done | bytes 262176 | tf_op jit(solution)/shard_map/ppermute | solution.py:55
  146.9 10.2 %collective-permute-done.26 = bf16[128,2048]{1,0:T(8,128)(2,1)S(1)} collective-permute-done((bf16[128,2048]{1,0:T(8,128)(2,1)S(1)}, bf16[128,2048]{1,0:T(8,128)(2,1)S(1)}, u32[]{:S(2)}, u32[]{:S(2)}) %collective-permute-start.26) | collective-permute-done | bytes 524320 | tf_op jit(solution)/shard_map/ppermute | solution.py:55
  165.4 9.0 %collective-permute-done.30 = bf16[128,2048]{1,0:T(8,128)(2,1)} collective-permute-done((bf16[128,2048]{1,0:T(8,128)(2,1)}, bf16[128,2048]{1,0:T(8,128)(2,1)}, u32[]{:S(2)}, u32[]{:S(2)}) %collective-permute-start.30) | collective-permute-done | bytes 524320 | tf_op jit(solution)/shard_map/ppermute | solution.py:55
  189.1 5.9 %all-gather.6.cloned.1.call-done = bf16[2048,1280]{1,0:T(8,128)(2,1)} async-done(((bf16[512,1280]{1,0:T(8,128)(2,1)}), bf16[2048,1280]{1,0:T(8,128)(2,1)}) %all-gather.6.cloned.1.call-update) | async-done | bytes 5242896 | tf_op jit(solution)/shard_map/all_gather | solution.py:492
  195.1 8.9 %fusion.44 = f32[1024,1280]{1,0:T(8,128)S(1)} fusion(bf16[1024,2048]{1,0:T(8,128)(2,1)} %constant_dynamic-update-slice_fusion.18, bf16[2048,1280]{1,0:T(8,128)(2,1)} %all-gather.6.cloned.1.call-done), kind=kOutput, calls=%fused_computation.181 | convolution fusion | flops 5368709120 | bytes 14680064 | tf_op jit(solution)/shard_map/dot_general | solution.py:51
  208.3 6.6 %convolution_convert_fusion.6 = bf16[640,2048]{1,0:T(8,128)(2,1)} fusion(bf16[1024,640]{1,0:T(8,128)(2,1)S(1)} %multiply_convert_fusion.1, bf16[1024,2048]{1,0:T(8,128)(2,1)} %constant_dynamic-update-slice_fusion.9), kind=kOutput, calls=%fused_computation.14 | convolution fusion | flops 2685665280 | bytes 8126464 | tf_op jit(solution)/shard_map/dot_general | solution.py:51
  215.2 35.2 %all-gather.8.cloned.1.call-done = bf16[640,2048]{1,0:T(8,128)(2,1)} async-done(((bf16[160,2048]{1,0:T(8,128)(2,1)}), bf16[640,2048]{1,0:T(8,128)(2,1)}) %all-gather.8.cloned.1.call-update) | async-done | bytes 2621456 | tf_op jit(solution)/shard_map/all_gather | solution.py:492
  250.4 9.4 %fusion.12 = (bf16[1024,640]{1,0:T(8,128)(2,1)S(1)}, bf16[1024,640]{1,0:T(8,128)(2,1)S(1)}) fusion(f32[1024,1280]{1,0:T(8,128)} %copy-done.5, bf16[1024,2048]{1,0:T(8,128)(2,1)} %constant_dynamic-update-slice_fusion.9, bf16[640,2048]{1,0:T(8,128)(2,1)} %all-gather.8.cloned.1.call-done), kind=kOutput, calls=%fused_computation.24 | convolution fusion | flops 2700083200 | bytes 14680064 | tf_op jit(solution)/shard_map/dot_general | solution.py:51
  260.0 9.9 %convolution_convert_fusion.2 = bf16[1024,2048]{1,0:T(8,128)(2,1)} fusion(bf16[2048,1280]{1,0:T(8,128)(2,1)} %all-gather.6.cloned.1.call-done, bf16[1024,640]{1,0:T(8,128)(2,1)S(1)} %get-tuple-element.111, bf16[1024,640]{1,0:T(8,128)(2,1)S(1)} %get-tuple-element.110), kind=kOutput, calls=%fused_computation.8 | convolution fusion | flops 5376049152 | bytes 12058624 | tf_op jit(solution)/shard_map/dot_general | solution.py:51
  269.9 7.6 %convolution_convert_fusion = bf16[2048,1280]{1,0:T(8,128)(2,1)} fusion(bf16[1024,2048]{1,0:T(8,128)(2,1)S(1)} %copy-done.24, bf16[1024,1280]{1,0:T(8,128)(2,1)S(1)} %pad_maximum_fusion), kind=kOutput, calls=%fused_computation.6 | convolution fusion | flops 5371330560 | bytes 12058624 | tf_op jit(solution)/shard_map/dot_general | solution.py:51
  286.9 5.3 %collective-permute-done.41 = bf16[64,2048]{1,0:T(8,128)(2,1)S(1)} collective-permute-done((bf16[64,2048]{1,0:T(8,128)(2,1)S(1)}, bf16[64,2048]{1,0:T(8,128)(2,1)S(1)}, u32[]{:S(2)}, u32[]{:S(2)}) %collective-permute-start.41) | collective-permute-done | bytes 262176 | tf_op jit(solution)/shard_map/ppermute | solution.py:55
  295.4 10.1 %collective-permute-done.42 = bf16[128,2048]{1,0:T(8,128)(2,1)S(1)} collective-permute-done((bf16[128,2048]{1,0:T(8,128)(2,1)S(1)}, bf16[128,2048]{1,0:T(8,128)(2,1)S(1)}, u32[]{:S(2)}, u32[]{:S(2)}) %collective-permute-start.42) | collective-permute-done | bytes 524320 | tf_op jit(solution)/shard_map/ppermute | solution.py:55
  312.2 5.6 %convolution_convert_fusion.1 = bf16[1024,2048]{1,0:T(8,128)(2,1)S(1)} fusion(bf16[1024,640]{1,0:T(8,128)(2,1)} %copy-done.22, bf16[640,2048]{1,0:T(8,128)(2,1)} %all-gather.8.cloned.1.call-done), kind=kOutput, calls=%fused_computation.7 | convolution fusion | flops 2686451712 | bytes 8126464 | tf_op jit(solution)/shard_map/dot_general | solution.py:51
  317.9 5.3 %collective-permute-done.46 = bf16[128,2048]{1,0:T(8,128)(2,1)S(1)} collective-permute-done((bf16[128,2048]{1,0:T(8,128)(2,1)}, bf16[128,2048]{1,0:T(8,128)(2,1)S(1)}, u32[]{:S(2)}, u32[]{:S(2)}) %collective-permute-start.46) | collective-permute-done | bytes 524320 | tf_op jit(solution)/shard_map/ppermute | solution.py:55
  337.7 20.5 %attend_backward.2 = (bf16[1024,768]{1,0:T(8,128)(2,1)}, f32[2,32,8,128]{3,2,1,0:T(8,128)}) custom-call(s32[1]{0:T(128)} %bitcast.2.base_ref, bf16[1024,768]{1,0:T(8,128)(2,1)} %fusion.13.q_ref.k_ref.v_ref, bf16[1024,768]{1,0:T(8,128)(2,1)} %fusion.13.q_ref.k_ref.v_ref, bf16[1024,768]{1,0:T(8,128)(2,1)} %fusion.13.q_ref.k_ref.v_ref, ...), custom_call_target="tpu_custom_call" | custom-call | tf_op jit(solution)/shard_map/attend_backward/pallas_call | solution.py:438
  361.9 20.1 %attend_backward.3 = (bf16[1024,768]{1,0:T(8,128)(2,1)}, f32[2,32,8,128]{3,2,1,0:T(8,128)}) custom-call(s32[1]{0:T(128)} %bitcast.2.base_ref, bf16[1024,768]{1,0:T(8,128)(2,1)} %fusion.13.q_ref.k_ref.v_ref, bf16[1024,768]{1,0:T(8,128)(2,1)} %fusion.13.q_ref.k_ref.v_ref, bf16[1024,768]{1,0:T(8,128)(2,1)} %fusion.13.q_ref.k_ref.v_ref, ...), custom_call_target="tpu_custom_call", output_to_operand_aliasing={{0}: (9, {})} | custom-call | tf_op jit(solution)/shard_map/attend_backward/pallas_call | solution.py:438
  382.1 6.6 %convolution_convert_fusion.5 = bf16[2048,768]{1,0:T(8,128)(2,1)} fusion(bf16[1024,2048]{1,0:T(8,128)(2,1)S(1)} %copy-done.10, bf16[1024,768]{1,0:T(8,128)(2,1)} %get-tuple-element.73), kind=kOutput, calls=%fused_computation.13 | convolution fusion | flops 3222798336 | bytes 8912896 | tf_op jit(solution)/shard_map/dot_general | solution.py:51
  388.7 6.9 %convolution_convert_fusion.4 = bf16[1024,2048]{1,0:T(8,128)(2,1)} fusion(bf16[1024,768]{1,0:T(8,128)(2,1)S(1)} %copy-done.19, bf16[2048,1024]{1,0:T(8,128)(2,1)} %all-gather.4.cloned.1.call-done), kind=kOutput, calls=%fused_computation.10 | convolution fusion | flops 3223322624 | bytes 8912896 | tf_op jit(solution)/shard_map/dot_general | solution.py:51
  411.2 10.0 %all-to-all-done.in_ref = bf16[8,64,1280]{2,1,0:T(8,128)(2,1)S(1)} async-done(((bf16[8,64,1280]{2,1,0:T(8,128)(2,1)}), bf16[8,64,1280]{2,1,0:T(8,128)(2,1)S(1)}, u32[]{:S(2)}, u32[]{:S(2)}) %all-to-all-start) | async-done | bytes 1310752 | tf_op jit(solution)/shard_map/all_to_all | solution.py:499
  449.2 4.2 all-to-all-start.2
  453.4 4.5 convolution_convert_fusion.7
  464.5 5.4 %collective-permute-done.65 = bf16[64,2048]{1,0:T(8,128)(2,1)S(1)} collective-permute-done((bf16[64,2048]{1,0:T(8,128)(2,1)S(1)}, bf16[64,2048]{1,0:T(8,128)(2,1)S(1)}, u32[]{:S(2)}, u32[]{:S(2)}) %collective-permute-start.65) | collective-permute-done | bytes 262176 | tf_op jit(solution)/shard_map/ppermute | solution.py:55
  485.9 7.1 %all-to-all-done.3.in_ref = bf16[8,64,768]{2,1,0:T(8,128)(2,1)S(1)} async-done(((bf16[8,64,768]{2,1,0:T(8,128)(2,1)}), bf16[8,64,768]{2,1,0:T(8,128)(2,1)S(1)}, u32[]{:S(2)}, u32[]{:S(2)}) %all-to-all-start.3) | async-done | bytes 786464 | tf_op jit(solution)/shard_map/all_to_all | solution.py:499
  (357 shorter events, 196.8 us)
Async XLA Ops:
  7.2 89.1 %all-gather.4.cloned.1.call-start = ((), (), s32[]{:S(2)}) async-start(), calls=%async_computation.8 | async-start | bytes 5242880 | tf_op jit(solution)/shard_map/all_gather | solution.py:492
  12.6 182.4 %all-gather.6.cloned.1.call-start = ((), (), s32[]{:S(2)}) async-start(), calls=%async_computation.9 | async-start | bytes 6553600 | tf_op jit(solution)/shard_map/all_gather | solution.py:492
  12.8 22.9 %collective-permute-start.10 = (bf16[2,512]{1,0:T(2,128)(2,1)S(1)}, bf16[2,512]{1,0:T(2,128)(2,1)S(1)}, u32[]{:S(2)}, u32[]{:S(2)}) collective-permute-start(bf16[2,512]{1,0:T(2,128)(2,1)S(1)} %pad_maximum_fusion.14), channel_id=1, source_target_pairs={{0,24},{8,0},{16,8},{24,16},{1,25},{9,1},{17,9},{25,17},{2,26},{10... | collective-permute-start | bytes 6152 | tf_op jit(solution)/shard_map/ppermute | solution.py:117
  17.9 17.7 %collective-permute-start.9 = (bf16[2,512]{1,0:T(2,128)(2,1)S(1)}, bf16[2,512]{1,0:T(2,128)(2,1)S(1)}, u32[]{:S(2)}, u32[]{:S(2)}) collective-permute-start(bf16[2,512]{1,0:T(2,128)(2,1)S(1)} %pad_maximum_fusion.14), channel_id=1, source_target_pairs={{0,16},{8,24},{16,0},{24,8},{1,17},{9,25},{17,1},{25,9},{2,18},{10... | collective-permute-start | bytes 6152 | tf_op jit(solution)/shard_map/ppermute | solution.py:117
  17.9 17.7 %collective-permute-start.8 = (bf16[2,512]{1,0:T(2,128)(2,1)S(1)}, bf16[2,512]{1,0:T(2,128)(2,1)S(1)}, u32[]{:S(2)}, u32[]{:S(2)}) collective-permute-start(bf16[2,512]{1,0:T(2,128)(2,1)S(1)} %pad_maximum_fusion.14), channel_id=1, source_target_pairs={{0,8},{8,16},{16,24},{24,0},{1,9},{9,17},{17,25},{25,1},{2,10},{10... | collective-permute-start | bytes 6152 | tf_op jit(solution)/shard_map/ppermute | solution.py:117
  18.9 16.8 %collective-permute-start.3 = (bf16[128,2048]{1,0:T(8,128)(2,1)S(1)}, bf16[128,2048]{1,0:T(8,128)(2,1)S(1)}, u32[]{:S(2)}, u32[]{:S(2)}) collective-permute-start(bf16[128,2048]{1,0:T(8,128)(2,1)S(1)} %copy-done.3), channel_id=1, source_target_pairs={{0,4},{1,5},{2,6},{3,7},{4,0},{5,1},{6,2},{7,3},{8,12},{9,13},{10,... | collective-permute-start | bytes 1572872 | tf_op jit(solution)/shard_map/ppermute | solution.py:55
  20.4 16.0 %collective-permute-start.1 = (bf16[128,2048]{1,0:T(8,128)(2,1)S(1)}, bf16[128,2048]{1,0:T(8,128)(2,1)S(1)}, u32[]{:S(2)}, u32[]{:S(2)}) collective-permute-start(bf16[128,2048]{1,0:T(8,128)(2,1)S(1)} %copy-done.3), channel_id=1, source_target_pairs={{0,2},{1,3},{2,0},{3,1},{4,6},{5,7},{6,4},{7,5},{8,10},{9,11},{10,... | collective-permute-start | bytes 1572872 | tf_op jit(solution)/shard_map/ppermute | solution.py:55
  27.6 222.8 %all-gather.8.cloned.1.call-start = ((), (), s32[]{:S(2)}) async-start(), calls=%async_computation.10 | async-start | bytes 3276800 | tf_op jit(solution)/shard_map/all_gather | solution.py:492
  53.2 14.4 %collective-permute-start.14 = (bf16[128,2048]{1,0:T(8,128)(2,1)S(1)}, bf16[128,2048]{1,0:T(8,128)(2,1)S(1)}, u32[]{:S(2)}, u32[]{:S(2)}) collective-permute-start(bf16[128,2048]{1,0:T(8,128)(2,1)S(1)} %copy-done.16), channel_id=1, source_target_pairs={{0,4},{1,5},{2,6},{3,7},{4,0},{5,1},{6,2},{7,3},{8,12},{9,13},{10,... | collective-permute-start | bytes 1572872 | tf_op jit(solution)/shard_map/ppermute | solution.py:55
  53.8 15.4 %collective-permute-start.12 = (bf16[128,2048]{1,0:T(8,128)(2,1)S(1)}, bf16[128,2048]{1,0:T(8,128)(2,1)S(1)}, u32[]{:S(2)}, u32[]{:S(2)}) collective-permute-start(bf16[128,2048]{1,0:T(8,128)(2,1)S(1)} %copy-done.16), channel_id=1, source_target_pairs={{0,2},{1,3},{2,0},{3,1},{4,6},{5,7},{6,4},{7,5},{8,10},{9,11},{10,... | collective-permute-start | bytes 1572872 | tf_op jit(solution)/shard_map/ppermute | solution.py:55
  55.3 15.0 %collective-permute-start.11 = (bf16[128,2048]{1,0:T(8,128)(2,1)S(1)}, bf16[128,2048]{1,0:T(8,128)(2,1)S(1)}, u32[]{:S(2)}, u32[]{:S(2)}) collective-permute-start(bf16[128,2048]{1,0:T(8,128)(2,1)S(1)} %copy-done.16), channel_id=1, source_target_pairs={{0,1},{1,0},{2,3},{3,2},{4,5},{5,4},{6,7},{7,6},{8,9},{9,8},{10,11... | collective-permute-start | bytes 1572872 | tf_op jit(solution)/shard_map/ppermute | solution.py:55
  143.8 13.3 %collective-permute-start.26 = (bf16[128,2048]{1,0:T(8,128)(2,1)S(1)}, bf16[128,2048]{1,0:T(8,128)(2,1)S(1)}, u32[]{:S(2)}, u32[]{:S(2)}) collective-permute-start(bf16[128,2048]{1,0:T(8,128)(2,1)S(1)} %pad_maximum_fusion.4), channel_id=1, source_target_pairs={{0,4},{1,5},{2,6},{3,7},{4,0},{5,1},{6,2},{7,3},{8,12},{9,13},{10,... | collective-permute-start | bytes 1572872 | tf_op jit(solution)/shard_map/ppermute | solution.py:55
  145.7 13.7 %collective-permute-start.23 = (bf16[128,2048]{1,0:T(8,128)(2,1)S(1)}, bf16[128,2048]{1,0:T(8,128)(2,1)S(1)}, u32[]{:S(2)}, u32[]{:S(2)}) collective-permute-start(bf16[128,2048]{1,0:T(8,128)(2,1)S(1)} %pad_maximum_fusion.3), channel_id=1, source_target_pairs={{0,2},{1,3},{2,0},{3,1},{4,6},{5,7},{6,4},{7,5},{8,10},{9,11},{10,... | collective-permute-start | bytes 1572872 | tf_op jit(solution)/shard_map/ppermute | solution.py:55
  161.2 13.2 %collective-permute-start.30 = (bf16[128,2048]{1,0:T(8,128)(2,1)}, bf16[128,2048]{1,0:T(8,128)(2,1)}, u32[]{:S(2)}, u32[]{:S(2)}) collective-permute-start(bf16[128,2048]{1,0:T(8,128)(2,1)} %get-tuple-element.107), channel_id=1, source_target_pairs={{0,4},{1,5},{2,6},{3,7},{4,0},{5,1},{6,2},{7,3},{8,12},{9,13},{10,... | collective-permute-start | bytes 1572872 | tf_op jit(solution)/shard_map/ppermute | solution.py:55
  162.6 13.1 %collective-permute-start.28 = (bf16[128,2048]{1,0:T(8,128)(2,1)}, bf16[128,2048]{1,0:T(8,128)(2,1)}, u32[]{:S(2)}, u32[]{:S(2)}) collective-permute-start(bf16[128,2048]{1,0:T(8,128)(2,1)} %get-tuple-element.107), channel_id=1, source_target_pairs={{0,2},{1,3},{2,0},{3,1},{4,6},{5,7},{6,4},{7,5},{8,10},{9,11},{10,... | collective-permute-start | bytes 1572872 | tf_op jit(solution)/shard_map/ppermute | solution.py:55
  163.2 15.8 %collective-permute-start.27 = (bf16[128,2048]{1,0:T(8,128)(2,1)}, bf16[128,2048]{1,0:T(8,128)(2,1)}, u32[]{:S(2)}, u32[]{:S(2)}) collective-permute-start(bf16[128,2048]{1,0:T(8,128)(2,1)} %get-tuple-element.107), channel_id=1, source_target_pairs={{0,1},{1,0},{2,3},{3,2},{4,5},{5,4},{6,7},{7,6},{8,9},{9,8},{10,11... | collective-permute-start | bytes 1572872 | tf_op jit(solution)/shard_map/ppermute | solution.py:55
  165.2 145.0 %reduce-scatter.5.cloned.1.call-start = ((), (), s32[]{:S(2)}) async-start(), calls=%async_computation.11 | async-start | bytes 3276800 | tf_op jit(solution)/shard_map/reduce_scatter | solution.py:495
  214.9 184.2 %reduce-scatter.7.cloned.1.call-start = ((), (), s32[]{:S(2)}) async-start(), calls=%async_computation.12 | async-start | bytes 6553600 | tf_op jit(solution)/shard_map/reduce_scatter | solution.py:495
  277.5 198.8 %reduce-scatter.9.cloned.1.call-start = ((), (), s32[]{:S(2)}) async-start(), calls=%async_computation.13 | async-start | bytes 3932160 | tf_op jit(solution)/shard_map/reduce_scatter | solution.py:495
  292.2 13.3 %collective-permute-start.42 = (bf16[128,2048]{1,0:T(8,128)(2,1)S(1)}, bf16[128,2048]{1,0:T(8,128)(2,1)S(1)}, u32[]{:S(2)}, u32[]{:S(2)}) collective-permute-start(bf16[128,2048]{1,0:T(8,128)(2,1)S(1)} %pad_maximum_fusion.7), channel_id=1, source_target_pairs={{0,4},{1,5},{2,6},{3,7},{4,0},{5,1},{6,2},{7,3},{8,12},{9,13},{10,... | collective-permute-start | bytes 1572872 | tf_op jit(solution)/shard_map/ppermute | solution.py:55
  294.2 13.7 %collective-permute-start.39 = (bf16[128,2048]{1,0:T(8,128)(2,1)S(1)}, bf16[128,2048]{1,0:T(8,128)(2,1)S(1)}, u32[]{:S(2)}, u32[]{:S(2)}) collective-permute-start(bf16[128,2048]{1,0:T(8,128)(2,1)S(1)} %pad_maximum_fusion.6), channel_id=1, source_target_pairs={{0,2},{1,3},{2,0},{3,1},{4,6},{5,7},{6,4},{7,5},{8,10},{9,11},{10,... | collective-permute-start | bytes 1572872 | tf_op jit(solution)/shard_map/ppermute | solution.py:55
  312.2 13.7 %collective-permute-start.43 = (bf16[128,2048]{1,0:T(8,128)(2,1)}, bf16[128,2048]{1,0:T(8,128)(2,1)S(1)}, u32[]{:S(2)}, u32[]{:S(2)}) collective-permute-start(bf16[128,2048]{1,0:T(8,128)(2,1)} %get-tuple-element.65), channel_id=1, source_target_pairs={{0,1},{1,0},{2,3},{3,2},{4,5},{5,4},{6,7},{7,6},{8,9},{9,8},{10,11... | collective-permute-start | bytes 1572872 | tf_op jit(solution)/shard_map/ppermute | solution.py:55
  334.6 23.6 %collective-permute-start.54 = (bf16[128,2048]{1,0:T(8,128)(2,1)}, bf16[128,2048]{1,0:T(8,128)(2,1)}, u32[]{:S(2)}, u32[]{:S(2)}) collective-permute-start(bf16[128,2048]{1,0:T(8,128)(2,1)} %get-tuple-element.124), channel_id=1, source_target_pairs={{0,1},{1,0},{2,3},{3,2},{4,5},{5,4},{6,7},{7,6},{8,9},{9,8},{10,11... | collective-permute-start | bytes 1572872 | tf_op jit(solution)/shard_map/ppermute | solution.py:55
  334.7 23.4 %collective-permute-start.53 = (bf16[128,2048]{1,0:T(8,128)(2,1)}, bf16[128,2048]{1,0:T(8,128)(2,1)}, u32[]{:S(2)}, u32[]{:S(2)}) collective-permute-start(bf16[128,2048]{1,0:T(8,128)(2,1)} %get-tuple-element.125), channel_id=1, source_target_pairs={{0,1},{1,0},{2,3},{3,2},{4,5},{5,4},{6,7},{7,6},{8,9},{9,8},{10,11... | collective-permute-start | bytes 1572872 | tf_op jit(solution)/shard_map/ppermute | solution.py:55
  335.1 23.1 %collective-permute-start.52 = (bf16[128,2048]{1,0:T(8,128)(2,1)S(1)}, bf16[128,2048]{1,0:T(8,128)(2,1)}, u32[]{:S(2)}, u32[]{:S(2)}) collective-permute-start(bf16[128,2048]{1,0:T(8,128)(2,1)S(1)} %get-tuple-element.126), channel_id=1, source_target_pairs={{0,1},{1,0},{2,3},{3,2},{4,5},{5,4},{6,7},{7,6},{8,9},{9,8},{10,11... | collective-permute-start | bytes 1572872 | tf_op jit(solution)/shard_map/ppermute | solution.py:55
  335.2 22.9 %collective-permute-start.51 = (bf16[128,2048]{1,0:T(8,128)(2,1)S(1)}, bf16[128,2048]{1,0:T(8,128)(2,1)}, u32[]{:S(2)}, u32[]{:S(2)}) collective-permute-start(bf16[128,2048]{1,0:T(8,128)(2,1)S(1)} %get-tuple-element.127), channel_id=1, source_target_pairs={{0,1},{1,0},{2,3},{3,2},{4,5},{5,4},{6,7},{7,6},{8,9},{9,8},{10,11... | collective-permute-start | bytes 1572872 | tf_op jit(solution)/shard_map/ppermute | solution.py:55
  399.1 22.0 %all-to-all-start = ((bf16[8,64,1280]{2,1,0:T(8,128)(2,1)}), bf16[8,64,1280]{2,1,0:T(8,128)(2,1)S(1)}, u32[]{:S(2)}, u32[]{:S(2)}) async-start(bf16[8,64,1280]{2,1,0:T(8,128)(2,1)} %bitcast.70), calls=%async_computation.2 | async-start | bytes 2621440 | tf_op jit(solution)/shard_map/all_to_all | solution.py:499
  422.1 13.6 %collective-permute-start.60 = (bf16[64,2048]{1,0:T(8,128)(2,1)}, bf16[64,2048]{1,0:T(8,128)(2,1)}, u32[]{:S(2)}, u32[]{:S(2)}) collective-permute-start(bf16[64,2048]{1,0:T(8,128)(2,1)} %get-tuple-element.144), channel_id=1, source_target_pairs={{0,2},{1,3},{2,0},{3,1},{4,6},{5,7},{6,4},{7,5},{8,10},{9,11},{10,... | collective-permute-start | bytes 786440 | tf_op jit(solution)/shard_map/ppermute | solution.py:55
  443.8 17.5 %collective-permute-start.61 = (bf16[128,2048]{1,0:T(8,128)(2,1)}, bf16[128,2048]{1,0:T(8,128)(2,1)}, u32[]{:S(2)}, u32[]{:S(2)}) collective-permute-start(bf16[128,2048]{1,0:T(8,128)(2,1)} %pad_maximum_fusion.9), channel_id=1, source_target_pairs={{0,2},{1,3},{2,0},{3,1},{4,6},{5,7},{6,4},{7,5},{8,10},{9,11},{10,... | collective-permute-start | bytes 1572872 | tf_op jit(solution)/shard_map/ppermute | solution.py:55
  445.5 15.9 %collective-permute-start.62 = (bf16[128,2048]{1,0:T(8,128)(2,1)}, bf16[128,2048]{1,0:T(8,128)(2,1)}, u32[]{:S(2)}, u32[]{:S(2)}) collective-permute-start(bf16[128,2048]{1,0:T(8,128)(2,1)} %pad_maximum_fusion.10), channel_id=1, source_target_pairs={{0,4},{1,5},{2,6},{3,7},{4,0},{5,1},{6,2},{7,3},{8,12},{9,13},{10,... | collective-permute-start | bytes 1572872 | tf_op jit(solution)/shard_map/ppermute | solution.py:55
  453.4 46.1 %reduce-scatter.11.cloned.1.call-start = ((), (), s32[]{:S(2)}) async-start(), calls=%async_computation.14 | async-start | bytes 1310720 | tf_op jit(solution)/shard_map/reduce_scatter | solution.py:495
  476.3 16.6 %all-to-all-start.3 = ((bf16[8,64,768]{2,1,0:T(8,128)(2,1)}), bf16[8,64,768]{2,1,0:T(8,128)(2,1)S(1)}, u32[]{:S(2)}, u32[]{:S(2)}) async-start(bf16[8,64,768]{2,1,0:T(8,128)(2,1)} %bitcast.71), calls=%async_computation.6 | async-start | bytes 1572864 | tf_op jit(solution)/shard_map/all_to_all | solution.py:499
  (77 other events, 606.3 us)
Sparse Core Ops, SparseCore 0:
  12.8 83.4 all-gather.3
  98.4 96.6 all-gather.5
  197.2 53.1 all-gather.7
  252.6 50.8 reduce-scatter.4
  305.6 93.4 reduce-scatter.6
  401.3 60.7 reduce-scatter.8
  464.4 27.1 reduce-scatter.10

commit v3 on v2

--- a/solution.py
+++ b/solution.py
@@ -482,7 +482,7 @@
     heads = H // members
     hidden = w_gate.shape[1] // members
     model = heads * DH
-    striped = H % (planes * members) == 0
+    striped = H == planes * members == BUCKETS
 
     def own_rows(weight):
         count = weight.shape[0] // members
@@ -582,23 +582,37 @@
         bias_parts.append(more)
     bias_parts = jnp.concatenate(bias_parts, axis=0)
     qkv_weight_grad = dot(normed, qkv_grad, ((0,), (0,))).astype(bf16)
-    qkv_sum = sum_planes(qkv_weight_grad)
+    bias_own = jnp.sum(bias_parts, axis=(2, 3))
+    qkv_sent = qkv_weight_grad
+    if striped:
+        bias_own = bias_own.T.astype(bf16).reshape(planes, members, heads)
+        bias_own = jnp.pad(bias_own, ((0, 0), (0, 0), (0, 3 * model - heads)))
+        qkv_sent = qkv_sent.reshape(planes, -1, 3 * model)
+        qkv_sent = jnp.concatenate([qkv_sent, bias_own], axis=1).reshape(-1, 3 * model)
+    qkv_sum = sum_planes(qkv_sent)
     normed_part = dot(after(qkv_grad, qkv_weight_grad), w_qkv, ((1,), (1,))).astype(bf16)
+    normed_sums, mix_sum, output_sums = lax.optimization_barrier(
+        (scatter_corner(scatter_chips(normed_part)), mix_sum, scatter_corner(output_sums))
+    )
+    out_weight_grad = dot(context_t, after_all((residual_low,), normed_sums)[0]).astype(bf16)
     moved_mix = trade(mix_sum)
-    normed_sums, moved_mix = lax.optimization_barrier((scatter_chips(normed_part), moved_mix))
-    out_weight_grad = dot(context_t, after(residual_low, moved_mix)).astype(bf16)
-    bias_own = jnp.sum(after(bias_parts, moved_mix), axis=(2, 3))
-    bias_rows = jnp.dot(bias_own.T, pick.T, precision=lax.Precision.HIGHEST)
-    bias_rows = jnp.transpose(bias_rows.reshape(planes, members, -1), (1, 0, 2))
-    bias_rows = jnp.sum(lax.all_to_all(bias_rows, "ctx", 0, 0, tiled=True), axis=0)
-    normed_sums, bias_rows = lax.optimization_barrier((scatter_corner(normed_sums), bias_rows))
-    bias_shard = jnp.sum(lax.all_to_all(bias_rows, "fsdp", 0, 0, tiled=True), axis=0)
+    normed_grad, moved_mix, output_sum = lax.optimization_barrier(
+        (scatter_sides(normed_sums), moved_mix, scatter_sides(output_sums))
+    )
+    output = (residual + output_sum).astype(bf16)
     gate_shard, up_shard = join_columns(moved_mix, 2, planes, of_hidden, "join_hidden")
-    normed_grad, bias_shard, gate_shard, up_shard, output_sums = lax.optimization_barrier(
-        (scatter_sides(normed_sums), bias_shard, gate_shard, up_shard, output_sums)
-    )
-    moved_qkv = trade(after(qkv_sum, normed_grad))
-    output = (residual + scatter_sides(scatter_corner(output_sums))).astype(bf16)
+    qkv_sum = after(qkv_sum, normed_grad)
+    if striped:
+        own = width // planes
+        moved_qkv = [qkv_sum[:own].reshape(members, -1, 3 * model), qkv_sum[own:][:, None]]
+        moved_qkv = jnp.concatenate(moved_qkv, axis=1)
+        moved_qkv = lax.all_to_all(moved_qkv, "ctx", 0, 0, tiled=True)
+        bias_shard = moved_qkv[:, -1, :heads].astype(f32).T.reshape(-1)
+        moved_qkv = moved_qkv[:, :-1]
+    else:
+        moved_qkv = trade(qkv_sum)
+        bias_rows = jnp.dot(bias_own.T, pick.T, precision=lax.Precision.HIGHEST).reshape(-1)
+        bias_shard = lax.psum_scatter(bias_rows, ("fsdp", "ctx"), scatter_dimension=0, tiled=True)
     first_back = jax.vjp(lambda v: rms_scale(v, gain_first), source)[1]
     input_grad = (residual_grad + first_back(normed_grad)[0]).astype(bf16)
 

time: 513 us -> 507 us (0.988)
  starting transfers between devices: 63.2 us -> 57.3 us
    all_to_all x2 -> x1, waiting for transfers between devices: 17 us -> 0.01 us  [trade(): return lax.all_to_all(moved, 'ctx', 0, 0, tiled=True)]
    ppermute x64, waiting for transfers between devices: 97.6 us -> 112 us  [swap(): lax.ppermute(block, 'ctx', [(i, i ^ mask) for i in range(lax.axis_size('c...]
    all_to_all x2 -> x1, waiting for transfers between devices: 0.01 us -> 9.91 us  [per_device(): moved_qkv = lax.all_to_all(moved_qkv, 'ctx', 0, 0, tiled=True)]
    unnamed x96 -> x77, local copies, waits for them, and re-layouts: 27.9 us -> 29.5 us
  transfers between devices with their start and end apart: 78 -> 76, of which waited for: 40 -> 37; matrix products, arithmetic and copies ran while one was open for 33% -> 32% of each run, Pallas kernels for 15% -> 15%
where the time goes in v3:
time: 507 us; the launch traced here: 503 us
  waiting for transfers between devices  178 us (35%)
  Pallas kernels  81.9 us (16%)
  matrix products  74.4 us (15%)
  starting transfers between devices  57.3 us (11%)
  other arithmetic  48.5 us (10%)
  local copies, waits for them, and re-layouts  47.8 us (9%)
  between operations  15.4 us (3%)
    ppermute x64, waiting for transfers between devices, swap(): lax.ppermute(block, 'ctx', [(i, i ^ mask) for i in range(lax.axis_size('c...  112 us
    dot_general x12, matrix products, dot(): lax.dot_general(left, right, (contract, ((), ())), preferred_element_type...  73.7 us
    all_gather x3, waiting for transfers between devices, over_planes(): return lax.all_gather(weight, 'fsdp', axis=0, tiled=True)  55.6 us
    ppermute x64, starting transfers between devices, swap(): lax.ppermute(block, 'ctx', [(i, i ^ mask) for i in range(lax.axis_size('c...  42.3 us
    pallas_call x2, Pallas kernels, attend_back(): pl.pallas_call(functools.partial(backward_kernel, kept=len(aliases)), gri...  40.3 us
    unnamed x77, local copies, waits for them, and re-layouts  29.5 us
    pallas_call x1, Pallas kernels, attend(): pl.pallas_call(forward_kernel, grid=(pairs,), out_shape=(jax.ShapeDtypeSt...  22.5 us
  transfers between devices with their start and end apart: 76, of which 37 were waited for; matrix products, arithmetic and copies ran while one was open for 32% of the time, Pallas kernels for 15%

profile of v3, /device:TPU:0, one launch (start us, length us, event | category | flops | bytes accessed | tf_op | source)
XLA Modules:
  0.0 503.0 jit_solution(14601874781619440731)
XLA Ops:
  7.9 4.8 cut_heads.1
  12.8 5.1 %collective-permute-start.10 = (bf16[2,512]{1,0:T(2,128)(2,1)S(1)}, bf16[2,512]{1,0:T(2,128)(2,1)S(1)}, u32[]{:S(2)}, u32[]{:S(2)}) collective-permute-start(bf16[2,512]{1,0:T(2,128)(2,1)S(1)} %pad_maximum_fusion.14), channel_id=1, source_target_pairs={{0,24},{8,0},{16,8},{24,16},{1,25},{9,1},{17,9},{25,17},{2,26},{10... | collective-permute-start | bytes 6152 | tf_op jit(solution)/shard_map/ppermute | solution.py:117
  22.5 5.1 %cut_hidden.1 = bf16[512,1280]{1,0:T(8,128)(2,1)} custom-call(s32[3]{0:T(128)} %add_add_fusion.3.start_ref, bf16[512,5120]{1,0:T(8,128)(2,1)} %refs_7_.3, bf16[512,5120]{1,0:T(8,128)(2,1)} %refs_7_.3, bf16[512,5120]{1,0:T(8,128)(2,1)} %refs_7_.3, bf16[512,5120]{1,0:T(8,128)(2,1)} %refs_7_.3, bf16[512,5120]{1,0:T(8,128)(2,1)} %refs_7_.3, ...), custom_call_target="tpu_custom_call" | custom-call | tf_op jit(solution)/shard_map/cut_hidden/pallas_call | solution.py:170
  30.9 4.2 bias_tiles.1.tiles_ref
  38.7 5.3 %collective-permute-done.6 = bf16[64,2048]{1,0:T(8,128)(2,1)S(1)} collective-permute-done((bf16[64,2048]{1,0:T(8,128)(2,1)S(1)}, bf16[64,2048]{1,0:T(8,128)(2,1)S(1)}, u32[]{:S(2)}, u32[]{:S(2)}) %collective-permute-start.6) | collective-permute-done | bytes 262176 | tf_op jit(solution)/shard_map/ppermute | solution.py:55
  58.7 8.5 %collective-permute-done.14 = bf16[128,2048]{1,0:T(8,128)(2,1)S(1)} collective-permute-done((bf16[128,2048]{1,0:T(8,128)(2,1)S(1)}, bf16[128,2048]{1,0:T(8,128)(2,1)S(1)}, u32[]{:S(2)}, u32[]{:S(2)}) %collective-permute-start.14) | collective-permute-done | bytes 524320 | tf_op jit(solution)/shard_map/ppermute | solution.py:55
  81.6 14.7 %all-gather.4.cloned.1.call-done = bf16[2048,1024]{1,0:T(8,128)(2,1)} async-done(((bf16[512,1024]{1,0:T(8,128)(2,1)}), bf16[2048,1024]{1,0:T(8,128)(2,1)}) %all-gather.4.cloned.1.call-update) | async-done | bytes 4194320 | tf_op jit(solution)/shard_map/all_gather | solution.py:492
  98.8 6.4 %fusion.15.q_ref.k_ref.v_ref = bf16[1024,768]{1,0:T(8,128)(2,1)} fusion(bf16[1024,2048]{1,0:T(8,128)(2,1)S(1)} %copy-done.6, bf16[2048,1024]{1,0:T(8,128)(2,1)} %all-gather.4.cloned.1.call-done), kind=kOutput, calls=%fused_computation.37 | convolution fusion | flops 3222011904 | bytes 8912896 | tf_op jit(solution)/shard_map/dot_general | solution.py:51
  106.2 22.5 %attend_forward.1 = (bf16[256,1024]{1,0:T(8,128)(2,1)}, f32[2,2,8,128]{3,2,1,0:T(8,128)}) custom-call(s32[1]{0:T(128)} %bitcast.2.base_ref, bf16[1024,768]{1,0:T(8,128)(2,1)} %fusion.15.q_ref.k_ref.v_ref, bf16[1024,768]{1,0:T(8,128)(2,1)} %fusion.15.q_ref.k_ref.v_ref, bf16[1024,768]{1,0:T(8,128)(2,1)} %fusion.15.q_ref.k_ref.v_ref, ...), custom_call_target="tpu_custom_call" | custom-call | tf_op jit(solution)/shard_map/attend_forward/pallas_call | solution.py:321
  138.3 5.4 %collective-permute-done.25 = bf16[64,2048]{1,0:T(8,128)(2,1)S(1)} collective-permute-done((bf16[64,2048]{1,0:T(8,128)(2,1)S(1)}, bf16[64,2048]{1,0:T(8,128)(2,1)S(1)}, u32[]{:S(2)}, u32[]{:S(2)}) %collective-permute-start.25) | collective-permute-done | bytes 262176 | tf_op jit(solution)/shard_map/ppermute | solution.py:55
  146.9 10.2 %collective-permute-done.26 = bf16[128,2048]{1,0:T(8,128)(2,1)S(1)} collective-permute-done((bf16[128,2048]{1,0:T(8,128)(2,1)S(1)}, bf16[128,2048]{1,0:T(8,128)(2,1)S(1)}, u32[]{:S(2)}, u32[]{:S(2)}) %collective-permute-start.26) | collective-permute-done | bytes 524320 | tf_op jit(solution)/shard_map/ppermute | solution.py:55
  165.5 8.9 %collective-permute-done.30 = bf16[128,2048]{1,0:T(8,128)(2,1)} collective-permute-done((bf16[128,2048]{1,0:T(8,128)(2,1)}, bf16[128,2048]{1,0:T(8,128)(2,1)}, u32[]{:S(2)}, u32[]{:S(2)}) %collective-permute-start.30) | collective-permute-done | bytes 524320 | tf_op jit(solution)/shard_map/ppermute | solution.py:55
  189.1 6.0 %all-gather.6.cloned.1.call-done = bf16[2048,1280]{1,0:T(8,128)(2,1)} async-done(((bf16[512,1280]{1,0:T(8,128)(2,1)}), bf16[2048,1280]{1,0:T(8,128)(2,1)}) %all-gather.6.cloned.1.call-update) | async-done | bytes 5242896 | tf_op jit(solution)/shard_map/all_gather | solution.py:492
  195.1 8.9 %fusion.46 = f32[1024,1280]{1,0:T(8,128)S(1)} fusion(bf16[1024,2048]{1,0:T(8,128)(2,1)} %constant_dynamic-update-slice_fusion.18, bf16[2048,1280]{1,0:T(8,128)(2,1)} %all-gather.6.cloned.1.call-done), kind=kOutput, calls=%fused_computation.189 | convolution fusion | flops 5368709120 | bytes 14680064 | tf_op jit(solution)/shard_map/dot_general | solution.py:51
  208.3 6.6 %convolution_convert_fusion.6 = bf16[640,2048]{1,0:T(8,128)(2,1)} fusion(bf16[1024,640]{1,0:T(8,128)(2,1)S(1)} %multiply_convert_fusion.1, bf16[1024,2048]{1,0:T(8,128)(2,1)} %constant_dynamic-update-slice_fusion.9), kind=kOutput, calls=%fused_computation.17 | convolution fusion | flops 2685665280 | bytes 8126464 | tf_op jit(solution)/shard_map/dot_general | solution.py:51
  215.4 35.0 %all-gather.8.cloned.1.call-done = bf16[640,2048]{1,0:T(8,128)(2,1)} async-done(((bf16[160,2048]{1,0:T(8,128)(2,1)}), bf16[640,2048]{1,0:T(8,128)(2,1)}) %all-gather.8.cloned.1.call-update) | async-done | bytes 2621456 | tf_op jit(solution)/shard_map/all_gather | solution.py:492
  250.4 9.4 %fusion.14 = (bf16[1024,640]{1,0:T(8,128)(2,1)S(1)}, bf16[1024,640]{1,0:T(8,128)(2,1)S(1)}) fusion(f32[1024,1280]{1,0:T(8,128)} %copy-done.5, bf16[1024,2048]{1,0:T(8,128)(2,1)} %constant_dynamic-update-slice_fusion.9, bf16[640,2048]{1,0:T(8,128)(2,1)} %all-gather.8.cloned.1.call-done), kind=kOutput, calls=%fused_computation.27 | convolution fusion | flops 2700083200 | bytes 14680064 | tf_op jit(solution)/shard_map/dot_general | solution.py:51
  260.0 8.4 %convolution_convert_fusion.2 = bf16[1024,2048]{1,0:T(8,128)(2,1)S(1)} fusion(bf16[2048,1280]{1,0:T(8,128)(2,1)} %all-gather.6.cloned.1.call-done, bf16[1024,640]{1,0:T(8,128)(2,1)S(1)} %get-tuple-element.95, bf16[1024,640]{1,0:T(8,128)(2,1)S(1)} %get-tuple-element.94), kind=kOutput, calls=%fused_computation.10 | convolution fusion | flops 5376049152 | bytes 12058624 | tf_op jit(solution)/shard_map/dot_general | solution.py:51
  273.4 7.6 %convolution_convert_fusion = bf16[2048,1280]{1,0:T(8,128)(2,1)} fusion(bf16[1024,2048]{1,0:T(8,128)(2,1)S(1)} %copy-done.15, bf16[1024,1280]{1,0:T(8,128)(2,1)S(1)} %pad_maximum_fusion), kind=kOutput, calls=%fused_computation.6 | convolution fusion | flops 5371330560 | bytes 12058624 | tf_op jit(solution)/shard_map/dot_general | solution.py:51
  286.9 4.9 collective-permute-done.41
  295.1 10.3 %collective-permute-done.42 = bf16[128,2048]{1,0:T(8,128)(2,1)S(1)} collective-permute-done((bf16[128,2048]{1,0:T(8,128)(2,1)S(1)}, bf16[128,2048]{1,0:T(8,128)(2,1)S(1)}, u32[]{:S(2)}, u32[]{:S(2)}) %collective-permute-start.42) | collective-permute-done | bytes 524320 | tf_op jit(solution)/shard_map/ppermute | solution.py:55
  314.3 5.6 %convolution_convert_fusion.1 = bf16[1024,2048]{1,0:T(8,128)(2,1)S(1)} fusion(bf16[1024,640]{1,0:T(8,128)(2,1)} %copy-done.10, bf16[640,2048]{1,0:T(8,128)(2,1)} %all-gather.8.cloned.1.call-done), kind=kOutput, calls=%fused_computation.9 | convolution fusion | flops 2686451712 | bytes 8126464 | tf_op jit(solution)/shard_map/dot_general | solution.py:51
  319.9 4.9 collective-permute-done.46
  339.8 20.0 %attend_backward.2 = (bf16[1024,768]{1,0:T(8,128)(2,1)}, f32[2,32,8,128]{3,2,1,0:T(8,128)}) custom-call(s32[1]{0:T(128)} %bitcast.2.base_ref, bf16[1024,768]{1,0:T(8,128)(2,1)} %fusion.15.q_ref.k_ref.v_ref, bf16[1024,768]{1,0:T(8,128)(2,1)} %fusion.15.q_ref.k_ref.v_ref, bf16[1024,768]{1,0:T(8,128)(2,1)} %fusion.15.q_ref.k_ref.v_ref, ...), custom_call_target="tpu_custom_call" | custom-call | tf_op jit(solution)/shard_map/attend_backward/pallas_call | solution.py:438
  363.5 20.3 %attend_backward.3 = (bf16[1024,768]{1,0:T(8,128)(2,1)}, f32[2,32,8,128]{3,2,1,0:T(8,128)}) custom-call(s32[1]{0:T(128)} %bitcast.2.base_ref, bf16[1024,768]{1,0:T(8,128)(2,1)} %fusion.15.q_ref.k_ref.v_ref, bf16[1024,768]{1,0:T(8,128)(2,1)} %fusion.15.q_ref.k_ref.v_ref, bf16[1024,768]{1,0:T(8,128)(2,1)} %fusion.15.q_ref.k_ref.v_ref, ...), custom_call_target="tpu_custom_call", output_to_operand_aliasing={{0}: (9, {})} | custom-call | tf_op jit(solution)/shard_map/attend_backward/pallas_call | solution.py:438
  385.1 6.2 %convolution_convert_fusion.5 = bf16[2048,768]{1,0:T(8,128)(2,1)S(1)} fusion(bf16[1024,2048]{1,0:T(8,128)(2,1)} %fusion.2, bf16[1024,768]{1,0:T(8,128)(2,1)} %get-tuple-element.65), kind=kOutput, calls=%fused_computation.15 | convolution fusion | flops 3222798336 | bytes 8912896 | tf_op jit(solution)/shard_map/dot_general | solution.py:51
  396.2 5.8 %convolution_convert_fusion.4 = bf16[1024,2048]{1,0:T(8,128)(2,1)S(1)} fusion(bf16[1024,768]{1,0:T(8,128)(2,1)} %get-tuple-element.65, bf16[2048,1024]{1,0:T(8,128)(2,1)} %all-gather.4.cloned.1.call-done), kind=kOutput, calls=%fused_computation.12 | convolution fusion | flops 3223322624 | bytes 8912896 | tf_op jit(solution)/shard_map/dot_general | solution.py:51
  411.5 5.0 collective-permute-done.60
  422.7 4.3 all-to-all-start
  427.0 4.4 convolution_convert_fusion.7
  437.7 20.0 %collective-permute-done.65 = bf16[128,2048]{1,0:T(8,128)(2,1)} collective-permute-done((bf16[128,2048]{1,0:T(8,128)(2,1)}, bf16[128,2048]{1,0:T(8,128)(2,1)}, u32[]{:S(2)}, u32[]{:S(2)}) %collective-permute-start.65) | collective-permute-done | bytes 524320 | tf_op jit(solution)/shard_map/ppermute | solution.py:55
  476.8 9.9 %all-to-all-done.1 = bf16[8,65,768]{2,1,0:T(8,128)(2,1)S(1)} async-done(((bf16[8,65,768]{2,1,0:T(8,128)(2,1)}), bf16[8,65,768]{2,1,0:T(8,128)(2,1)S(1)}, u32[]{:S(2)}, u32[]{:S(2)}) %all-to-all-start.1) | async-done | bytes 798752 | tf_op jit(solution)/shard_map/all_to_all | solution.py:609
  (335 shorter events, 183.2 us)
Async XLA Ops:
  7.2 89.1 %all-gather.4.cloned.1.call-start = ((), (), s32[]{:S(2)}) async-start(), calls=%async_computation.6 | async-start | bytes 5242880 | tf_op jit(solution)/shard_map/all_gather | solution.py:492
  12.6 182.4 %all-gather.6.cloned.1.call-start = ((), (), s32[]{:S(2)}) async-start(), calls=%async_computation.7 | async-start | bytes 6553600 | tf_op jit(solution)/shard_map/all_gather | solution.py:492
  12.8 22.4 %collective-permute-start.10 = (bf16[2,512]{1,0:T(2,128)(2,1)S(1)}, bf16[2,512]{1,0:T(2,128)(2,1)S(1)}, u32[]{:S(2)}, u32[]{:S(2)}) collective-permute-start(bf16[2,512]{1,0:T(2,128)(2,1)S(1)} %pad_maximum_fusion.14), channel_id=1, source_target_pairs={{0,24},{8,0},{16,8},{24,16},{1,25},{9,1},{17,9},{25,17},{2,26},{10... | collective-permute-start | bytes 6152 | tf_op jit(solution)/shard_map/ppermute | solution.py:117
  17.9 17.3 %collective-permute-start.9 = (bf16[2,512]{1,0:T(2,128)(2,1)S(1)}, bf16[2,512]{1,0:T(2,128)(2,1)S(1)}, u32[]{:S(2)}, u32[]{:S(2)}) collective-permute-start(bf16[2,512]{1,0:T(2,128)(2,1)S(1)} %pad_maximum_fusion.14), channel_id=1, source_target_pairs={{0,16},{8,24},{16,0},{24,8},{1,17},{9,25},{17,1},{25,9},{2,18},{10... | collective-permute-start | bytes 6152 | tf_op jit(solution)/shard_map/ppermute | solution.py:117
  17.9 17.3 %collective-permute-start.8 = (bf16[2,512]{1,0:T(2,128)(2,1)S(1)}, bf16[2,512]{1,0:T(2,128)(2,1)S(1)}, u32[]{:S(2)}, u32[]{:S(2)}) collective-permute-start(bf16[2,512]{1,0:T(2,128)(2,1)S(1)} %pad_maximum_fusion.14), channel_id=1, source_target_pairs={{0,8},{8,16},{16,24},{24,0},{1,9},{9,17},{17,25},{25,1},{2,10},{10... | collective-permute-start | bytes 6152 | tf_op jit(solution)/shard_map/ppermute | solution.py:117
  18.9 16.4 %collective-permute-start.3 = (bf16[128,2048]{1,0:T(8,128)(2,1)S(1)}, bf16[128,2048]{1,0:T(8,128)(2,1)S(1)}, u32[]{:S(2)}, u32[]{:S(2)}) collective-permute-start(bf16[128,2048]{1,0:T(8,128)(2,1)S(1)} %copy-done.3), channel_id=1, source_target_pairs={{0,4},{1,5},{2,6},{3,7},{4,0},{5,1},{6,2},{7,3},{8,12},{9,13},{10,... | collective-permute-start | bytes 1572872 | tf_op jit(solution)/shard_map/ppermute | solution.py:55
  20.4 15.6 %collective-permute-start.1 = (bf16[128,2048]{1,0:T(8,128)(2,1)S(1)}, bf16[128,2048]{1,0:T(8,128)(2,1)S(1)}, u32[]{:S(2)}, u32[]{:S(2)}) collective-permute-start(bf16[128,2048]{1,0:T(8,128)(2,1)S(1)} %copy-done.3), channel_id=1, source_target_pairs={{0,2},{1,3},{2,0},{3,1},{4,6},{5,7},{6,4},{7,5},{8,10},{9,11},{10,... | collective-permute-start | bytes 1572872 | tf_op jit(solution)/shard_map/ppermute | solution.py:55
  27.6 222.8 %all-gather.8.cloned.1.call-start = ((), (), s32[]{:S(2)}) async-start(), calls=%async_computation.8 | async-start | bytes 3276800 | tf_op jit(solution)/shard_map/all_gather | solution.py:492
  52.8 14.4 %collective-permute-start.14 = (bf16[128,2048]{1,0:T(8,128)(2,1)S(1)}, bf16[128,2048]{1,0:T(8,128)(2,1)S(1)}, u32[]{:S(2)}, u32[]{:S(2)}) collective-permute-start(bf16[128,2048]{1,0:T(8,128)(2,1)S(1)} %copy-done.8), channel_id=1, source_target_pairs={{0,4},{1,5},{2,6},{3,7},{4,0},{5,1},{6,2},{7,3},{8,12},{9,13},{10,... | collective-permute-start | bytes 1572872 | tf_op jit(solution)/shard_map/ppermute | solution.py:55
  53.4 15.4 %collective-permute-start.12 = (bf16[128,2048]{1,0:T(8,128)(2,1)S(1)}, bf16[128,2048]{1,0:T(8,128)(2,1)S(1)}, u32[]{:S(2)}, u32[]{:S(2)}) collective-permute-start(bf16[128,2048]{1,0:T(8,128)(2,1)S(1)} %copy-done.8), channel_id=1, source_target_pairs={{0,2},{1,3},{2,0},{3,1},{4,6},{5,7},{6,4},{7,5},{8,10},{9,11},{10,... | collective-permute-start | bytes 1572872 | tf_op jit(solution)/shard_map/ppermute | solution.py:55
  54.9 15.0 %collective-permute-start.11 = (bf16[128,2048]{1,0:T(8,128)(2,1)S(1)}, bf16[128,2048]{1,0:T(8,128)(2,1)S(1)}, u32[]{:S(2)}, u32[]{:S(2)}) collective-permute-start(bf16[128,2048]{1,0:T(8,128)(2,1)S(1)} %copy-done.8), channel_id=1, source_target_pairs={{0,1},{1,0},{2,3},{3,2},{4,5},{5,4},{6,7},{7,6},{8,9},{9,8},{10,11... | collective-permute-start | bytes 1572872 | tf_op jit(solution)/shard_map/ppermute | solution.py:55
  143.8 13.3 %collective-permute-start.26 = (bf16[128,2048]{1,0:T(8,128)(2,1)S(1)}, bf16[128,2048]{1,0:T(8,128)(2,1)S(1)}, u32[]{:S(2)}, u32[]{:S(2)}) collective-permute-start(bf16[128,2048]{1,0:T(8,128)(2,1)S(1)} %pad_maximum_fusion.5), channel_id=1, source_target_pairs={{0,4},{1,5},{2,6},{3,7},{4,0},{5,1},{6,2},{7,3},{8,12},{9,13},{10,... | collective-permute-start | bytes 1572872 | tf_op jit(solution)/shard_map/ppermute | solution.py:55
  145.7 13.7 %collective-permute-start.23 = (bf16[128,2048]{1,0:T(8,128)(2,1)S(1)}, bf16[128,2048]{1,0:T(8,128)(2,1)S(1)}, u32[]{:S(2)}, u32[]{:S(2)}) collective-permute-start(bf16[128,2048]{1,0:T(8,128)(2,1)S(1)} %pad_maximum_fusion.4), channel_id=1, source_target_pairs={{0,2},{1,3},{2,0},{3,1},{4,6},{5,7},{6,4},{7,5},{8,10},{9,11},{10,... | collective-permute-start | bytes 1572872 | tf_op jit(solution)/shard_map/ppermute | solution.py:55
  161.2 13.2 %collective-permute-start.30 = (bf16[128,2048]{1,0:T(8,128)(2,1)}, bf16[128,2048]{1,0:T(8,128)(2,1)}, u32[]{:S(2)}, u32[]{:S(2)}) collective-permute-start(bf16[128,2048]{1,0:T(8,128)(2,1)} %get-tuple-element.91), channel_id=1, source_target_pairs={{0,4},{1,5},{2,6},{3,7},{4,0},{5,1},{6,2},{7,3},{8,12},{9,13},{10,... | collective-permute-start | bytes 1572872 | tf_op jit(solution)/shard_map/ppermute | solution.py:55
  163.2 15.8 %collective-permute-start.27 = (bf16[128,2048]{1,0:T(8,128)(2,1)}, bf16[128,2048]{1,0:T(8,128)(2,1)}, u32[]{:S(2)}, u32[]{:S(2)}) collective-permute-start(bf16[128,2048]{1,0:T(8,128)(2,1)} %get-tuple-element.91), channel_id=1, source_target_pairs={{0,1},{1,0},{2,3},{3,2},{4,5},{5,4},{6,7},{7,6},{8,9},{9,8},{10,11... | collective-permute-start | bytes 1572872 | tf_op jit(solution)/shard_map/ppermute | solution.py:55
  165.2 147.1 %reduce-scatter.5.cloned.1.call-start = ((), (), s32[]{:S(2)}) async-start(), calls=%async_computation.9 | async-start | bytes 3276800 | tf_op jit(solution)/shard_map/reduce_scatter | solution.py:495
  215.0 204.1 %reduce-scatter.7.cloned.1.call-start = ((), (), s32[]{:S(2)}) async-start(), calls=%async_computation.10 | async-start | bytes 6553600 | tf_op jit(solution)/shard_map/reduce_scatter | solution.py:495
  281.0 185.6 %reduce-scatter.9.cloned.1.call-start = ((), (), s32[]{:S(2)}) async-start(), calls=%async_computation.11 | async-start | bytes 3993600 | tf_op jit(solution)/shard_map/reduce_scatter | solution.py:495
  291.9 13.5 %collective-permute-start.42 = (bf16[128,2048]{1,0:T(8,128)(2,1)S(1)}, bf16[128,2048]{1,0:T(8,128)(2,1)S(1)}, u32[]{:S(2)}, u32[]{:S(2)}) collective-permute-start(bf16[128,2048]{1,0:T(8,128)(2,1)S(1)} %pad_maximum_fusion.8), channel_id=1, source_target_pairs={{0,4},{1,5},{2,6},{3,7},{4,0},{5,1},{6,2},{7,3},{8,12},{9,13},{10,... | collective-permute-start | bytes 1572872 | tf_op jit(solution)/shard_map/ppermute | solution.py:55
  294.7 13.3 %collective-permute-start.39 = (bf16[128,2048]{1,0:T(8,128)(2,1)S(1)}, bf16[128,2048]{1,0:T(8,128)(2,1)S(1)}, u32[]{:S(2)}, u32[]{:S(2)}) collective-permute-start(bf16[128,2048]{1,0:T(8,128)(2,1)S(1)} %pad_maximum_fusion.7), channel_id=1, source_target_pairs={{0,2},{1,3},{2,0},{3,1},{4,6},{5,7},{6,4},{7,5},{8,10},{9,11},{10,... | collective-permute-start | bytes 1572872 | tf_op jit(solution)/shard_map/ppermute | solution.py:55
  314.3 13.7 %collective-permute-start.43 = (bf16[128,2048]{1,0:T(8,128)(2,1)}, bf16[128,2048]{1,0:T(8,128)(2,1)S(1)}, u32[]{:S(2)}, u32[]{:S(2)}) collective-permute-start(bf16[128,2048]{1,0:T(8,128)(2,1)} %get-tuple-element.57), channel_id=1, source_target_pairs={{0,1},{1,0},{2,3},{3,2},{4,5},{5,4},{6,7},{7,6},{8,9},{9,8},{10,11... | collective-permute-start | bytes 1572872 | tf_op jit(solution)/shard_map/ppermute | solution.py:55
  336.7 23.1 %collective-permute-start.54 = (bf16[128,2048]{1,0:T(8,128)(2,1)}, bf16[128,2048]{1,0:T(8,128)(2,1)}, u32[]{:S(2)}, u32[]{:S(2)}) collective-permute-start(bf16[128,2048]{1,0:T(8,128)(2,1)} %get-tuple-element.108), channel_id=1, source_target_pairs={{0,1},{1,0},{2,3},{3,2},{4,5},{5,4},{6,7},{7,6},{8,9},{9,8},{10,11... | collective-permute-start | bytes 1572872 | tf_op jit(solution)/shard_map/ppermute | solution.py:55
  336.9 23.0 %collective-permute-start.53 = (bf16[128,2048]{1,0:T(8,128)(2,1)}, bf16[128,2048]{1,0:T(8,128)(2,1)}, u32[]{:S(2)}, u32[]{:S(2)}) collective-permute-start(bf16[128,2048]{1,0:T(8,128)(2,1)} %get-tuple-element.109), channel_id=1, source_target_pairs={{0,1},{1,0},{2,3},{3,2},{4,5},{5,4},{6,7},{7,6},{8,9},{9,8},{10,11... | collective-permute-start | bytes 1572872 | tf_op jit(solution)/shard_map/ppermute | solution.py:55
  337.2 22.6 %collective-permute-start.52 = (bf16[128,2048]{1,0:T(8,128)(2,1)S(1)}, bf16[128,2048]{1,0:T(8,128)(2,1)}, u32[]{:S(2)}, u32[]{:S(2)}) collective-permute-start(bf16[128,2048]{1,0:T(8,128)(2,1)S(1)} %get-tuple-element.110), channel_id=1, source_target_pairs={{0,1},{1,0},{2,3},{3,2},{4,5},{5,4},{6,7},{7,6},{8,9},{9,8},{10,11... | collective-permute-start | bytes 1572872 | tf_op jit(solution)/shard_map/ppermute | solution.py:55
  337.4 22.5 %collective-permute-start.51 = (bf16[128,2048]{1,0:T(8,128)(2,1)S(1)}, bf16[128,2048]{1,0:T(8,128)(2,1)}, u32[]{:S(2)}, u32[]{:S(2)}) collective-permute-start(bf16[128,2048]{1,0:T(8,128)(2,1)S(1)} %get-tuple-element.111), channel_id=1, source_target_pairs={{0,1},{1,0},{2,3},{3,2},{4,5},{5,4},{6,7},{7,6},{8,9},{9,8},{10,11... | collective-permute-start | bytes 1572872 | tf_op jit(solution)/shard_map/ppermute | solution.py:55
  419.1 15.7 %collective-permute-start.63 = (bf16[128,2048]{1,0:T(8,128)(2,1)}, bf16[128,2048]{1,0:T(8,128)(2,1)}, u32[]{:S(2)}, u32[]{:S(2)}) collective-permute-start(bf16[128,2048]{1,0:T(8,128)(2,1)} %pad_maximum_fusion.10), channel_id=1, source_target_pairs={{0,2},{1,3},{2,0},{3,1},{4,6},{5,7},{6,4},{7,5},{8,10},{9,11},{10,... | collective-permute-start | bytes 1572872 | tf_op jit(solution)/shard_map/ppermute | solution.py:55
  420.2 15.8 %collective-permute-start.64 = (bf16[128,2048]{1,0:T(8,128)(2,1)}, bf16[128,2048]{1,0:T(8,128)(2,1)}, u32[]{:S(2)}, u32[]{:S(2)}) collective-permute-start(bf16[128,2048]{1,0:T(8,128)(2,1)} %pad_maximum_fusion.11), channel_id=1, source_target_pairs={{0,4},{1,5},{2,6},{3,7},{4,0},{5,1},{6,2},{7,3},{8,12},{9,13},{10,... | collective-permute-start | bytes 1572872 | tf_op jit(solution)/shard_map/ppermute | solution.py:55
  422.7 38.4 %all-to-all-start = ((bf16[8,64,1280]{2,1,0:T(8,128)(2,1)}), bf16[8,64,1280]{2,1,0:T(8,128)(2,1)}, u32[]{:S(2)}, u32[]{:S(2)}) async-start(bf16[8,64,1280]{2,1,0:T(8,128)(2,1)} %bitcast.73), calls=%async_computation.2 | async-start | bytes 2621440 | tf_op jit(solution)/shard_map/all_to_all | solution.py:499
  427.0 67.2 %reduce-scatter.11.cloned.1.call-start = ((), (), s32[]{:S(2)}) async-start(), calls=%async_computation.12 | async-start | bytes 1310720 | tf_op jit(solution)/shard_map/reduce_scatter | solution.py:495
  431.5 26.2 %collective-permute-start.65 = (bf16[128,2048]{1,0:T(8,128)(2,1)}, bf16[128,2048]{1,0:T(8,128)(2,1)}, u32[]{:S(2)}, u32[]{:S(2)}) collective-permute-start(bf16[128,2048]{1,0:T(8,128)(2,1)} %pad_maximum_fusion.12), channel_id=1, source_target_pairs={{0,2},{1,3},{2,0},{3,1},{4,6},{5,7},{6,4},{7,5},{8,10},{9,11},{10,... | collective-permute-start | bytes 1572872 | tf_op jit(solution)/shard_map/ppermute | solution.py:55
  433.3 25.1 %collective-permute-start.66 = (bf16[128,2048]{1,0:T(8,128)(2,1)S(1)}, bf16[128,2048]{1,0:T(8,128)(2,1)}, u32[]{:S(2)}, u32[]{:S(2)}) collective-permute-start(bf16[128,2048]{1,0:T(8,128)(2,1)S(1)} %pad_maximum_fusion.13), channel_id=1, source_target_pairs={{0,4},{1,5},{2,6},{3,7},{4,0},{5,1},{6,2},{7,3},{8,12},{9,13},{10,... | collective-permute-start | bytes 1572872 | tf_op jit(solution)/shard_map/ppermute | solution.py:55
  469.6 17.1 %all-to-all-start.1 = ((bf16[8,65,768]{2,1,0:T(8,128)(2,1)}), bf16[8,65,768]{2,1,0:T(8,128)(2,1)S(1)}, u32[]{:S(2)}, u32[]{:S(2)}) async-start(bf16[8,65,768]{2,1,0:T(8,128)(2,1)} %pad_maximum_fusion.1), calls=%async_computation.4 | async-start | bytes 1769472 | tf_op jit(solution)/shard_map/all_to_all | solution.py:609
  (66 other events, 500.9 us)
Sparse Core Ops, SparseCore 0:
  12.8 83.4 all-gather.3
  98.4 96.6 all-gather.5
  197.2 53.1 all-gather.7
  252.6 50.8 reduce-scatter.4
  305.6 93.4 reduce-scatter.6
  401.3 61.6 reduce-scatter.8
  465.4 27.2 reduce-scatter.10

commit v4 on v3

--- a/solution.py
+++ b/solution.py
@@ -180,6 +180,66 @@
         out_shape=jax.ShapeDtypeStruct((rows, columns), bf16),
         name=name,
     )(jnp.stack([start, shift, me]).astype(jnp.int32), *operands)
+
+
+def cut_heads_kernel(q_ref, k_ref, v_ref, rows_ref, out_ref, held, held_rows, sems, *, pieces, members):
+    me = lax.axis_index("ctx")
+    tiles = members * DH // TILE
+    weights = (q_ref, k_ref, v_ref)
+    count = held_rows.shape[0]
+    copies = []
+    for source, weight in enumerate(weights):
+        for piece in range(pieces):
+            first = pl.multiple_of((piece * tiles + me * DH // TILE) * TILE, TILE)
+            at = source * pieces + piece
+            copies.append(
+                pltpu.make_async_copy(weight.at[:, pl.ds(first, TILE)], held.at[at], sems.at[at])
+            )
+    first = pl.multiple_of(me * count, count)
+    copies.append(
+        pltpu.make_async_copy(
+            rows_ref.at[pl.ds(first, count), :], held_rows, sems.at[len(weights) * pieces]
+        )
+    )
+    for copy in copies:
+        copy.start()
+    row = lax.broadcasted_iota(jnp.int32, (TILE, TILE), 0)
+    column = lax.broadcasted_iota(jnp.int32, (TILE, TILE), 1)
+    same = row - lax.rem(me * DH, TILE) == lax.rem(column, DH)
+    pick = [(same & (column // DH == side)).astype(bf16) for side in range(2)]
+    for source in range(len(weights)):
+        for pair in range(pieces // 2):
+            at = source * pieces + 2 * pair
+            copies[at].wait()
+            copies[at + 1].wait()
+            both = jnp.dot(held[at], pick[0], preferred_element_type=f32)
+            both = both + jnp.dot(held[at + 1], pick[1], preferred_element_type=f32)
+            target = (pair * 3 + source) * TILE
+            out_ref[:, target : target + TILE] = both.astype(bf16)
+    copies[-1].wait()
+    along = out_ref.shape[1] - len(weights) * pieces * DH
+    for group in range(held_rows.shape[1] // along):
+        part = held_rows[:, group * along : (group + 1) * along]
+        out_ref[group * count : (group + 1) * count, out_ref.shape[1] - along :] = part
+
+
+def cut_heads_at_once(w_query, w_key, w_value, w_out, pieces, members):
+    rows, width = w_query.shape
+    count = w_out.shape[0] // members
+    columns = 3 * pieces * DH + count * width // rows
+    return pl.pallas_call(
+        functools.partial(cut_heads_kernel, pieces=pieces, members=members),
+        out_shape=jax.ShapeDtypeStruct((rows, columns), bf16),
+        in_specs=[pl.BlockSpec(memory_space=pl.ANY)] * 4,
+        out_specs=pl.BlockSpec(memory_space=pltpu.VMEM),
+        scratch_shapes=[
+            pltpu.VMEM((3 * pieces, rows, TILE), bf16),
+            pltpu.VMEM((count, width), bf16),
+            pltpu.SemaphoreType.DMA((3 * pieces + 1,)),
+        ],
+        compiler_params=pltpu.CompilerParams(vmem_limit_bytes=VMEM_BYTES),
+        name="cut_heads",
+    )(w_query, w_key, w_value, w_out)
 
 
 def join_kernel(in_ref, *out_refs, pieces, cut, moves):
@@ -501,10 +561,12 @@
     head_pieces = planes if striped else 1
     of_heads = head_moves(head_pieces, heads)
     of_hidden = block_moves(2, planes, hidden // planes)
-    own_qkv = cut_columns(
-        [w_query, w_key, w_value], head_pieces, me, members, of_heads, "cut_heads",
-        w_out if striped else None,
-    )
+    if striped:
+        own_qkv = cut_heads_at_once(w_query, w_key, w_value, w_out, planes, members)
+    else:
+        own_qkv = cut_columns(
+            [w_query, w_key, w_value], head_pieces, me, members, of_heads, "cut_heads"
+        )
     if striped:
         gathered = over_planes(own_qkv)
         w_qkv = gathered[:, : 3 * model]

time: 507 us -> 506 us (level)
    ppermute x64, waiting for transfers between devices: 112 us -> 106 us  [swap(): lax.ppermute(block, 'ctx', [(i, i ^ mask) for i in range(lax.axis_size('c...]
where the time goes in v4:
time: 506 us; the launch traced here: 501 us
  waiting for transfers between devices  176 us (35%)
  Pallas kernels  80.7 us (16%)
  matrix products  74.5 us (15%)
  starting transfers between devices  59.4 us (12%)
  local copies, waits for them, and re-layouts  47.8 us (9%)
  other arithmetic  47.7 us (9%)
  between operations  15.3 us (3%)
    ppermute x64, waiting for transfers between devices, swap(): lax.ppermute(block, 'ctx', [(i, i ^ mask) for i in range(lax.axis_size('c...  106 us
    dot_general x12, matrix products, dot(): lax.dot_general(left, right, (contract, ((), ())), preferred_element_type...  73.7 us
    all_gather x3, waiting for transfers between devices, over_planes(): return lax.all_gather(weight, 'fsdp', axis=0, tiled=True)  56.3 us
    ppermute x64, starting transfers between devices, swap(): lax.ppermute(block, 'ctx', [(i, i ^ mask) for i in range(lax.axis_size('c...  44.8 us
    pallas_call x2, Pallas kernels, attend_back(): pl.pallas_call(functools.partial(backward_kernel, kept=len(aliases)), gri...  40.3 us
    unnamed x77, local copies, waits for them, and re-layouts  29.5 us
    pallas_call x1, Pallas kernels, attend(): pl.pallas_call(forward_kernel, grid=(pairs,), out_shape=(jax.ShapeDtypeSt...  22.5 us
  transfers between devices with their start and end apart: 76, of which 37 were waited for; matrix products, arithmetic and copies ran while one was open for 32% of the time, Pallas kernels for 15%

profile of v4, /device:TPU:0, one launch (start us, length us, event | category | flops | bytes accessed | tf_op | source)
XLA Modules:
  0.0 501.3 jit_solution(8405277681058555926)
XLA Ops:
  7.3 3.8 cut_heads.1
  20.6 5.1 %cut_hidden.1 = bf16[512,1280]{1,0:T(8,128)(2,1)} custom-call(s32[3]{0:T(128)} %pad_add_fusion.start_ref, bf16[512,5120]{1,0:T(8,128)(2,1)} %refs_7_.1, bf16[512,5120]{1,0:T(8,128)(2,1)} %refs_7_.1, bf16[512,5120]{1,0:T(8,128)(2,1)} %refs_7_.1, bf16[512,5120]{1,0:T(8,128)(2,1)} %refs_7_.1, bf16[512,5120]{1,0:T(8,128)(2,1)} %refs_7_.1, ...), custom_call_target="tpu_custom_call" | custom-call | tf_op jit(solution)/shard_map/cut_hidden/pallas_call | solution.py:170
  29.0 4.0 bias_tiles.1.tiles_ref
  60.7 5.7 %collective-permute-done.12 = bf16[128,2048]{1,0:T(8,128)(2,1)S(1)} collective-permute-done((bf16[128,2048]{1,0:T(8,128)(2,1)S(1)}, bf16[128,2048]{1,0:T(8,128)(2,1)S(1)}, u32[]{:S(2)}, u32[]{:S(2)}) %collective-permute-start.12) | collective-permute-done | bytes 524320 | tf_op jit(solution)/shard_map/ppermute | solution.py:55
  79.4 15.3 %all-gather.4.cloned.1.call-done = bf16[2048,1024]{1,0:T(8,128)(2,1)} async-done(((bf16[512,1024]{1,0:T(8,128)(2,1)}), bf16[2048,1024]{1,0:T(8,128)(2,1)}) %all-gather.4.cloned.1.call-update) | async-done | bytes 4194320 | tf_op jit(solution)/shard_map/all_gather | solution.py:552
  97.2 6.4 %fusion.15.q_ref.k_ref.v_ref = bf16[1024,768]{1,0:T(8,128)(2,1)} fusion(bf16[1024,2048]{1,0:T(8,128)(2,1)S(1)} %copy-done.6, bf16[2048,1024]{1,0:T(8,128)(2,1)} %all-gather.4.cloned.1.call-done), kind=kOutput, calls=%fused_computation.37 | convolution fusion | flops 3222011904 | bytes 8912896 | tf_op jit(solution)/shard_map/dot_general | solution.py:51
  104.6 22.5 %attend_forward.1 = (bf16[256,1024]{1,0:T(8,128)(2,1)}, f32[2,2,8,128]{3,2,1,0:T(8,128)}) custom-call(s32[1]{0:T(128)} %bitcast.base_ref, bf16[1024,768]{1,0:T(8,128)(2,1)} %fusion.15.q_ref.k_ref.v_ref, bf16[1024,768]{1,0:T(8,128)(2,1)} %fusion.15.q_ref.k_ref.v_ref, bf16[1024,768]{1,0:T(8,128)(2,1)} %fusion.15.q_ref.k_ref.v_ref, ...), custom_call_target="tpu_custom_call" | custom-call | tf_op jit(solution)/shard_map/attend_forward/pallas_call | solution.py:381
  136.9 5.2 %collective-permute-done.22 = bf16[64,2048]{1,0:T(8,128)(2,1)S(1)} collective-permute-done((bf16[64,2048]{1,0:T(8,128)(2,1)S(1)}, bf16[64,2048]{1,0:T(8,128)(2,1)S(1)}, u32[]{:S(2)}, u32[]{:S(2)}) %collective-permute-start.22) | collective-permute-done | bytes 262176 | tf_op jit(solution)/shard_map/ppermute | solution.py:55
  145.5 10.1 %collective-permute-done.23 = bf16[128,2048]{1,0:T(8,128)(2,1)S(1)} collective-permute-done((bf16[128,2048]{1,0:T(8,128)(2,1)S(1)}, bf16[128,2048]{1,0:T(8,128)(2,1)S(1)}, u32[]{:S(2)}, u32[]{:S(2)}) %collective-permute-start.23) | collective-permute-done | bytes 524320 | tf_op jit(solution)/shard_map/ppermute | solution.py:55
  163.9 8.9 %collective-permute-done.28 = bf16[128,2048]{1,0:T(8,128)(2,1)} collective-permute-done((bf16[128,2048]{1,0:T(8,128)(2,1)}, bf16[128,2048]{1,0:T(8,128)(2,1)}, u32[]{:S(2)}, u32[]{:S(2)}) %collective-permute-start.28) | collective-permute-done | bytes 524320 | tf_op jit(solution)/shard_map/ppermute | solution.py:55
  187.5 5.9 %all-gather.6.cloned.1.call-done = bf16[2048,1280]{1,0:T(8,128)(2,1)} async-done(((bf16[512,1280]{1,0:T(8,128)(2,1)}), bf16[2048,1280]{1,0:T(8,128)(2,1)}) %all-gather.6.cloned.1.call-update) | async-done | bytes 5242896 | tf_op jit(solution)/shard_map/all_gather | solution.py:552
  193.5 8.9 %fusion.46 = f32[1024,1280]{1,0:T(8,128)S(1)} fusion(bf16[1024,2048]{1,0:T(8,128)(2,1)} %constant_dynamic-update-slice_fusion.18, bf16[2048,1280]{1,0:T(8,128)(2,1)} %all-gather.6.cloned.1.call-done), kind=kOutput, calls=%fused_computation.188 | convolution fusion | flops 5368709120 | bytes 14680064 | tf_op jit(solution)/shard_map/dot_general | solution.py:51
  206.7 6.6 %convolution_convert_fusion.6 = bf16[640,2048]{1,0:T(8,128)(2,1)} fusion(bf16[1024,640]{1,0:T(8,128)(2,1)S(1)} %multiply_convert_fusion.1, bf16[1024,2048]{1,0:T(8,128)(2,1)} %constant_dynamic-update-slice_fusion.9), kind=kOutput, calls=%fused_computation.17 | convolution fusion | flops 2685665280 | bytes 8126464 | tf_op jit(solution)/shard_map/dot_general | solution.py:51
  213.9 35.0 %all-gather.8.cloned.1.call-done = bf16[640,2048]{1,0:T(8,128)(2,1)} async-done(((bf16[160,2048]{1,0:T(8,128)(2,1)}), bf16[640,2048]{1,0:T(8,128)(2,1)}) %all-gather.8.cloned.1.call-update) | async-done | bytes 2621456 | tf_op jit(solution)/shard_map/all_gather | solution.py:552
  248.9 9.4 %fusion.14 = (bf16[1024,640]{1,0:T(8,128)(2,1)S(1)}, bf16[1024,640]{1,0:T(8,128)(2,1)S(1)}) fusion(f32[1024,1280]{1,0:T(8,128)} %copy-done.5, bf16[1024,2048]{1,0:T(8,128)(2,1)} %constant_dynamic-update-slice_fusion.9, bf16[640,2048]{1,0:T(8,128)(2,1)} %all-gather.8.cloned.1.call-done), kind=kOutput, calls=%fused_computation.27 | convolution fusion | flops 2700083200 | bytes 14680064 | tf_op jit(solution)/shard_map/dot_general | solution.py:51
  258.4 8.4 %convolution_convert_fusion.2 = bf16[1024,2048]{1,0:T(8,128)(2,1)S(1)} fusion(bf16[2048,1280]{1,0:T(8,128)(2,1)} %all-gather.6.cloned.1.call-done, bf16[1024,640]{1,0:T(8,128)(2,1)S(1)} %get-tuple-element.95, bf16[1024,640]{1,0:T(8,128)(2,1)S(1)} %get-tuple-element.94), kind=kOutput, calls=%fused_computation.10 | convolution fusion | flops 5376049152 | bytes 12058624 | tf_op jit(solution)/shard_map/dot_general | solution.py:51
  271.8 7.6 %convolution_convert_fusion = bf16[2048,1280]{1,0:T(8,128)(2,1)} fusion(bf16[1024,2048]{1,0:T(8,128)(2,1)S(1)} %copy-done.15, bf16[1024,1280]{1,0:T(8,128)(2,1)S(1)} %pad_maximum_fusion), kind=kOutput, calls=%fused_computation.6 | convolution fusion | flops 5371330560 | bytes 12058624 | tf_op jit(solution)/shard_map/dot_general | solution.py:51
  285.4 4.9 collective-permute-done.38
  293.6 10.3 %collective-permute-done.39 = bf16[128,2048]{1,0:T(8,128)(2,1)S(1)} collective-permute-done((bf16[128,2048]{1,0:T(8,128)(2,1)S(1)}, bf16[128,2048]{1,0:T(8,128)(2,1)S(1)}, u32[]{:S(2)}, u32[]{:S(2)}) %collective-permute-start.39) | collective-permute-done | bytes 524320 | tf_op jit(solution)/shard_map/ppermute | solution.py:55
  312.7 5.6 %convolution_convert_fusion.1 = bf16[1024,2048]{1,0:T(8,128)(2,1)S(1)} fusion(bf16[1024,640]{1,0:T(8,128)(2,1)} %copy-done.10, bf16[640,2048]{1,0:T(8,128)(2,1)} %all-gather.8.cloned.1.call-done), kind=kOutput, calls=%fused_computation.9 | convolution fusion | flops 2686451712 | bytes 8126464 | tf_op jit(solution)/shard_map/dot_general | solution.py:51
  318.3 4.9 collective-permute-done.44
  326.5 3.6 collective-permute-done.48
  338.2 20.0 %attend_backward.2 = (bf16[1024,768]{1,0:T(8,128)(2,1)}, f32[2,32,8,128]{3,2,1,0:T(8,128)}) custom-call(s32[1]{0:T(128)} %bitcast.base_ref, bf16[1024,768]{1,0:T(8,128)(2,1)} %fusion.15.q_ref.k_ref.v_ref, bf16[1024,768]{1,0:T(8,128)(2,1)} %fusion.15.q_ref.k_ref.v_ref, bf16[1024,768]{1,0:T(8,128)(2,1)} %fusion.15.q_ref.k_ref.v_ref, ...), custom_call_target="tpu_custom_call" | custom-call | tf_op jit(solution)/shard_map/attend_backward/pallas_call | solution.py:498
  358.3 3.6 add_convert_fusion.2
  361.9 20.3 %attend_backward.3 = (bf16[1024,768]{1,0:T(8,128)(2,1)}, f32[2,32,8,128]{3,2,1,0:T(8,128)}) custom-call(s32[1]{0:T(128)} %bitcast.base_ref, bf16[1024,768]{1,0:T(8,128)(2,1)} %fusion.15.q_ref.k_ref.v_ref, bf16[1024,768]{1,0:T(8,128)(2,1)} %fusion.15.q_ref.k_ref.v_ref, bf16[1024,768]{1,0:T(8,128)(2,1)} %fusion.15.q_ref.k_ref.v_ref, ...), custom_call_target="tpu_custom_call", output_to_operand_aliasing={{0}: (9, {})} | custom-call | tf_op jit(solution)/shard_map/attend_backward/pallas_call | solution.py:498
  383.5 6.2 %convolution_convert_fusion.5 = bf16[2048,768]{1,0:T(8,128)(2,1)S(1)} fusion(bf16[1024,2048]{1,0:T(8,128)(2,1)} %fusion.2, bf16[1024,768]{1,0:T(8,128)(2,1)} %get-tuple-element.65), kind=kOutput, calls=%fused_computation.15 | convolution fusion | flops 3222798336 | bytes 8912896 | tf_op jit(solution)/shard_map/dot_general | solution.py:51
  394.6 5.8 %convolution_convert_fusion.4 = bf16[1024,2048]{1,0:T(8,128)(2,1)S(1)} fusion(bf16[1024,768]{1,0:T(8,128)(2,1)} %get-tuple-element.65, bf16[2048,1024]{1,0:T(8,128)(2,1)} %all-gather.4.cloned.1.call-done), kind=kOutput, calls=%fused_computation.12 | convolution fusion | flops 3223322624 | bytes 8912896 | tf_op jit(solution)/shard_map/dot_general | solution.py:51
  409.9 5.0 collective-permute-done.60
  420.8 4.3 all-to-all-start
  425.1 4.4 convolution_convert_fusion.7
  436.0 20.2 %collective-permute-done.65 = bf16[128,2048]{1,0:T(8,128)(2,1)} collective-permute-done((bf16[128,2048]{1,0:T(8,128)(2,1)}, bf16[128,2048]{1,0:T(8,128)(2,1)}, u32[]{:S(2)}, u32[]{:S(2)}) %collective-permute-start.65) | collective-permute-done | bytes 524320 | tf_op jit(solution)/shard_map/ppermute | solution.py:55
  475.2 9.9 %all-to-all-done.1 = bf16[8,65,768]{2,1,0:T(8,128)(2,1)S(1)} async-done(((bf16[8,65,768]{2,1,0:T(8,128)(2,1)}), bf16[8,65,768]{2,1,0:T(8,128)(2,1)S(1)}, u32[]{:S(2)}, u32[]{:S(2)}) %all-to-all-start.1) | async-done | bytes 798752 | tf_op jit(solution)/shard_map/all_to_all | solution.py:671
  (334 shorter events, 188.2 us)
Async XLA Ops:
  7.2 87.5 %all-gather.4.cloned.1.call-start = ((), (), s32[]{:S(2)}) async-start(), calls=%async_computation.6 | async-start | bytes 5242880 | tf_op jit(solution)/shard_map/all_gather | solution.py:552
  11.1 182.4 %all-gather.6.cloned.1.call-start = ((), (), s32[]{:S(2)}) async-start(), calls=%async_computation.7 | async-start | bytes 6553600 | tf_op jit(solution)/shard_map/all_gather | solution.py:552
  11.1 29.3 %collective-permute-start = (bf16[128,2048]{1,0:T(8,128)(2,1)S(1)}, bf16[128,2048]{1,0:T(8,128)(2,1)S(1)}, u32[]{:S(2)}, u32[]{:S(2)}) collective-permute-start(bf16[128,2048]{1,0:T(8,128)(2,1)S(1)} %copy-done.3), channel_id=1, source_target_pairs={{0,1},{1,0},{2,3},{3,2},{4,5},{5,4},{6,7},{7,6},{8,9},{9,8},{10,11... | collective-permute-start | bytes 1572872 | tf_op jit(solution)/shard_map/ppermute | solution.py:55
  11.7 26.5 %collective-permute-start.1 = (bf16[128,2048]{1,0:T(8,128)(2,1)S(1)}, bf16[128,2048]{1,0:T(8,128)(2,1)S(1)}, u32[]{:S(2)}, u32[]{:S(2)}) collective-permute-start(bf16[128,2048]{1,0:T(8,128)(2,1)S(1)} %copy-done.3), channel_id=1, source_target_pairs={{0,2},{1,3},{2,0},{3,1},{4,6},{5,7},{6,4},{7,5},{8,10},{9,11},{10,... | collective-permute-start | bytes 1572872 | tf_op jit(solution)/shard_map/ppermute | solution.py:55
  14.2 25.5 %collective-permute-start.3 = (bf16[128,2048]{1,0:T(8,128)(2,1)S(1)}, bf16[128,2048]{1,0:T(8,128)(2,1)S(1)}, u32[]{:S(2)}, u32[]{:S(2)}) collective-permute-start(bf16[128,2048]{1,0:T(8,128)(2,1)S(1)} %copy-done.3), channel_id=1, source_target_pairs={{0,4},{1,5},{2,6},{3,7},{4,0},{5,1},{6,2},{7,3},{8,12},{9,13},{10,... | collective-permute-start | bytes 1572872 | tf_op jit(solution)/shard_map/ppermute | solution.py:55
  15.8 17.3 %collective-permute-start.8 = (bf16[2,512]{1,0:T(2,128)(2,1)S(1)}, bf16[2,512]{1,0:T(2,128)(2,1)S(1)}, u32[]{:S(2)}, u32[]{:S(2)}) collective-permute-start(bf16[2,512]{1,0:T(2,128)(2,1)S(1)} %pad_maximum_fusion.14), channel_id=1, source_target_pairs={{0,8},{8,16},{16,24},{24,0},{1,9},{9,17},{17,25},{25,1},{2,10},{10... | collective-permute-start | bytes 6152 | tf_op jit(solution)/shard_map/ppermute | solution.py:117
  17.4 17.1 %collective-permute-start.9 = (bf16[2,512]{1,0:T(2,128)(2,1)S(1)}, bf16[2,512]{1,0:T(2,128)(2,1)S(1)}, u32[]{:S(2)}, u32[]{:S(2)}) collective-permute-start(bf16[2,512]{1,0:T(2,128)(2,1)S(1)} %pad_maximum_fusion.14), channel_id=1, source_target_pairs={{0,16},{8,24},{16,0},{24,8},{1,17},{9,25},{17,1},{25,9},{2,18},{10... | collective-permute-start | bytes 6152 | tf_op jit(solution)/shard_map/ppermute | solution.py:117
  25.7 223.1 %all-gather.8.cloned.1.call-start = ((), (), s32[]{:S(2)}) async-start(), calls=%async_computation.8 | async-start | bytes 3276800 | tf_op jit(solution)/shard_map/all_gather | solution.py:552
  52.1 17.1 %collective-permute-start.11 = (bf16[128,2048]{1,0:T(8,128)(2,1)S(1)}, bf16[128,2048]{1,0:T(8,128)(2,1)S(1)}, u32[]{:S(2)}, u32[]{:S(2)}) collective-permute-start(bf16[128,2048]{1,0:T(8,128)(2,1)S(1)} %copy-done.8), channel_id=1, source_target_pairs={{0,1},{1,0},{2,3},{3,2},{4,5},{5,4},{6,7},{7,6},{8,9},{9,8},{10,11... | collective-permute-start | bytes 1572872 | tf_op jit(solution)/shard_map/ppermute | solution.py:55
  52.6 13.8 %collective-permute-start.12 = (bf16[128,2048]{1,0:T(8,128)(2,1)S(1)}, bf16[128,2048]{1,0:T(8,128)(2,1)S(1)}, u32[]{:S(2)}, u32[]{:S(2)}) collective-permute-start(bf16[128,2048]{1,0:T(8,128)(2,1)S(1)} %copy-done.8), channel_id=1, source_target_pairs={{0,2},{1,3},{2,0},{3,1},{4,6},{5,7},{6,4},{7,5},{8,10},{9,11},{10,... | collective-permute-start | bytes 1572872 | tf_op jit(solution)/shard_map/ppermute | solution.py:55
  52.7 14.4 %collective-permute-start.14 = (bf16[128,2048]{1,0:T(8,128)(2,1)S(1)}, bf16[128,2048]{1,0:T(8,128)(2,1)S(1)}, u32[]{:S(2)}, u32[]{:S(2)}) collective-permute-start(bf16[128,2048]{1,0:T(8,128)(2,1)S(1)} %copy-done.8), channel_id=1, source_target_pairs={{0,4},{1,5},{2,6},{3,7},{4,0},{5,1},{6,2},{7,3},{8,12},{9,13},{10,... | collective-permute-start | bytes 1572872 | tf_op jit(solution)/shard_map/ppermute | solution.py:55
  142.2 13.3 %collective-permute-start.23 = (bf16[128,2048]{1,0:T(8,128)(2,1)S(1)}, bf16[128,2048]{1,0:T(8,128)(2,1)S(1)}, u32[]{:S(2)}, u32[]{:S(2)}) collective-permute-start(bf16[128,2048]{1,0:T(8,128)(2,1)S(1)} %pad_maximum_fusion.4), channel_id=1, source_target_pairs={{0,2},{1,3},{2,0},{3,1},{4,6},{5,7},{6,4},{7,5},{8,10},{9,11},{10,... | collective-permute-start | bytes 1572872 | tf_op jit(solution)/shard_map/ppermute | solution.py:55
  144.1 13.7 %collective-permute-start.26 = (bf16[128,2048]{1,0:T(8,128)(2,1)S(1)}, bf16[128,2048]{1,0:T(8,128)(2,1)S(1)}, u32[]{:S(2)}, u32[]{:S(2)}) collective-permute-start(bf16[128,2048]{1,0:T(8,128)(2,1)S(1)} %pad_maximum_fusion.5), channel_id=1, source_target_pairs={{0,4},{1,5},{2,6},{3,7},{4,0},{5,1},{6,2},{7,3},{8,12},{9,13},{10,... | collective-permute-start | bytes 1572872 | tf_op jit(solution)/shard_map/ppermute | solution.py:55
  159.6 13.2 %collective-permute-start.28 = (bf16[128,2048]{1,0:T(8,128)(2,1)}, bf16[128,2048]{1,0:T(8,128)(2,1)}, u32[]{:S(2)}, u32[]{:S(2)}) collective-permute-start(bf16[128,2048]{1,0:T(8,128)(2,1)} %get-tuple-element.91), channel_id=1, source_target_pairs={{0,2},{1,3},{2,0},{3,1},{4,6},{5,7},{6,4},{7,5},{8,10},{9,11},{10,... | collective-permute-start | bytes 1572872 | tf_op jit(solution)/shard_map/ppermute | solution.py:55
  161.6 15.8 %collective-permute-start.27 = (bf16[128,2048]{1,0:T(8,128)(2,1)}, bf16[128,2048]{1,0:T(8,128)(2,1)}, u32[]{:S(2)}, u32[]{:S(2)}) collective-permute-start(bf16[128,2048]{1,0:T(8,128)(2,1)} %get-tuple-element.91), channel_id=1, source_target_pairs={{0,1},{1,0},{2,3},{3,2},{4,5},{5,4},{6,7},{7,6},{8,9},{9,8},{10,11... | collective-permute-start | bytes 1572872 | tf_op jit(solution)/shard_map/ppermute | solution.py:55
  163.6 147.1 %reduce-scatter.5.cloned.1.call-start = ((), (), s32[]{:S(2)}) async-start(), calls=%async_computation.9 | async-start | bytes 3276800 | tf_op jit(solution)/shard_map/reduce_scatter | solution.py:555
  213.4 204.3 %reduce-scatter.7.cloned.1.call-start = ((), (), s32[]{:S(2)}) async-start(), calls=%async_computation.10 | async-start | bytes 6553600 | tf_op jit(solution)/shard_map/reduce_scatter | solution.py:555
  279.4 185.5 %reduce-scatter.9.cloned.1.call-start = ((), (), s32[]{:S(2)}) async-start(), calls=%async_computation.11 | async-start | bytes 3993600 | tf_op jit(solution)/shard_map/reduce_scatter | solution.py:555
  290.4 13.4 %collective-permute-start.39 = (bf16[128,2048]{1,0:T(8,128)(2,1)S(1)}, bf16[128,2048]{1,0:T(8,128)(2,1)S(1)}, u32[]{:S(2)}, u32[]{:S(2)}) collective-permute-start(bf16[128,2048]{1,0:T(8,128)(2,1)S(1)} %pad_maximum_fusion.7), channel_id=1, source_target_pairs={{0,2},{1,3},{2,0},{3,1},{4,6},{5,7},{6,4},{7,5},{8,10},{9,11},{10,... | collective-permute-start | bytes 1572872 | tf_op jit(solution)/shard_map/ppermute | solution.py:55
  293.1 13.3 %collective-permute-start.42 = (bf16[128,2048]{1,0:T(8,128)(2,1)S(1)}, bf16[128,2048]{1,0:T(8,128)(2,1)S(1)}, u32[]{:S(2)}, u32[]{:S(2)}) collective-permute-start(bf16[128,2048]{1,0:T(8,128)(2,1)S(1)} %pad_maximum_fusion.8), channel_id=1, source_target_pairs={{0,4},{1,5},{2,6},{3,7},{4,0},{5,1},{6,2},{7,3},{8,12},{9,13},{10,... | collective-permute-start | bytes 1572872 | tf_op jit(solution)/shard_map/ppermute | solution.py:55
  312.7 13.7 %collective-permute-start.43 = (bf16[128,2048]{1,0:T(8,128)(2,1)}, bf16[128,2048]{1,0:T(8,128)(2,1)S(1)}, u32[]{:S(2)}, u32[]{:S(2)}) collective-permute-start(bf16[128,2048]{1,0:T(8,128)(2,1)} %get-tuple-element.57), channel_id=1, source_target_pairs={{0,1},{1,0},{2,3},{3,2},{4,5},{5,4},{6,7},{7,6},{8,9},{9,8},{10,11... | collective-permute-start | bytes 1572872 | tf_op jit(solution)/shard_map/ppermute | solution.py:55
  335.1 23.1 %collective-permute-start.51 = (bf16[128,2048]{1,0:T(8,128)(2,1)}, bf16[128,2048]{1,0:T(8,128)(2,1)}, u32[]{:S(2)}, u32[]{:S(2)}) collective-permute-start(bf16[128,2048]{1,0:T(8,128)(2,1)} %get-tuple-element.111), channel_id=1, source_target_pairs={{0,1},{1,0},{2,3},{3,2},{4,5},{5,4},{6,7},{7,6},{8,9},{9,8},{10,11... | collective-permute-start | bytes 1572872 | tf_op jit(solution)/shard_map/ppermute | solution.py:55
  335.3 23.0 %collective-permute-start.52 = (bf16[128,2048]{1,0:T(8,128)(2,1)}, bf16[128,2048]{1,0:T(8,128)(2,1)}, u32[]{:S(2)}, u32[]{:S(2)}) collective-permute-start(bf16[128,2048]{1,0:T(8,128)(2,1)} %get-tuple-element.110), channel_id=1, source_target_pairs={{0,1},{1,0},{2,3},{3,2},{4,5},{5,4},{6,7},{7,6},{8,9},{9,8},{10,11... | collective-permute-start | bytes 1572872 | tf_op jit(solution)/shard_map/ppermute | solution.py:55
  335.6 22.6 %collective-permute-start.53 = (bf16[128,2048]{1,0:T(8,128)(2,1)S(1)}, bf16[128,2048]{1,0:T(8,128)(2,1)}, u32[]{:S(2)}, u32[]{:S(2)}) collective-permute-start(bf16[128,2048]{1,0:T(8,128)(2,1)S(1)} %get-tuple-element.109), channel_id=1, source_target_pairs={{0,1},{1,0},{2,3},{3,2},{4,5},{5,4},{6,7},{7,6},{8,9},{9,8},{10,11... | collective-permute-start | bytes 1572872 | tf_op jit(solution)/shard_map/ppermute | solution.py:55
  335.8 22.5 %collective-permute-start.54 = (bf16[128,2048]{1,0:T(8,128)(2,1)S(1)}, bf16[128,2048]{1,0:T(8,128)(2,1)}, u32[]{:S(2)}, u32[]{:S(2)}) collective-permute-start(bf16[128,2048]{1,0:T(8,128)(2,1)S(1)} %get-tuple-element.108), channel_id=1, source_target_pairs={{0,1},{1,0},{2,3},{3,2},{4,5},{5,4},{6,7},{7,6},{8,9},{9,8},{10,11... | collective-permute-start | bytes 1572872 | tf_op jit(solution)/shard_map/ppermute | solution.py:55
  417.8 15.2 %collective-permute-start.63 = (bf16[128,2048]{1,0:T(8,128)(2,1)}, bf16[128,2048]{1,0:T(8,128)(2,1)}, u32[]{:S(2)}, u32[]{:S(2)}) collective-permute-start(bf16[128,2048]{1,0:T(8,128)(2,1)} %pad_maximum_fusion.10), channel_id=1, source_target_pairs={{0,2},{1,3},{2,0},{3,1},{4,6},{5,7},{6,4},{7,5},{8,10},{9,11},{10,... | collective-permute-start | bytes 1572872 | tf_op jit(solution)/shard_map/ppermute | solution.py:55
  418.5 15.8 %collective-permute-start.64 = (bf16[128,2048]{1,0:T(8,128)(2,1)}, bf16[128,2048]{1,0:T(8,128)(2,1)}, u32[]{:S(2)}, u32[]{:S(2)}) collective-permute-start(bf16[128,2048]{1,0:T(8,128)(2,1)} %pad_maximum_fusion.11), channel_id=1, source_target_pairs={{0,4},{1,5},{2,6},{3,7},{4,0},{5,1},{6,2},{7,3},{8,12},{9,13},{10,... | collective-permute-start | bytes 1572872 | tf_op jit(solution)/shard_map/ppermute | solution.py:55
  420.8 38.7 %all-to-all-start = ((bf16[8,64,1280]{2,1,0:T(8,128)(2,1)}), bf16[8,64,1280]{2,1,0:T(8,128)(2,1)}, u32[]{:S(2)}, u32[]{:S(2)}) async-start(bf16[8,64,1280]{2,1,0:T(8,128)(2,1)} %bitcast.71), calls=%async_computation.2 | async-start | bytes 2621440 | tf_op jit(solution)/shard_map/all_to_all | solution.py:559
  425.0 66.8 %reduce-scatter.11.cloned.1.call-start = ((), (), s32[]{:S(2)}) async-start(), calls=%async_computation.12 | async-start | bytes 1310720 | tf_op jit(solution)/shard_map/reduce_scatter | solution.py:555
  429.5 26.7 %collective-permute-start.65 = (bf16[128,2048]{1,0:T(8,128)(2,1)}, bf16[128,2048]{1,0:T(8,128)(2,1)}, u32[]{:S(2)}, u32[]{:S(2)}) collective-permute-start(bf16[128,2048]{1,0:T(8,128)(2,1)} %pad_maximum_fusion.12), channel_id=1, source_target_pairs={{0,2},{1,3},{2,0},{3,1},{4,6},{5,7},{6,4},{7,5},{8,10},{9,11},{10,... | collective-permute-start | bytes 1572872 | tf_op jit(solution)/shard_map/ppermute | solution.py:55
  431.4 25.4 %collective-permute-start.66 = (bf16[128,2048]{1,0:T(8,128)(2,1)S(1)}, bf16[128,2048]{1,0:T(8,128)(2,1)}, u32[]{:S(2)}, u32[]{:S(2)}) collective-permute-start(bf16[128,2048]{1,0:T(8,128)(2,1)S(1)} %pad_maximum_fusion.13), channel_id=1, source_target_pairs={{0,4},{1,5},{2,6},{3,7},{4,0},{5,1},{6,2},{7,3},{8,12},{9,13},{10,... | collective-permute-start | bytes 1572872 | tf_op jit(solution)/shard_map/ppermute | solution.py:55
  468.0 17.1 %all-to-all-start.1 = ((bf16[8,65,768]{2,1,0:T(8,128)(2,1)}), bf16[8,65,768]{2,1,0:T(8,128)(2,1)S(1)}, u32[]{:S(2)}, u32[]{:S(2)}) async-start(bf16[8,65,768]{2,1,0:T(8,128)(2,1)} %pad_maximum_fusion.1), calls=%async_computation.4 | async-start | bytes 1769472 | tf_op jit(solution)/shard_map/all_to_all | solution.py:671
  (66 other events, 493.4 us)
Sparse Core Ops, SparseCore 0:
  11.2 83.4 all-gather.3
  96.9 96.5 all-gather.5
  195.6 53.1 all-gather.7
  251.0 50.8 reduce-scatter.4
  304.1 93.4 reduce-scatter.6
  399.7 61.6 reduce-scatter.8
  463.8 27.2 reduce-scatter.10

commit v5 on v4

--- a/solution.py
+++ b/solution.py
@@ -182,7 +182,9 @@
     )(jnp.stack([start, shift, me]).astype(jnp.int32), *operands)
 
 
-def cut_heads_kernel(q_ref, k_ref, v_ref, rows_ref, out_ref, held, held_rows, sems, *, pieces, members):
+def cut_heads_kernel(
+    q_ref, k_ref, v_ref, rows_ref, out_ref, held, held_rows, made, sems, out_sems, *, pieces, members
+):
     me = lax.axis_index("ctx")
     tiles = members * DH // TILE
     weights = (q_ref, k_ref, v_ref)
@@ -203,6 +205,15 @@
     )
     for copy in copies:
         copy.start()
+    sent = []
+
+    def send(first, columns, values):
+        made[:, first : first + columns] = values
+        part = (slice(None), slice(first, first + columns))
+        copy = pltpu.make_async_copy(made.at[part], out_ref.at[part], out_sems.at[len(sent)])
+        copy.start()
+        sent.append(copy)
+
     row = lax.broadcasted_iota(jnp.int32, (TILE, TILE), 0)
     column = lax.broadcasted_iota(jnp.int32, (TILE, TILE), 1)
     same = row - lax.rem(me * DH, TILE) == lax.rem(column, DH)
@@ -214,13 +225,17 @@
             copies[at + 1].wait()
             both = jnp.dot(held[at], pick[0], preferred_element_type=f32)
             both = both + jnp.dot(held[at + 1], pick[1], preferred_element_type=f32)
-            target = (pair * 3 + source) * TILE
-            out_ref[:, target : target + TILE] = both.astype(bf16)
+            send((pair * 3 + source) * TILE, TILE, both.astype(bf16))
     copies[-1].wait()
-    along = out_ref.shape[1] - len(weights) * pieces * DH
-    for group in range(held_rows.shape[1] // along):
-        part = held_rows[:, group * along : (group + 1) * along]
-        out_ref[group * count : (group + 1) * count, out_ref.shape[1] - along :] = part
+    first = len(weights) * pieces * DH
+    along = made.shape[1] - first
+    parts = [
+        held_rows[:, group * along : (group + 1) * along]
+        for group in range(held_rows.shape[1] // along)
+    ]
+    send(first, along, jnp.concatenate(parts, axis=0))
+    for copy in sent:
+        copy.wait()
 
 
 def cut_heads_at_once(w_query, w_key, w_value, w_out, pieces, members):
@@ -231,11 +246,13 @@
         functools.partial(cut_heads_kernel, pieces=pieces, members=members),
         out_shape=jax.ShapeDtypeStruct((rows, columns), bf16),
         in_specs=[pl.BlockSpec(memory_space=pl.ANY)] * 4,
-        out_specs=pl.BlockSpec(memory_space=pltpu.VMEM),
+        out_specs=pl.BlockSpec(memory_space=pl.ANY),
         scratch_shapes=[
             pltpu.VMEM((3 * pieces, rows, TILE), bf16),
             pltpu.VMEM((count, width), bf16),
+            pltpu.VMEM((rows, columns), bf16),
             pltpu.SemaphoreType.DMA((3 * pieces + 1,)),
+            pltpu.SemaphoreType.DMA((3 * pieces // 2 + 1,)),
         ],
         compiler_params=pltpu.CompilerParams(vmem_limit_bytes=VMEM_BYTES),
         name="cut_heads",

time: 506 us -> 506 us (level)
  no operation moved by 1% of the time
where the time goes in v5:
time: 506 us; the launch traced here: 501 us
  waiting for transfers between devices  176 us (35%)
  Pallas kernels  80.5 us (16%)
  matrix products  74.4 us (15%)
  starting transfers between devices  59 us (12%)
  local copies, waits for them, and re-layouts  47.8 us (9%)
  other arithmetic  47.7 us (9%)
  between operations  15.3 us (3%)
    ppermute x64, waiting for transfers between devices, swap(): lax.ppermute(block, 'ctx', [(i, i ^ mask) for i in range(lax.axis_size('c...  106 us
    dot_general x12, matrix products, dot(): lax.dot_general(left, right, (contract, ((), ())), preferred_element_type...  73.7 us
    all_gather x3, waiting for transfers between devices, over_planes(): return lax.all_gather(weight, 'fsdp', axis=0, tiled=True)  56.3 us
    ppermute x64, starting transfers between devices, swap(): lax.ppermute(block, 'ctx', [(i, i ^ mask) for i in range(lax.axis_size('c...  44.4 us
    pallas_call x2, Pallas kernels, attend_back(): pl.pallas_call(functools.partial(backward_kernel, kept=len(aliases)), gri...  40.3 us
    unnamed x77, local copies, waits for them, and re-layouts  29.5 us
    pallas_call x1, Pallas kernels, attend(): pl.pallas_call(forward_kernel, grid=(pairs,), out_shape=(jax.ShapeDtypeSt...  22.5 us
  transfers between devices with their start and end apart: 76, of which 37 were waited for; matrix products, arithmetic and copies ran while one was open for 32% of the time, Pallas kernels for 15%

profile of v5, /device:TPU:0, one launch (start us, length us, event | category | flops | bytes accessed | tf_op | source)
XLA Modules:
  0.0 501.1 jit_solution(11085667665579951377)
XLA Ops:
  7.3 3.6 cut_heads.1
  20.4 5.1 %cut_hidden.1 = bf16[512,1280]{1,0:T(8,128)(2,1)} custom-call(s32[3]{0:T(128)} %pad_add_fusion.start_ref, bf16[512,5120]{1,0:T(8,128)(2,1)} %refs_7_.1, bf16[512,5120]{1,0:T(8,128)(2,1)} %refs_7_.1, bf16[512,5120]{1,0:T(8,128)(2,1)} %refs_7_.1, bf16[512,5120]{1,0:T(8,128)(2,1)} %refs_7_.1, bf16[512,5120]{1,0:T(8,128)(2,1)} %refs_7_.1, ...), custom_call_target="tpu_custom_call" | custom-call | tf_op jit(solution)/shard_map/cut_hidden/pallas_call | solution.py:170
  28.8 4.0 bias_tiles.1.tiles_ref
  60.5 5.7 %collective-permute-done.12 = bf16[128,2048]{1,0:T(8,128)(2,1)S(1)} collective-permute-done((bf16[128,2048]{1,0:T(8,128)(2,1)S(1)}, bf16[128,2048]{1,0:T(8,128)(2,1)S(1)}, u32[]{:S(2)}, u32[]{:S(2)}) %collective-permute-start.12) | collective-permute-done | bytes 524320 | tf_op jit(solution)/shard_map/ppermute | solution.py:55
  79.2 15.3 %all-gather.4.cloned.1.call-done = bf16[2048,1024]{1,0:T(8,128)(2,1)} async-done(((bf16[512,1024]{1,0:T(8,128)(2,1)}), bf16[2048,1024]{1,0:T(8,128)(2,1)}) %all-gather.4.cloned.1.call-update) | async-done | bytes 4194320 | tf_op jit(solution)/shard_map/all_gather | solution.py:569
  97.0 6.4 %fusion.15.q_ref.k_ref.v_ref = bf16[1024,768]{1,0:T(8,128)(2,1)} fusion(bf16[1024,2048]{1,0:T(8,128)(2,1)S(1)} %copy-done.6, bf16[2048,1024]{1,0:T(8,128)(2,1)} %all-gather.4.cloned.1.call-done), kind=kOutput, calls=%fused_computation.37 | convolution fusion | flops 3222011904 | bytes 8912896 | tf_op jit(solution)/shard_map/dot_general | solution.py:51
  104.4 22.5 %attend_forward.1 = (bf16[256,1024]{1,0:T(8,128)(2,1)}, f32[2,2,8,128]{3,2,1,0:T(8,128)}) custom-call(s32[1]{0:T(128)} %bitcast.base_ref, bf16[1024,768]{1,0:T(8,128)(2,1)} %fusion.15.q_ref.k_ref.v_ref, bf16[1024,768]{1,0:T(8,128)(2,1)} %fusion.15.q_ref.k_ref.v_ref, bf16[1024,768]{1,0:T(8,128)(2,1)} %fusion.15.q_ref.k_ref.v_ref, ...), custom_call_target="tpu_custom_call" | custom-call | tf_op jit(solution)/shard_map/attend_forward/pallas_call | solution.py:398
  136.6 5.3 %collective-permute-done.22 = bf16[64,2048]{1,0:T(8,128)(2,1)S(1)} collective-permute-done((bf16[64,2048]{1,0:T(8,128)(2,1)S(1)}, bf16[64,2048]{1,0:T(8,128)(2,1)S(1)}, u32[]{:S(2)}, u32[]{:S(2)}) %collective-permute-start.22) | collective-permute-done | bytes 262176 | tf_op jit(solution)/shard_map/ppermute | solution.py:55
  145.2 10.2 %collective-permute-done.23 = bf16[128,2048]{1,0:T(8,128)(2,1)S(1)} collective-permute-done((bf16[128,2048]{1,0:T(8,128)(2,1)S(1)}, bf16[128,2048]{1,0:T(8,128)(2,1)S(1)}, u32[]{:S(2)}, u32[]{:S(2)}) %collective-permute-start.23) | collective-permute-done | bytes 524320 | tf_op jit(solution)/shard_map/ppermute | solution.py:55
  163.7 9.0 %collective-permute-done.28 = bf16[128,2048]{1,0:T(8,128)(2,1)} collective-permute-done((bf16[128,2048]{1,0:T(8,128)(2,1)}, bf16[128,2048]{1,0:T(8,128)(2,1)}, u32[]{:S(2)}, u32[]{:S(2)}) %collective-permute-start.28) | collective-permute-done | bytes 524320 | tf_op jit(solution)/shard_map/ppermute | solution.py:55
  187.4 5.9 %all-gather.6.cloned.1.call-done = bf16[2048,1280]{1,0:T(8,128)(2,1)} async-done(((bf16[512,1280]{1,0:T(8,128)(2,1)}), bf16[2048,1280]{1,0:T(8,128)(2,1)}) %all-gather.6.cloned.1.call-update) | async-done | bytes 5242896 | tf_op jit(solution)/shard_map/all_gather | solution.py:569
  193.3 8.9 %fusion.46 = f32[1024,1280]{1,0:T(8,128)S(1)} fusion(bf16[1024,2048]{1,0:T(8,128)(2,1)} %constant_dynamic-update-slice_fusion.18, bf16[2048,1280]{1,0:T(8,128)(2,1)} %all-gather.6.cloned.1.call-done), kind=kOutput, calls=%fused_computation.188 | convolution fusion | flops 5368709120 | bytes 14680064 | tf_op jit(solution)/shard_map/dot_general | solution.py:51
  206.5 6.6 %convolution_convert_fusion.6 = bf16[640,2048]{1,0:T(8,128)(2,1)} fusion(bf16[1024,640]{1,0:T(8,128)(2,1)S(1)} %multiply_convert_fusion.1, bf16[1024,2048]{1,0:T(8,128)(2,1)} %constant_dynamic-update-slice_fusion.9), kind=kOutput, calls=%fused_computation.17 | convolution fusion | flops 2685665280 | bytes 8126464 | tf_op jit(solution)/shard_map/dot_general | solution.py:51
  213.7 35.0 %all-gather.8.cloned.1.call-done = bf16[640,2048]{1,0:T(8,128)(2,1)} async-done(((bf16[160,2048]{1,0:T(8,128)(2,1)}), bf16[640,2048]{1,0:T(8,128)(2,1)}) %all-gather.8.cloned.1.call-update) | async-done | bytes 2621456 | tf_op jit(solution)/shard_map/all_gather | solution.py:569
  248.7 9.4 %fusion.14 = (bf16[1024,640]{1,0:T(8,128)(2,1)S(1)}, bf16[1024,640]{1,0:T(8,128)(2,1)S(1)}) fusion(f32[1024,1280]{1,0:T(8,128)} %copy-done.5, bf16[1024,2048]{1,0:T(8,128)(2,1)} %constant_dynamic-update-slice_fusion.9, bf16[640,2048]{1,0:T(8,128)(2,1)} %all-gather.8.cloned.1.call-done), kind=kOutput, calls=%fused_computation.27 | convolution fusion | flops 2700083200 | bytes 14680064 | tf_op jit(solution)/shard_map/dot_general | solution.py:51
  258.2 8.4 %convolution_convert_fusion.2 = bf16[1024,2048]{1,0:T(8,128)(2,1)S(1)} fusion(bf16[2048,1280]{1,0:T(8,128)(2,1)} %all-gather.6.cloned.1.call-done, bf16[1024,640]{1,0:T(8,128)(2,1)S(1)} %get-tuple-element.95, bf16[1024,640]{1,0:T(8,128)(2,1)S(1)} %get-tuple-element.94), kind=kOutput, calls=%fused_computation.10 | convolution fusion | flops 5376049152 | bytes 12058624 | tf_op jit(solution)/shard_map/dot_general | solution.py:51
  271.6 7.6 %convolution_convert_fusion = bf16[2048,1280]{1,0:T(8,128)(2,1)} fusion(bf16[1024,2048]{1,0:T(8,128)(2,1)S(1)} %copy-done.15, bf16[1024,1280]{1,0:T(8,128)(2,1)S(1)} %pad_maximum_fusion), kind=kOutput, calls=%fused_computation.6 | convolution fusion | flops 5371330560 | bytes 12058624 | tf_op jit(solution)/shard_map/dot_general | solution.py:51
  285.2 4.9 collective-permute-done.38
  293.4 10.3 %collective-permute-done.39 = bf16[128,2048]{1,0:T(8,128)(2,1)S(1)} collective-permute-done((bf16[128,2048]{1,0:T(8,128)(2,1)S(1)}, bf16[128,2048]{1,0:T(8,128)(2,1)S(1)}, u32[]{:S(2)}, u32[]{:S(2)}) %collective-permute-start.39) | collective-permute-done | bytes 524320 | tf_op jit(solution)/shard_map/ppermute | solution.py:55
  312.5 5.6 %convolution_convert_fusion.1 = bf16[1024,2048]{1,0:T(8,128)(2,1)S(1)} fusion(bf16[1024,640]{1,0:T(8,128)(2,1)} %copy-done.10, bf16[640,2048]{1,0:T(8,128)(2,1)} %all-gather.8.cloned.1.call-done), kind=kOutput, calls=%fused_computation.9 | convolution fusion | flops 2686451712 | bytes 8126464 | tf_op jit(solution)/shard_map/dot_general | solution.py:51
  318.1 4.9 collective-permute-done.44
  326.3 3.6 collective-permute-done.48
  338.1 20.0 %attend_backward.2 = (bf16[1024,768]{1,0:T(8,128)(2,1)}, f32[2,32,8,128]{3,2,1,0:T(8,128)}) custom-call(s32[1]{0:T(128)} %bitcast.base_ref, bf16[1024,768]{1,0:T(8,128)(2,1)} %fusion.15.q_ref.k_ref.v_ref, bf16[1024,768]{1,0:T(8,128)(2,1)} %fusion.15.q_ref.k_ref.v_ref, bf16[1024,768]{1,0:T(8,128)(2,1)} %fusion.15.q_ref.k_ref.v_ref, ...), custom_call_target="tpu_custom_call" | custom-call | tf_op jit(solution)/shard_map/attend_backward/pallas_call | solution.py:515
  358.1 3.6 add_convert_fusion.2
  361.7 20.3 %attend_backward.3 = (bf16[1024,768]{1,0:T(8,128)(2,1)}, f32[2,32,8,128]{3,2,1,0:T(8,128)}) custom-call(s32[1]{0:T(128)} %bitcast.base_ref, bf16[1024,768]{1,0:T(8,128)(2,1)} %fusion.15.q_ref.k_ref.v_ref, bf16[1024,768]{1,0:T(8,128)(2,1)} %fusion.15.q_ref.k_ref.v_ref, bf16[1024,768]{1,0:T(8,128)(2,1)} %fusion.15.q_ref.k_ref.v_ref, ...), custom_call_target="tpu_custom_call", output_to_operand_aliasing={{0}: (9, {})} | custom-call | tf_op jit(solution)/shard_map/attend_backward/pallas_call | solution.py:515
  383.4 6.2 %convolution_convert_fusion.5 = bf16[2048,768]{1,0:T(8,128)(2,1)S(1)} fusion(bf16[1024,2048]{1,0:T(8,128)(2,1)} %fusion.2, bf16[1024,768]{1,0:T(8,128)(2,1)} %get-tuple-element.65), kind=kOutput, calls=%fused_computation.15 | convolution fusion | flops 3222798336 | bytes 8912896 | tf_op jit(solution)/shard_map/dot_general | solution.py:51
  394.4 5.8 %convolution_convert_fusion.4 = bf16[1024,2048]{1,0:T(8,128)(2,1)S(1)} fusion(bf16[1024,768]{1,0:T(8,128)(2,1)} %get-tuple-element.65, bf16[2048,1024]{1,0:T(8,128)(2,1)} %all-gather.4.cloned.1.call-done), kind=kOutput, calls=%fused_computation.12 | convolution fusion | flops 3223322624 | bytes 8912896 | tf_op jit(solution)/shard_map/dot_general | solution.py:51
  409.7 5.0 collective-permute-done.60
  420.6 4.3 all-to-all-start
  424.9 4.4 convolution_convert_fusion.7
  435.8 20.3 %collective-permute-done.65 = bf16[128,2048]{1,0:T(8,128)(2,1)} collective-permute-done((bf16[128,2048]{1,0:T(8,128)(2,1)}, bf16[128,2048]{1,0:T(8,128)(2,1)}, u32[]{:S(2)}, u32[]{:S(2)}) %collective-permute-start.65) | collective-permute-done | bytes 524320 | tf_op jit(solution)/shard_map/ppermute | solution.py:55
  475.0 9.9 %all-to-all-done.1 = bf16[8,65,768]{2,1,0:T(8,128)(2,1)S(1)} async-done(((bf16[8,65,768]{2,1,0:T(8,128)(2,1)}), bf16[8,65,768]{2,1,0:T(8,128)(2,1)S(1)}, u32[]{:S(2)}, u32[]{:S(2)}) %all-to-all-start.1) | async-done | bytes 798752 | tf_op jit(solution)/shard_map/all_to_all | solution.py:688
  (334 shorter events, 188.0 us)
Async XLA Ops:
  7.2 87.3 %all-gather.4.cloned.1.call-start = ((), (), s32[]{:S(2)}) async-start(), calls=%async_computation.6 | async-start | bytes 5242880 | tf_op jit(solution)/shard_map/all_gather | solution.py:569
  10.9 182.4 %all-gather.6.cloned.1.call-start = ((), (), s32[]{:S(2)}) async-start(), calls=%async_computation.7 | async-start | bytes 6553600 | tf_op jit(solution)/shard_map/all_gather | solution.py:569
  10.9 29.3 %collective-permute-start = (bf16[128,2048]{1,0:T(8,128)(2,1)S(1)}, bf16[128,2048]{1,0:T(8,128)(2,1)S(1)}, u32[]{:S(2)}, u32[]{:S(2)}) collective-permute-start(bf16[128,2048]{1,0:T(8,128)(2,1)S(1)} %copy-done.3), channel_id=1, source_target_pairs={{0,1},{1,0},{2,3},{3,2},{4,5},{5,4},{6,7},{7,6},{8,9},{9,8},{10,11... | collective-permute-start | bytes 1572872 | tf_op jit(solution)/shard_map/ppermute | solution.py:55
  11.5 26.5 %collective-permute-start.1 = (bf16[128,2048]{1,0:T(8,128)(2,1)S(1)}, bf16[128,2048]{1,0:T(8,128)(2,1)S(1)}, u32[]{:S(2)}, u32[]{:S(2)}) collective-permute-start(bf16[128,2048]{1,0:T(8,128)(2,1)S(1)} %copy-done.3), channel_id=1, source_target_pairs={{0,2},{1,3},{2,0},{3,1},{4,6},{5,7},{6,4},{7,5},{8,10},{9,11},{10,... | collective-permute-start | bytes 1572872 | tf_op jit(solution)/shard_map/ppermute | solution.py:55
  14.0 25.5 %collective-permute-start.3 = (bf16[128,2048]{1,0:T(8,128)(2,1)S(1)}, bf16[128,2048]{1,0:T(8,128)(2,1)S(1)}, u32[]{:S(2)}, u32[]{:S(2)}) collective-permute-start(bf16[128,2048]{1,0:T(8,128)(2,1)S(1)} %copy-done.3), channel_id=1, source_target_pairs={{0,4},{1,5},{2,6},{3,7},{4,0},{5,1},{6,2},{7,3},{8,12},{9,13},{10,... | collective-permute-start | bytes 1572872 | tf_op jit(solution)/shard_map/ppermute | solution.py:55
  15.6 17.3 %collective-permute-start.8 = (bf16[2,512]{1,0:T(2,128)(2,1)S(1)}, bf16[2,512]{1,0:T(2,128)(2,1)S(1)}, u32[]{:S(2)}, u32[]{:S(2)}) collective-permute-start(bf16[2,512]{1,0:T(2,128)(2,1)S(1)} %pad_maximum_fusion.14), channel_id=1, source_target_pairs={{0,8},{8,16},{16,24},{24,0},{1,9},{9,17},{17,25},{25,1},{2,10},{10... | collective-permute-start | bytes 6152 | tf_op jit(solution)/shard_map/ppermute | solution.py:117
  17.2 17.1 %collective-permute-start.9 = (bf16[2,512]{1,0:T(2,128)(2,1)S(1)}, bf16[2,512]{1,0:T(2,128)(2,1)S(1)}, u32[]{:S(2)}, u32[]{:S(2)}) collective-permute-start(bf16[2,512]{1,0:T(2,128)(2,1)S(1)} %pad_maximum_fusion.14), channel_id=1, source_target_pairs={{0,16},{8,24},{16,0},{24,8},{1,17},{9,25},{17,1},{25,9},{2,18},{10... | collective-permute-start | bytes 6152 | tf_op jit(solution)/shard_map/ppermute | solution.py:117
  25.5 223.1 %all-gather.8.cloned.1.call-start = ((), (), s32[]{:S(2)}) async-start(), calls=%async_computation.8 | async-start | bytes 3276800 | tf_op jit(solution)/shard_map/all_gather | solution.py:569
  51.9 17.1 %collective-permute-start.11 = (bf16[128,2048]{1,0:T(8,128)(2,1)S(1)}, bf16[128,2048]{1,0:T(8,128)(2,1)S(1)}, u32[]{:S(2)}, u32[]{:S(2)}) collective-permute-start(bf16[128,2048]{1,0:T(8,128)(2,1)S(1)} %copy-done.8), channel_id=1, source_target_pairs={{0,1},{1,0},{2,3},{3,2},{4,5},{5,4},{6,7},{7,6},{8,9},{9,8},{10,11... | collective-permute-start | bytes 1572872 | tf_op jit(solution)/shard_map/ppermute | solution.py:55
  52.4 13.8 %collective-permute-start.12 = (bf16[128,2048]{1,0:T(8,128)(2,1)S(1)}, bf16[128,2048]{1,0:T(8,128)(2,1)S(1)}, u32[]{:S(2)}, u32[]{:S(2)}) collective-permute-start(bf16[128,2048]{1,0:T(8,128)(2,1)S(1)} %copy-done.8), channel_id=1, source_target_pairs={{0,2},{1,3},{2,0},{3,1},{4,6},{5,7},{6,4},{7,5},{8,10},{9,11},{10,... | collective-permute-start | bytes 1572872 | tf_op jit(solution)/shard_map/ppermute | solution.py:55
  52.5 14.4 %collective-permute-start.14 = (bf16[128,2048]{1,0:T(8,128)(2,1)S(1)}, bf16[128,2048]{1,0:T(8,128)(2,1)S(1)}, u32[]{:S(2)}, u32[]{:S(2)}) collective-permute-start(bf16[128,2048]{1,0:T(8,128)(2,1)S(1)} %copy-done.8), channel_id=1, source_target_pairs={{0,4},{1,5},{2,6},{3,7},{4,0},{5,1},{6,2},{7,3},{8,12},{9,13},{10,... | collective-permute-start | bytes 1572872 | tf_op jit(solution)/shard_map/ppermute | solution.py:55
  142.1 13.3 %collective-permute-start.23 = (bf16[128,2048]{1,0:T(8,128)(2,1)S(1)}, bf16[128,2048]{1,0:T(8,128)(2,1)S(1)}, u32[]{:S(2)}, u32[]{:S(2)}) collective-permute-start(bf16[128,2048]{1,0:T(8,128)(2,1)S(1)} %pad_maximum_fusion.4), channel_id=1, source_target_pairs={{0,2},{1,3},{2,0},{3,1},{4,6},{5,7},{6,4},{7,5},{8,10},{9,11},{10,... | collective-permute-start | bytes 1572872 | tf_op jit(solution)/shard_map/ppermute | solution.py:55
  144.0 13.7 %collective-permute-start.26 = (bf16[128,2048]{1,0:T(8,128)(2,1)S(1)}, bf16[128,2048]{1,0:T(8,128)(2,1)S(1)}, u32[]{:S(2)}, u32[]{:S(2)}) collective-permute-start(bf16[128,2048]{1,0:T(8,128)(2,1)S(1)} %pad_maximum_fusion.5), channel_id=1, source_target_pairs={{0,4},{1,5},{2,6},{3,7},{4,0},{5,1},{6,2},{7,3},{8,12},{9,13},{10,... | collective-permute-start | bytes 1572872 | tf_op jit(solution)/shard_map/ppermute | solution.py:55
  159.5 13.2 %collective-permute-start.28 = (bf16[128,2048]{1,0:T(8,128)(2,1)}, bf16[128,2048]{1,0:T(8,128)(2,1)}, u32[]{:S(2)}, u32[]{:S(2)}) collective-permute-start(bf16[128,2048]{1,0:T(8,128)(2,1)} %get-tuple-element.91), channel_id=1, source_target_pairs={{0,2},{1,3},{2,0},{3,1},{4,6},{5,7},{6,4},{7,5},{8,10},{9,11},{10,... | collective-permute-start | bytes 1572872 | tf_op jit(solution)/shard_map/ppermute | solution.py:55
  161.4 15.8 %collective-permute-start.27 = (bf16[128,2048]{1,0:T(8,128)(2,1)}, bf16[128,2048]{1,0:T(8,128)(2,1)}, u32[]{:S(2)}, u32[]{:S(2)}) collective-permute-start(bf16[128,2048]{1,0:T(8,128)(2,1)} %get-tuple-element.91), channel_id=1, source_target_pairs={{0,1},{1,0},{2,3},{3,2},{4,5},{5,4},{6,7},{7,6},{8,9},{9,8},{10,11... | collective-permute-start | bytes 1572872 | tf_op jit(solution)/shard_map/ppermute | solution.py:55
  163.4 147.1 %reduce-scatter.5.cloned.1.call-start = ((), (), s32[]{:S(2)}) async-start(), calls=%async_computation.9 | async-start | bytes 3276800 | tf_op jit(solution)/shard_map/reduce_scatter | solution.py:572
  213.2 204.4 %reduce-scatter.7.cloned.1.call-start = ((), (), s32[]{:S(2)}) async-start(), calls=%async_computation.10 | async-start | bytes 6553600 | tf_op jit(solution)/shard_map/reduce_scatter | solution.py:572
  279.3 185.5 %reduce-scatter.9.cloned.1.call-start = ((), (), s32[]{:S(2)}) async-start(), calls=%async_computation.11 | async-start | bytes 3993600 | tf_op jit(solution)/shard_map/reduce_scatter | solution.py:572
  290.2 13.4 %collective-permute-start.39 = (bf16[128,2048]{1,0:T(8,128)(2,1)S(1)}, bf16[128,2048]{1,0:T(8,128)(2,1)S(1)}, u32[]{:S(2)}, u32[]{:S(2)}) collective-permute-start(bf16[128,2048]{1,0:T(8,128)(2,1)S(1)} %pad_maximum_fusion.7), channel_id=1, source_target_pairs={{0,2},{1,3},{2,0},{3,1},{4,6},{5,7},{6,4},{7,5},{8,10},{9,11},{10,... | collective-permute-start | bytes 1572872 | tf_op jit(solution)/shard_map/ppermute | solution.py:55
  292.9 13.3 %collective-permute-start.42 = (bf16[128,2048]{1,0:T(8,128)(2,1)S(1)}, bf16[128,2048]{1,0:T(8,128)(2,1)S(1)}, u32[]{:S(2)}, u32[]{:S(2)}) collective-permute-start(bf16[128,2048]{1,0:T(8,128)(2,1)S(1)} %pad_maximum_fusion.8), channel_id=1, source_target_pairs={{0,4},{1,5},{2,6},{3,7},{4,0},{5,1},{6,2},{7,3},{8,12},{9,13},{10,... | collective-permute-start | bytes 1572872 | tf_op jit(solution)/shard_map/ppermute | solution.py:55
  312.5 13.7 %collective-permute-start.43 = (bf16[128,2048]{1,0:T(8,128)(2,1)}, bf16[128,2048]{1,0:T(8,128)(2,1)S(1)}, u32[]{:S(2)}, u32[]{:S(2)}) collective-permute-start(bf16[128,2048]{1,0:T(8,128)(2,1)} %get-tuple-element.57), channel_id=1, source_target_pairs={{0,1},{1,0},{2,3},{3,2},{4,5},{5,4},{6,7},{7,6},{8,9},{9,8},{10,11... | collective-permute-start | bytes 1572872 | tf_op jit(solution)/shard_map/ppermute | solution.py:55
  335.0 23.1 %collective-permute-start.51 = (bf16[128,2048]{1,0:T(8,128)(2,1)}, bf16[128,2048]{1,0:T(8,128)(2,1)}, u32[]{:S(2)}, u32[]{:S(2)}) collective-permute-start(bf16[128,2048]{1,0:T(8,128)(2,1)} %get-tuple-element.111), channel_id=1, source_target_pairs={{0,1},{1,0},{2,3},{3,2},{4,5},{5,4},{6,7},{7,6},{8,9},{9,8},{10,11... | collective-permute-start | bytes 1572872 | tf_op jit(solution)/shard_map/ppermute | solution.py:55
  335.1 23.0 %collective-permute-start.52 = (bf16[128,2048]{1,0:T(8,128)(2,1)}, bf16[128,2048]{1,0:T(8,128)(2,1)}, u32[]{:S(2)}, u32[]{:S(2)}) collective-permute-start(bf16[128,2048]{1,0:T(8,128)(2,1)} %get-tuple-element.110), channel_id=1, source_target_pairs={{0,1},{1,0},{2,3},{3,2},{4,5},{5,4},{6,7},{7,6},{8,9},{9,8},{10,11... | collective-permute-start | bytes 1572872 | tf_op jit(solution)/shard_map/ppermute | solution.py:55
  335.5 22.6 %collective-permute-start.53 = (bf16[128,2048]{1,0:T(8,128)(2,1)S(1)}, bf16[128,2048]{1,0:T(8,128)(2,1)}, u32[]{:S(2)}, u32[]{:S(2)}) collective-permute-start(bf16[128,2048]{1,0:T(8,128)(2,1)S(1)} %get-tuple-element.109), channel_id=1, source_target_pairs={{0,1},{1,0},{2,3},{3,2},{4,5},{5,4},{6,7},{7,6},{8,9},{9,8},{10,11... | collective-permute-start | bytes 1572872 | tf_op jit(solution)/shard_map/ppermute | solution.py:55
  335.6 22.5 %collective-permute-start.54 = (bf16[128,2048]{1,0:T(8,128)(2,1)S(1)}, bf16[128,2048]{1,0:T(8,128)(2,1)}, u32[]{:S(2)}, u32[]{:S(2)}) collective-permute-start(bf16[128,2048]{1,0:T(8,128)(2,1)S(1)} %get-tuple-element.108), channel_id=1, source_target_pairs={{0,1},{1,0},{2,3},{3,2},{4,5},{5,4},{6,7},{7,6},{8,9},{9,8},{10,11... | collective-permute-start | bytes 1572872 | tf_op jit(solution)/shard_map/ppermute | solution.py:55
  417.6 15.2 %collective-permute-start.63 = (bf16[128,2048]{1,0:T(8,128)(2,1)}, bf16[128,2048]{1,0:T(8,128)(2,1)}, u32[]{:S(2)}, u32[]{:S(2)}) collective-permute-start(bf16[128,2048]{1,0:T(8,128)(2,1)} %pad_maximum_fusion.10), channel_id=1, source_target_pairs={{0,2},{1,3},{2,0},{3,1},{4,6},{5,7},{6,4},{7,5},{8,10},{9,11},{10,... | collective-permute-start | bytes 1572872 | tf_op jit(solution)/shard_map/ppermute | solution.py:55
  418.3 15.8 %collective-permute-start.64 = (bf16[128,2048]{1,0:T(8,128)(2,1)}, bf16[128,2048]{1,0:T(8,128)(2,1)}, u32[]{:S(2)}, u32[]{:S(2)}) collective-permute-start(bf16[128,2048]{1,0:T(8,128)(2,1)} %pad_maximum_fusion.11), channel_id=1, source_target_pairs={{0,4},{1,5},{2,6},{3,7},{4,0},{5,1},{6,2},{7,3},{8,12},{9,13},{10,... | collective-permute-start | bytes 1572872 | tf_op jit(solution)/shard_map/ppermute | solution.py:55
  420.6 38.7 %all-to-all-start = ((bf16[8,64,1280]{2,1,0:T(8,128)(2,1)}), bf16[8,64,1280]{2,1,0:T(8,128)(2,1)}, u32[]{:S(2)}, u32[]{:S(2)}) async-start(bf16[8,64,1280]{2,1,0:T(8,128)(2,1)} %bitcast.71), calls=%async_computation.2 | async-start | bytes 2621440 | tf_op jit(solution)/shard_map/all_to_all | solution.py:576
  424.8 66.8 %reduce-scatter.11.cloned.1.call-start = ((), (), s32[]{:S(2)}) async-start(), calls=%async_computation.12 | async-start | bytes 1310720 | tf_op jit(solution)/shard_map/reduce_scatter | solution.py:572
  429.3 26.7 %collective-permute-start.65 = (bf16[128,2048]{1,0:T(8,128)(2,1)}, bf16[128,2048]{1,0:T(8,128)(2,1)}, u32[]{:S(2)}, u32[]{:S(2)}) collective-permute-start(bf16[128,2048]{1,0:T(8,128)(2,1)} %pad_maximum_fusion.12), channel_id=1, source_target_pairs={{0,2},{1,3},{2,0},{3,1},{4,6},{5,7},{6,4},{7,5},{8,10},{9,11},{10,... | collective-permute-start | bytes 1572872 | tf_op jit(solution)/shard_map/ppermute | solution.py:55
  431.2 25.4 %collective-permute-start.66 = (bf16[128,2048]{1,0:T(8,128)(2,1)S(1)}, bf16[128,2048]{1,0:T(8,128)(2,1)}, u32[]{:S(2)}, u32[]{:S(2)}) collective-permute-start(bf16[128,2048]{1,0:T(8,128)(2,1)S(1)} %pad_maximum_fusion.13), channel_id=1, source_target_pairs={{0,4},{1,5},{2,6},{3,7},{4,0},{5,1},{6,2},{7,3},{8,12},{9,13},{10,... | collective-permute-start | bytes 1572872 | tf_op jit(solution)/shard_map/ppermute | solution.py:55
  467.8 17.1 %all-to-all-start.1 = ((bf16[8,65,768]{2,1,0:T(8,128)(2,1)}), bf16[8,65,768]{2,1,0:T(8,128)(2,1)S(1)}, u32[]{:S(2)}, u32[]{:S(2)}) async-start(bf16[8,65,768]{2,1,0:T(8,128)(2,1)} %pad_maximum_fusion.1), calls=%async_computation.4 | async-start | bytes 1769472 | tf_op jit(solution)/shard_map/all_to_all | solution.py:688
  (66 other events, 492.6 us)
Sparse Core Ops, SparseCore 0:
  11.0 83.4 all-gather.3
  96.7 96.5 all-gather.5
  195.4 53.1 all-gather.7
  250.8 50.8 reduce-scatter.4
  303.9 93.4 reduce-scatter.6
  399.5 61.6 reduce-scatter.8
  463.6 27.2 reduce-scatter.10

commit v6 on v4

--- a/solution.py
+++ b/solution.py
@@ -679,9 +679,8 @@
     input_grad = (residual_grad + first_back(normed_grad)[0]).astype(bf16)
 
     def gain_grad(gain, pairs):
-        return sum(jnp.sum(own_rows(w).astype(f32) * g, axis=1) for w, g in pairs) / own_rows(
-            gain
-        ).astype(f32)
+        products = sum(own_rows(w).astype(f32) * g for w, g in pairs)
+        return jnp.sum(products, axis=1) / own_rows(gain).astype(f32)
 
     down_shard = down_sum.astype(f32)
     ff_gain_shard = gain_grad(gain_ff, ((w_gate, gate_shard), (w_up, up_shard)))

time: 506 us -> 505 us (level)
  transfers between devices with their start and end apart: 76 -> 76, of which waited for: 37 -> 38; matrix products, arithmetic and copies ran while one was open for 32% -> 32% of each run, Pallas kernels for 15% -> 15%
where the time goes in v6:
time: 505 us; the launch traced here: 501 us
  waiting for transfers between devices  176 us (35%)
  Pallas kernels  80.7 us (16%)
  matrix products  74.4 us (15%)
  starting transfers between devices  59.1 us (12%)
  local copies, waits for them, and re-layouts  47.9 us (9%)
  other arithmetic  46.8 us (9%)
  between operations  15.3 us (3%)
    ppermute x64, waiting for transfers between devices, swap(): lax.ppermute(block, 'ctx', [(i, i ^ mask) for i in range(lax.axis_size('c...  106 us
    dot_general x12, matrix products, dot(): lax.dot_general(left, right, (contract, ((), ())), preferred_element_type...  73.7 us
    all_gather x3, waiting for transfers between devices, over_planes(): return lax.all_gather(weight, 'fsdp', axis=0, tiled=True)  56.3 us
    ppermute x64, starting transfers between devices, swap(): lax.ppermute(block, 'ctx', [(i, i ^ mask) for i in range(lax.axis_size('c...  44.5 us
    pallas_call x2, Pallas kernels, attend_back(): pl.pallas_call(functools.partial(backward_kernel, kept=len(aliases)), gri...  40.2 us
    unnamed x77, local copies, waits for them, and re-layouts  29.5 us
    pallas_call x1, Pallas kernels, attend(): pl.pallas_call(forward_kernel, grid=(pairs,), out_shape=(jax.ShapeDtypeSt...  22.5 us
  transfers between devices with their start and end apart: 76, of which 38 were waited for; matrix products, arithmetic and copies ran while one was open for 32% of the time, Pallas kernels for 15%

profile of v6, /device:TPU:0, one launch (start us, length us, event | category | flops | bytes accessed | tf_op | source)
XLA Modules:
  0.0 500.6 jit_solution(12051491184610809832)
XLA Ops:
  7.3 3.8 cut_heads.1
  20.6 5.1 %cut_hidden.1 = bf16[512,1280]{1,0:T(8,128)(2,1)} custom-call(s32[3]{0:T(128)} %pad_add_fusion.start_ref, bf16[512,5120]{1,0:T(8,128)(2,1)} %refs_7_.1, bf16[512,5120]{1,0:T(8,128)(2,1)} %refs_7_.1, bf16[512,5120]{1,0:T(8,128)(2,1)} %refs_7_.1, bf16[512,5120]{1,0:T(8,128)(2,1)} %refs_7_.1, bf16[512,5120]{1,0:T(8,128)(2,1)} %refs_7_.1, ...), custom_call_target="tpu_custom_call" | custom-call | tf_op jit(solution)/shard_map/cut_hidden/pallas_call | solution.py:170
  29.0 4.0 bias_tiles.1.tiles_ref
  60.7 5.7 %collective-permute-done.12 = bf16[128,2048]{1,0:T(8,128)(2,1)S(1)} collective-permute-done((bf16[128,2048]{1,0:T(8,128)(2,1)S(1)}, bf16[128,2048]{1,0:T(8,128)(2,1)S(1)}, u32[]{:S(2)}, u32[]{:S(2)}) %collective-permute-start.12) | collective-permute-done | bytes 524320 | tf_op jit(solution)/shard_map/ppermute | solution.py:55
  79.4 15.4 %all-gather.4.cloned.1.call-done = bf16[2048,1024]{1,0:T(8,128)(2,1)} async-done(((bf16[512,1024]{1,0:T(8,128)(2,1)}), bf16[2048,1024]{1,0:T(8,128)(2,1)}) %all-gather.4.cloned.1.call-update) | async-done | bytes 4194320 | tf_op jit(solution)/shard_map/all_gather | solution.py:552
  97.2 6.4 %fusion.15.q_ref.k_ref.v_ref = bf16[1024,768]{1,0:T(8,128)(2,1)} fusion(bf16[1024,2048]{1,0:T(8,128)(2,1)S(1)} %copy-done.6, bf16[2048,1024]{1,0:T(8,128)(2,1)} %all-gather.4.cloned.1.call-done), kind=kOutput, calls=%fused_computation.37 | convolution fusion | flops 3222011904 | bytes 8912896 | tf_op jit(solution)/shard_map/dot_general | solution.py:51
  104.7 22.5 %attend_forward.1 = (bf16[256,1024]{1,0:T(8,128)(2,1)}, f32[2,2,8,128]{3,2,1,0:T(8,128)}) custom-call(s32[1]{0:T(128)} %bitcast.base_ref, bf16[1024,768]{1,0:T(8,128)(2,1)} %fusion.15.q_ref.k_ref.v_ref, bf16[1024,768]{1,0:T(8,128)(2,1)} %fusion.15.q_ref.k_ref.v_ref, bf16[1024,768]{1,0:T(8,128)(2,1)} %fusion.15.q_ref.k_ref.v_ref, ...), custom_call_target="tpu_custom_call" | custom-call | tf_op jit(solution)/shard_map/attend_forward/pallas_call | solution.py:381
  136.8 5.3 %collective-permute-done.22 = bf16[64,2048]{1,0:T(8,128)(2,1)S(1)} collective-permute-done((bf16[64,2048]{1,0:T(8,128)(2,1)S(1)}, bf16[64,2048]{1,0:T(8,128)(2,1)S(1)}, u32[]{:S(2)}, u32[]{:S(2)}) %collective-permute-start.22) | collective-permute-done | bytes 262176 | tf_op jit(solution)/shard_map/ppermute | solution.py:55
  145.4 10.2 %collective-permute-done.23 = bf16[128,2048]{1,0:T(8,128)(2,1)S(1)} collective-permute-done((bf16[128,2048]{1,0:T(8,128)(2,1)S(1)}, bf16[128,2048]{1,0:T(8,128)(2,1)S(1)}, u32[]{:S(2)}, u32[]{:S(2)}) %collective-permute-start.23) | collective-permute-done | bytes 524320 | tf_op jit(solution)/shard_map/ppermute | solution.py:55
  163.9 8.9 %collective-permute-done.28 = bf16[128,2048]{1,0:T(8,128)(2,1)} collective-permute-done((bf16[128,2048]{1,0:T(8,128)(2,1)}, bf16[128,2048]{1,0:T(8,128)(2,1)}, u32[]{:S(2)}, u32[]{:S(2)}) %collective-permute-start.28) | collective-permute-done | bytes 524320 | tf_op jit(solution)/shard_map/ppermute | solution.py:55
  187.6 5.9 %all-gather.6.cloned.1.call-done = bf16[2048,1280]{1,0:T(8,128)(2,1)} async-done(((bf16[512,1280]{1,0:T(8,128)(2,1)}), bf16[2048,1280]{1,0:T(8,128)(2,1)}) %all-gather.6.cloned.1.call-update) | async-done | bytes 5242896 | tf_op jit(solution)/shard_map/all_gather | solution.py:552
  193.5 8.9 %fusion.46 = f32[1024,1280]{1,0:T(8,128)S(1)} fusion(bf16[1024,2048]{1,0:T(8,128)(2,1)} %constant_dynamic-update-slice_fusion.18, bf16[2048,1280]{1,0:T(8,128)(2,1)} %all-gather.6.cloned.1.call-done), kind=kOutput, calls=%fused_computation.185 | convolution fusion | flops 5368709120 | bytes 14680064 | tf_op jit(solution)/shard_map/dot_general | solution.py:51
  206.7 6.6 %convolution_convert_fusion.6 = bf16[640,2048]{1,0:T(8,128)(2,1)} fusion(bf16[1024,640]{1,0:T(8,128)(2,1)S(1)} %multiply_convert_fusion.1, bf16[1024,2048]{1,0:T(8,128)(2,1)} %constant_dynamic-update-slice_fusion.9), kind=kOutput, calls=%fused_computation.17 | convolution fusion | flops 2685665280 | bytes 8126464 | tf_op jit(solution)/shard_map/dot_general | solution.py:51
  213.8 35.0 %all-gather.8.cloned.1.call-done = bf16[640,2048]{1,0:T(8,128)(2,1)} async-done(((bf16[160,2048]{1,0:T(8,128)(2,1)}), bf16[640,2048]{1,0:T(8,128)(2,1)}) %all-gather.8.cloned.1.call-update) | async-done | bytes 2621456 | tf_op jit(solution)/shard_map/all_gather | solution.py:552
  248.9 9.4 %fusion.14 = (bf16[1024,640]{1,0:T(8,128)(2,1)S(1)}, bf16[1024,640]{1,0:T(8,128)(2,1)S(1)}) fusion(f32[1024,1280]{1,0:T(8,128)} %copy-done.5, bf16[1024,2048]{1,0:T(8,128)(2,1)} %constant_dynamic-update-slice_fusion.9, bf16[640,2048]{1,0:T(8,128)(2,1)} %all-gather.8.cloned.1.call-done), kind=kOutput, calls=%fused_computation.27 | convolution fusion | flops 2700083200 | bytes 14680064 | tf_op jit(solution)/shard_map/dot_general | solution.py:51
  258.4 8.4 %convolution_convert_fusion.2 = bf16[1024,2048]{1,0:T(8,128)(2,1)S(1)} fusion(bf16[2048,1280]{1,0:T(8,128)(2,1)} %all-gather.6.cloned.1.call-done, bf16[1024,640]{1,0:T(8,128)(2,1)S(1)} %get-tuple-element.95, bf16[1024,640]{1,0:T(8,128)(2,1)S(1)} %get-tuple-element.94), kind=kOutput, calls=%fused_computation.10 | convolution fusion | flops 5376049152 | bytes 12058624 | tf_op jit(solution)/shard_map/dot_general | solution.py:51
  271.8 7.6 %convolution_convert_fusion = bf16[2048,1280]{1,0:T(8,128)(2,1)} fusion(bf16[1024,2048]{1,0:T(8,128)(2,1)S(1)} %copy-done.15, bf16[1024,1280]{1,0:T(8,128)(2,1)S(1)} %pad_maximum_fusion), kind=kOutput, calls=%fused_computation.6 | convolution fusion | flops 5371330560 | bytes 12058624 | tf_op jit(solution)/shard_map/dot_general | solution.py:51
  285.4 4.9 collective-permute-done.38
  293.6 10.3 %collective-permute-done.39 = bf16[128,2048]{1,0:T(8,128)(2,1)S(1)} collective-permute-done((bf16[128,2048]{1,0:T(8,128)(2,1)S(1)}, bf16[128,2048]{1,0:T(8,128)(2,1)S(1)}, u32[]{:S(2)}, u32[]{:S(2)}) %collective-permute-start.39) | collective-permute-done | bytes 524320 | tf_op jit(solution)/shard_map/ppermute | solution.py:55
  312.7 5.6 %convolution_convert_fusion.1 = bf16[1024,2048]{1,0:T(8,128)(2,1)S(1)} fusion(bf16[1024,640]{1,0:T(8,128)(2,1)} %copy-done.10, bf16[640,2048]{1,0:T(8,128)(2,1)} %all-gather.8.cloned.1.call-done), kind=kOutput, calls=%fused_computation.9 | convolution fusion | flops 2686451712 | bytes 8126464 | tf_op jit(solution)/shard_map/dot_general | solution.py:51
  318.3 4.9 collective-permute-done.44
  326.5 3.6 collective-permute-done.48
  338.3 20.0 %attend_backward.2 = (bf16[1024,768]{1,0:T(8,128)(2,1)}, f32[2,32,8,128]{3,2,1,0:T(8,128)}) custom-call(s32[1]{0:T(128)} %bitcast.base_ref, bf16[1024,768]{1,0:T(8,128)(2,1)} %fusion.15.q_ref.k_ref.v_ref, bf16[1024,768]{1,0:T(8,128)(2,1)} %fusion.15.q_ref.k_ref.v_ref, bf16[1024,768]{1,0:T(8,128)(2,1)} %fusion.15.q_ref.k_ref.v_ref, ...), custom_call_target="tpu_custom_call" | custom-call | tf_op jit(solution)/shard_map/attend_backward/pallas_call | solution.py:498
  358.3 3.6 add_convert_fusion.2
  361.9 20.3 %attend_backward.3 = (bf16[1024,768]{1,0:T(8,128)(2,1)}, f32[2,32,8,128]{3,2,1,0:T(8,128)}) custom-call(s32[1]{0:T(128)} %bitcast.base_ref, bf16[1024,768]{1,0:T(8,128)(2,1)} %fusion.15.q_ref.k_ref.v_ref, bf16[1024,768]{1,0:T(8,128)(2,1)} %fusion.15.q_ref.k_ref.v_ref, bf16[1024,768]{1,0:T(8,128)(2,1)} %fusion.15.q_ref.k_ref.v_ref, ...), custom_call_target="tpu_custom_call", output_to_operand_aliasing={{0}: (9, {})} | custom-call | tf_op jit(solution)/shard_map/attend_backward/pallas_call | solution.py:498
  383.5 6.2 %convolution_convert_fusion.5 = bf16[2048,768]{1,0:T(8,128)(2,1)S(1)} fusion(bf16[1024,2048]{1,0:T(8,128)(2,1)} %fusion.2, bf16[1024,768]{1,0:T(8,128)(2,1)} %get-tuple-element.65), kind=kOutput, calls=%fused_computation.15 | convolution fusion | flops 3222798336 | bytes 8912896 | tf_op jit(solution)/shard_map/dot_general | solution.py:51
  394.6 5.8 %convolution_convert_fusion.4 = bf16[1024,2048]{1,0:T(8,128)(2,1)S(1)} fusion(bf16[1024,768]{1,0:T(8,128)(2,1)} %get-tuple-element.65, bf16[2048,1024]{1,0:T(8,128)(2,1)} %all-gather.4.cloned.1.call-done), kind=kOutput, calls=%fused_computation.12 | convolution fusion | flops 3223322624 | bytes 8912896 | tf_op jit(solution)/shard_map/dot_general | solution.py:51
  409.9 5.0 %collective-permute-done.60 = bf16[64,2048]{1,0:T(8,128)(2,1)S(1)} collective-permute-done((bf16[64,2048]{1,0:T(8,128)(2,1)S(1)}, bf16[64,2048]{1,0:T(8,128)(2,1)S(1)}, u32[]{:S(2)}, u32[]{:S(2)}) %collective-permute-start.60) | collective-permute-done | bytes 262176 | tf_op jit(solution)/shard_map/ppermute | solution.py:55
  420.8 4.3 all-to-all-start
  425.2 4.4 convolution_convert_fusion.7
  436.1 20.2 %collective-permute-done.65 = bf16[128,2048]{1,0:T(8,128)(2,1)} collective-permute-done((bf16[128,2048]{1,0:T(8,128)(2,1)}, bf16[128,2048]{1,0:T(8,128)(2,1)}, u32[]{:S(2)}, u32[]{:S(2)}) %collective-permute-start.65) | collective-permute-done | bytes 524320 | tf_op jit(solution)/shard_map/ppermute | solution.py:55
  475.2 9.9 %all-to-all-done.1 = bf16[8,65,768]{2,1,0:T(8,128)(2,1)S(1)} async-done(((bf16[8,65,768]{2,1,0:T(8,128)(2,1)}), bf16[8,65,768]{2,1,0:T(8,128)(2,1)S(1)}, u32[]{:S(2)}, u32[]{:S(2)}) %all-to-all-start.1) | async-done | bytes 798752 | tf_op jit(solution)/shard_map/all_to_all | solution.py:671
  (333 shorter events, 187.2 us)
Async XLA Ops:
  7.2 87.5 %all-gather.4.cloned.1.call-start = ((), (), s32[]{:S(2)}) async-start(), calls=%async_computation.6 | async-start | bytes 5242880 | tf_op jit(solution)/shard_map/all_gather | solution.py:552
  11.1 182.4 %all-gather.6.cloned.1.call-start = ((), (), s32[]{:S(2)}) async-start(), calls=%async_computation.7 | async-start | bytes 6553600 | tf_op jit(solution)/shard_map/all_gather | solution.py:552
  11.1 29.3 %collective-permute-start = (bf16[128,2048]{1,0:T(8,128)(2,1)S(1)}, bf16[128,2048]{1,0:T(8,128)(2,1)S(1)}, u32[]{:S(2)}, u32[]{:S(2)}) collective-permute-start(bf16[128,2048]{1,0:T(8,128)(2,1)S(1)} %copy-done.3), channel_id=1, source_target_pairs={{0,1},{1,0},{2,3},{3,2},{4,5},{5,4},{6,7},{7,6},{8,9},{9,8},{10,11... | collective-permute-start | bytes 1572872 | tf_op jit(solution)/shard_map/ppermute | solution.py:55
  11.7 26.5 %collective-permute-start.1 = (bf16[128,2048]{1,0:T(8,128)(2,1)S(1)}, bf16[128,2048]{1,0:T(8,128)(2,1)S(1)}, u32[]{:S(2)}, u32[]{:S(2)}) collective-permute-start(bf16[128,2048]{1,0:T(8,128)(2,1)S(1)} %copy-done.3), channel_id=1, source_target_pairs={{0,2},{1,3},{2,0},{3,1},{4,6},{5,7},{6,4},{7,5},{8,10},{9,11},{10,... | collective-permute-start | bytes 1572872 | tf_op jit(solution)/shard_map/ppermute | solution.py:55
  14.2 25.5 %collective-permute-start.3 = (bf16[128,2048]{1,0:T(8,128)(2,1)S(1)}, bf16[128,2048]{1,0:T(8,128)(2,1)S(1)}, u32[]{:S(2)}, u32[]{:S(2)}) collective-permute-start(bf16[128,2048]{1,0:T(8,128)(2,1)S(1)} %copy-done.3), channel_id=1, source_target_pairs={{0,4},{1,5},{2,6},{3,7},{4,0},{5,1},{6,2},{7,3},{8,12},{9,13},{10,... | collective-permute-start | bytes 1572872 | tf_op jit(solution)/shard_map/ppermute | solution.py:55
  15.8 17.3 %collective-permute-start.8 = (bf16[2,512]{1,0:T(2,128)(2,1)S(1)}, bf16[2,512]{1,0:T(2,128)(2,1)S(1)}, u32[]{:S(2)}, u32[]{:S(2)}) collective-permute-start(bf16[2,512]{1,0:T(2,128)(2,1)S(1)} %pad_maximum_fusion.14), channel_id=1, source_target_pairs={{0,8},{8,16},{16,24},{24,0},{1,9},{9,17},{17,25},{25,1},{2,10},{10... | collective-permute-start | bytes 6152 | tf_op jit(solution)/shard_map/ppermute | solution.py:117
  17.4 17.1 %collective-permute-start.9 = (bf16[2,512]{1,0:T(2,128)(2,1)S(1)}, bf16[2,512]{1,0:T(2,128)(2,1)S(1)}, u32[]{:S(2)}, u32[]{:S(2)}) collective-permute-start(bf16[2,512]{1,0:T(2,128)(2,1)S(1)} %pad_maximum_fusion.14), channel_id=1, source_target_pairs={{0,16},{8,24},{16,0},{24,8},{1,17},{9,25},{17,1},{25,9},{2,18},{10... | collective-permute-start | bytes 6152 | tf_op jit(solution)/shard_map/ppermute | solution.py:117
  25.7 223.1 %all-gather.8.cloned.1.call-start = ((), (), s32[]{:S(2)}) async-start(), calls=%async_computation.8 | async-start | bytes 3276800 | tf_op jit(solution)/shard_map/all_gather | solution.py:552
  52.1 17.1 %collective-permute-start.11 = (bf16[128,2048]{1,0:T(8,128)(2,1)S(1)}, bf16[128,2048]{1,0:T(8,128)(2,1)S(1)}, u32[]{:S(2)}, u32[]{:S(2)}) collective-permute-start(bf16[128,2048]{1,0:T(8,128)(2,1)S(1)} %copy-done.8), channel_id=1, source_target_pairs={{0,1},{1,0},{2,3},{3,2},{4,5},{5,4},{6,7},{7,6},{8,9},{9,8},{10,11... | collective-permute-start | bytes 1572872 | tf_op jit(solution)/shard_map/ppermute | solution.py:55
  52.6 13.8 %collective-permute-start.12 = (bf16[128,2048]{1,0:T(8,128)(2,1)S(1)}, bf16[128,2048]{1,0:T(8,128)(2,1)S(1)}, u32[]{:S(2)}, u32[]{:S(2)}) collective-permute-start(bf16[128,2048]{1,0:T(8,128)(2,1)S(1)} %copy-done.8), channel_id=1, source_target_pairs={{0,2},{1,3},{2,0},{3,1},{4,6},{5,7},{6,4},{7,5},{8,10},{9,11},{10,... | collective-permute-start | bytes 1572872 | tf_op jit(solution)/shard_map/ppermute | solution.py:55
  52.7 14.4 %collective-permute-start.14 = (bf16[128,2048]{1,0:T(8,128)(2,1)S(1)}, bf16[128,2048]{1,0:T(8,128)(2,1)S(1)}, u32[]{:S(2)}, u32[]{:S(2)}) collective-permute-start(bf16[128,2048]{1,0:T(8,128)(2,1)S(1)} %copy-done.8), channel_id=1, source_target_pairs={{0,4},{1,5},{2,6},{3,7},{4,0},{5,1},{6,2},{7,3},{8,12},{9,13},{10,... | collective-permute-start | bytes 1572872 | tf_op jit(solution)/shard_map/ppermute | solution.py:55
  142.2 13.3 %collective-permute-start.23 = (bf16[128,2048]{1,0:T(8,128)(2,1)S(1)}, bf16[128,2048]{1,0:T(8,128)(2,1)S(1)}, u32[]{:S(2)}, u32[]{:S(2)}) collective-permute-start(bf16[128,2048]{1,0:T(8,128)(2,1)S(1)} %pad_maximum_fusion.4), channel_id=1, source_target_pairs={{0,2},{1,3},{2,0},{3,1},{4,6},{5,7},{6,4},{7,5},{8,10},{9,11},{10,... | collective-permute-start | bytes 1572872 | tf_op jit(solution)/shard_map/ppermute | solution.py:55
  144.1 13.7 %collective-permute-start.26 = (bf16[128,2048]{1,0:T(8,128)(2,1)S(1)}, bf16[128,2048]{1,0:T(8,128)(2,1)S(1)}, u32[]{:S(2)}, u32[]{:S(2)}) collective-permute-start(bf16[128,2048]{1,0:T(8,128)(2,1)S(1)} %pad_maximum_fusion.5), channel_id=1, source_target_pairs={{0,4},{1,5},{2,6},{3,7},{4,0},{5,1},{6,2},{7,3},{8,12},{9,13},{10,... | collective-permute-start | bytes 1572872 | tf_op jit(solution)/shard_map/ppermute | solution.py:55
  159.6 13.2 %collective-permute-start.28 = (bf16[128,2048]{1,0:T(8,128)(2,1)}, bf16[128,2048]{1,0:T(8,128)(2,1)}, u32[]{:S(2)}, u32[]{:S(2)}) collective-permute-start(bf16[128,2048]{1,0:T(8,128)(2,1)} %get-tuple-element.91), channel_id=1, source_target_pairs={{0,2},{1,3},{2,0},{3,1},{4,6},{5,7},{6,4},{7,5},{8,10},{9,11},{10,... | collective-permute-start | bytes 1572872 | tf_op jit(solution)/shard_map/ppermute | solution.py:55
  161.6 15.8 %collective-permute-start.27 = (bf16[128,2048]{1,0:T(8,128)(2,1)}, bf16[128,2048]{1,0:T(8,128)(2,1)}, u32[]{:S(2)}, u32[]{:S(2)}) collective-permute-start(bf16[128,2048]{1,0:T(8,128)(2,1)} %get-tuple-element.91), channel_id=1, source_target_pairs={{0,1},{1,0},{2,3},{3,2},{4,5},{5,4},{6,7},{7,6},{8,9},{9,8},{10,11... | collective-permute-start | bytes 1572872 | tf_op jit(solution)/shard_map/ppermute | solution.py:55
  163.6 147.1 %reduce-scatter.5.cloned.1.call-start = ((), (), s32[]{:S(2)}) async-start(), calls=%async_computation.9 | async-start | bytes 3276800 | tf_op jit(solution)/shard_map/reduce_scatter | solution.py:555
  213.4 204.4 %reduce-scatter.7.cloned.1.call-start = ((), (), s32[]{:S(2)}) async-start(), calls=%async_computation.10 | async-start | bytes 6553600 | tf_op jit(solution)/shard_map/reduce_scatter | solution.py:555
  279.5 185.6 %reduce-scatter.9.cloned.1.call-start = ((), (), s32[]{:S(2)}) async-start(), calls=%async_computation.11 | async-start | bytes 3993600 | tf_op jit(solution)/shard_map/reduce_scatter | solution.py:555
  290.4 13.4 %collective-permute-start.39 = (bf16[128,2048]{1,0:T(8,128)(2,1)S(1)}, bf16[128,2048]{1,0:T(8,128)(2,1)S(1)}, u32[]{:S(2)}, u32[]{:S(2)}) collective-permute-start(bf16[128,2048]{1,0:T(8,128)(2,1)S(1)} %pad_maximum_fusion.7), channel_id=1, source_target_pairs={{0,2},{1,3},{2,0},{3,1},{4,6},{5,7},{6,4},{7,5},{8,10},{9,11},{10,... | collective-permute-start | bytes 1572872 | tf_op jit(solution)/shard_map/ppermute | solution.py:55
  293.1 13.3 %collective-permute-start.42 = (bf16[128,2048]{1,0:T(8,128)(2,1)S(1)}, bf16[128,2048]{1,0:T(8,128)(2,1)S(1)}, u32[]{:S(2)}, u32[]{:S(2)}) collective-permute-start(bf16[128,2048]{1,0:T(8,128)(2,1)S(1)} %pad_maximum_fusion.8), channel_id=1, source_target_pairs={{0,4},{1,5},{2,6},{3,7},{4,0},{5,1},{6,2},{7,3},{8,12},{9,13},{10,... | collective-permute-start | bytes 1572872 | tf_op jit(solution)/shard_map/ppermute | solution.py:55
  312.7 13.7 %collective-permute-start.43 = (bf16[128,2048]{1,0:T(8,128)(2,1)}, bf16[128,2048]{1,0:T(8,128)(2,1)S(1)}, u32[]{:S(2)}, u32[]{:S(2)}) collective-permute-start(bf16[128,2048]{1,0:T(8,128)(2,1)} %get-tuple-element.57), channel_id=1, source_target_pairs={{0,1},{1,0},{2,3},{3,2},{4,5},{5,4},{6,7},{7,6},{8,9},{9,8},{10,11... | collective-permute-start | bytes 1572872 | tf_op jit(solution)/shard_map/ppermute | solution.py:55
  335.2 23.1 %collective-permute-start.51 = (bf16[128,2048]{1,0:T(8,128)(2,1)}, bf16[128,2048]{1,0:T(8,128)(2,1)}, u32[]{:S(2)}, u32[]{:S(2)}) collective-permute-start(bf16[128,2048]{1,0:T(8,128)(2,1)} %get-tuple-element.111), channel_id=1, source_target_pairs={{0,1},{1,0},{2,3},{3,2},{4,5},{5,4},{6,7},{7,6},{8,9},{9,8},{10,11... | collective-permute-start | bytes 1572872 | tf_op jit(solution)/shard_map/ppermute | solution.py:55
  335.3 23.0 %collective-permute-start.52 = (bf16[128,2048]{1,0:T(8,128)(2,1)}, bf16[128,2048]{1,0:T(8,128)(2,1)}, u32[]{:S(2)}, u32[]{:S(2)}) collective-permute-start(bf16[128,2048]{1,0:T(8,128)(2,1)} %get-tuple-element.110), channel_id=1, source_target_pairs={{0,1},{1,0},{2,3},{3,2},{4,5},{5,4},{6,7},{7,6},{8,9},{9,8},{10,11... | collective-permute-start | bytes 1572872 | tf_op jit(solution)/shard_map/ppermute | solution.py:55
  335.7 22.6 %collective-permute-start.53 = (bf16[128,2048]{1,0:T(8,128)(2,1)S(1)}, bf16[128,2048]{1,0:T(8,128)(2,1)}, u32[]{:S(2)}, u32[]{:S(2)}) collective-permute-start(bf16[128,2048]{1,0:T(8,128)(2,1)S(1)} %get-tuple-element.109), channel_id=1, source_target_pairs={{0,1},{1,0},{2,3},{3,2},{4,5},{5,4},{6,7},{7,6},{8,9},{9,8},{10,11... | collective-permute-start | bytes 1572872 | tf_op jit(solution)/shard_map/ppermute | solution.py:55
  335.8 22.5 %collective-permute-start.54 = (bf16[128,2048]{1,0:T(8,128)(2,1)S(1)}, bf16[128,2048]{1,0:T(8,128)(2,1)}, u32[]{:S(2)}, u32[]{:S(2)}) collective-permute-start(bf16[128,2048]{1,0:T(8,128)(2,1)S(1)} %get-tuple-element.108), channel_id=1, source_target_pairs={{0,1},{1,0},{2,3},{3,2},{4,5},{5,4},{6,7},{7,6},{8,9},{9,8},{10,11... | collective-permute-start | bytes 1572872 | tf_op jit(solution)/shard_map/ppermute | solution.py:55
  417.8 15.2 %collective-permute-start.63 = (bf16[128,2048]{1,0:T(8,128)(2,1)}, bf16[128,2048]{1,0:T(8,128)(2,1)}, u32[]{:S(2)}, u32[]{:S(2)}) collective-permute-start(bf16[128,2048]{1,0:T(8,128)(2,1)} %pad_maximum_fusion.10), channel_id=1, source_target_pairs={{0,2},{1,3},{2,0},{3,1},{4,6},{5,7},{6,4},{7,5},{8,10},{9,11},{10,... | collective-permute-start | bytes 1572872 | tf_op jit(solution)/shard_map/ppermute | solution.py:55
  418.6 15.9 %collective-permute-start.64 = (bf16[128,2048]{1,0:T(8,128)(2,1)}, bf16[128,2048]{1,0:T(8,128)(2,1)}, u32[]{:S(2)}, u32[]{:S(2)}) collective-permute-start(bf16[128,2048]{1,0:T(8,128)(2,1)} %pad_maximum_fusion.11), channel_id=1, source_target_pairs={{0,4},{1,5},{2,6},{3,7},{4,0},{5,1},{6,2},{7,3},{8,12},{9,13},{10,... | collective-permute-start | bytes 1572872 | tf_op jit(solution)/shard_map/ppermute | solution.py:55
  420.8 38.7 %all-to-all-start = ((bf16[8,64,1280]{2,1,0:T(8,128)(2,1)}), bf16[8,64,1280]{2,1,0:T(8,128)(2,1)}, u32[]{:S(2)}, u32[]{:S(2)}) async-start(bf16[8,64,1280]{2,1,0:T(8,128)(2,1)} %bitcast.71), calls=%async_computation.2 | async-start | bytes 2621440 | tf_op jit(solution)/shard_map/all_to_all | solution.py:559
  425.1 66.0 %reduce-scatter.11.cloned.1.call-start = ((), (), s32[]{:S(2)}) async-start(), calls=%async_computation.12 | async-start | bytes 1310720 | tf_op jit(solution)/shard_map/reduce_scatter | solution.py:555
  429.6 26.7 %collective-permute-start.65 = (bf16[128,2048]{1,0:T(8,128)(2,1)}, bf16[128,2048]{1,0:T(8,128)(2,1)}, u32[]{:S(2)}, u32[]{:S(2)}) collective-permute-start(bf16[128,2048]{1,0:T(8,128)(2,1)} %pad_maximum_fusion.12), channel_id=1, source_target_pairs={{0,2},{1,3},{2,0},{3,1},{4,6},{5,7},{6,4},{7,5},{8,10},{9,11},{10,... | collective-permute-start | bytes 1572872 | tf_op jit(solution)/shard_map/ppermute | solution.py:55
  431.4 25.4 %collective-permute-start.66 = (bf16[128,2048]{1,0:T(8,128)(2,1)S(1)}, bf16[128,2048]{1,0:T(8,128)(2,1)}, u32[]{:S(2)}, u32[]{:S(2)}) collective-permute-start(bf16[128,2048]{1,0:T(8,128)(2,1)S(1)} %pad_maximum_fusion.13), channel_id=1, source_target_pairs={{0,4},{1,5},{2,6},{3,7},{4,0},{5,1},{6,2},{7,3},{8,12},{9,13},{10,... | collective-permute-start | bytes 1572872 | tf_op jit(solution)/shard_map/ppermute | solution.py:55
  468.0 17.1 %all-to-all-start.1 = ((bf16[8,65,768]{2,1,0:T(8,128)(2,1)}), bf16[8,65,768]{2,1,0:T(8,128)(2,1)S(1)}, u32[]{:S(2)}, u32[]{:S(2)}) async-start(bf16[8,65,768]{2,1,0:T(8,128)(2,1)} %pad_maximum_fusion.1), calls=%async_computation.4 | async-start | bytes 1769472 | tf_op jit(solution)/shard_map/all_to_all | solution.py:671
  (66 other events, 491.9 us)
Sparse Core Ops, SparseCore 0:
  11.2 83.4 all-gather.3
  96.9 96.5 all-gather.5
  195.6 53.1 all-gather.7
  251.0 50.8 reduce-scatter.4
  304.1 93.4 reduce-scatter.6
  399.7 61.6 reduce-scatter.8
  463.8 27.2 reduce-scatter.10

commit v7 on v5

--- a/solution.py
+++ b/solution.py
@@ -696,9 +696,8 @@
     input_grad = (residual_grad + first_back(normed_grad)[0]).astype(bf16)
 
     def gain_grad(gain, pairs):
-        return sum(jnp.sum(own_rows(w).astype(f32) * g, axis=1) for w, g in pairs) / own_rows(
-            gain
-        ).astype(f32)
+        products = sum(own_rows(w).astype(f32) * g for w, g in pairs)
+        return jnp.sum(products, axis=1) / own_rows(gain).astype(f32)
 
     down_shard = down_sum.astype(f32)
     ff_gain_shard = gain_grad(gain_ff, ((w_gate, gate_shard), (w_up, up_shard)))

time: 506 us -> 505 us (level)
  transfers between devices with their start and end apart: 76 -> 76, of which waited for: 37 -> 38; matrix products, arithmetic and copies ran while one was open for 32% -> 32% of each run, Pallas kernels for 15% -> 15%
where the time goes in v7:
time: 505 us; the launch traced here: 500 us
  waiting for transfers between devices  177 us (35%)
  Pallas kernels  80.5 us (16%)
  matrix products  74.4 us (15%)
  starting transfers between devices  58.8 us (12%)
  local copies, waits for them, and re-layouts  47.9 us (9%)
  other arithmetic  46.8 us (9%)
  between operations  15.3 us (3%)
    ppermute x64, waiting for transfers between devices, swap(): lax.ppermute(block, 'ctx', [(i, i ^ mask) for i in range(lax.axis_size('c...  107 us
    dot_general x12, matrix products, dot(): lax.dot_general(left, right, (contract, ((), ())), preferred_element_type...  73.7 us
    all_gather x3, waiting for transfers between devices, over_planes(): return lax.all_gather(weight, 'fsdp', axis=0, tiled=True)  56.3 us
    ppermute x64, starting transfers between devices, swap(): lax.ppermute(block, 'ctx', [(i, i ^ mask) for i in range(lax.axis_size('c...  44.2 us
    pallas_call x2, Pallas kernels, attend_back(): pl.pallas_call(functools.partial(backward_kernel, kept=len(aliases)), gri...  40.2 us
    unnamed x77, local copies, waits for them, and re-layouts  29.5 us
    pallas_call x1, Pallas kernels, attend(): pl.pallas_call(forward_kernel, grid=(pairs,), out_shape=(jax.ShapeDtypeSt...  22.5 us
  transfers between devices with their start and end apart: 76, of which 38 were waited for; matrix products, arithmetic and copies ran while one was open for 32% of the time, Pallas kernels for 15%

profile of v7, /device:TPU:0, one launch (start us, length us, event | category | flops | bytes accessed | tf_op | source)
XLA Modules:
  0.0 500.4 jit_solution(2333628321641483381)
XLA Ops:
  7.3 3.6 cut_heads.1
  20.4 5.1 %cut_hidden.1 = bf16[512,1280]{1,0:T(8,128)(2,1)} custom-call(s32[3]{0:T(128)} %pad_add_fusion.start_ref, bf16[512,5120]{1,0:T(8,128)(2,1)} %refs_7_.1, bf16[512,5120]{1,0:T(8,128)(2,1)} %refs_7_.1, bf16[512,5120]{1,0:T(8,128)(2,1)} %refs_7_.1, bf16[512,5120]{1,0:T(8,128)(2,1)} %refs_7_.1, bf16[512,5120]{1,0:T(8,128)(2,1)} %refs_7_.1, ...), custom_call_target="tpu_custom_call" | custom-call | tf_op jit(solution)/shard_map/cut_hidden/pallas_call | solution.py:170
  28.8 4.0 bias_tiles.1.tiles_ref
  60.5 5.7 %collective-permute-done.12 = bf16[128,2048]{1,0:T(8,128)(2,1)S(1)} collective-permute-done((bf16[128,2048]{1,0:T(8,128)(2,1)S(1)}, bf16[128,2048]{1,0:T(8,128)(2,1)S(1)}, u32[]{:S(2)}, u32[]{:S(2)}) %collective-permute-start.12) | collective-permute-done | bytes 524320 | tf_op jit(solution)/shard_map/ppermute | solution.py:55
  79.2 15.4 %all-gather.4.cloned.1.call-done = bf16[2048,1024]{1,0:T(8,128)(2,1)} async-done(((bf16[512,1024]{1,0:T(8,128)(2,1)}), bf16[2048,1024]{1,0:T(8,128)(2,1)}) %all-gather.4.cloned.1.call-update) | async-done | bytes 4194320 | tf_op jit(solution)/shard_map/all_gather | solution.py:569
  97.0 6.4 %fusion.15.q_ref.k_ref.v_ref = bf16[1024,768]{1,0:T(8,128)(2,1)} fusion(bf16[1024,2048]{1,0:T(8,128)(2,1)S(1)} %copy-done.6, bf16[2048,1024]{1,0:T(8,128)(2,1)} %all-gather.4.cloned.1.call-done), kind=kOutput, calls=%fused_computation.37 | convolution fusion | flops 3222011904 | bytes 8912896 | tf_op jit(solution)/shard_map/dot_general | solution.py:51
  104.5 22.5 %attend_forward.1 = (bf16[256,1024]{1,0:T(8,128)(2,1)}, f32[2,2,8,128]{3,2,1,0:T(8,128)}) custom-call(s32[1]{0:T(128)} %bitcast.base_ref, bf16[1024,768]{1,0:T(8,128)(2,1)} %fusion.15.q_ref.k_ref.v_ref, bf16[1024,768]{1,0:T(8,128)(2,1)} %fusion.15.q_ref.k_ref.v_ref, bf16[1024,768]{1,0:T(8,128)(2,1)} %fusion.15.q_ref.k_ref.v_ref, ...), custom_call_target="tpu_custom_call" | custom-call | tf_op jit(solution)/shard_map/attend_forward/pallas_call | solution.py:398
  136.6 5.3 %collective-permute-done.22 = bf16[64,2048]{1,0:T(8,128)(2,1)S(1)} collective-permute-done((bf16[64,2048]{1,0:T(8,128)(2,1)S(1)}, bf16[64,2048]{1,0:T(8,128)(2,1)S(1)}, u32[]{:S(2)}, u32[]{:S(2)}) %collective-permute-start.22) | collective-permute-done | bytes 262176 | tf_op jit(solution)/shard_map/ppermute | solution.py:55
  145.2 10.2 %collective-permute-done.23 = bf16[128,2048]{1,0:T(8,128)(2,1)S(1)} collective-permute-done((bf16[128,2048]{1,0:T(8,128)(2,1)S(1)}, bf16[128,2048]{1,0:T(8,128)(2,1)S(1)}, u32[]{:S(2)}, u32[]{:S(2)}) %collective-permute-start.23) | collective-permute-done | bytes 524320 | tf_op jit(solution)/shard_map/ppermute | solution.py:55
  163.7 9.0 %collective-permute-done.28 = bf16[128,2048]{1,0:T(8,128)(2,1)} collective-permute-done((bf16[128,2048]{1,0:T(8,128)(2,1)}, bf16[128,2048]{1,0:T(8,128)(2,1)}, u32[]{:S(2)}, u32[]{:S(2)}) %collective-permute-start.28) | collective-permute-done | bytes 524320 | tf_op jit(solution)/shard_map/ppermute | solution.py:55
  187.4 5.9 %all-gather.6.cloned.1.call-done = bf16[2048,1280]{1,0:T(8,128)(2,1)} async-done(((bf16[512,1280]{1,0:T(8,128)(2,1)}), bf16[2048,1280]{1,0:T(8,128)(2,1)}) %all-gather.6.cloned.1.call-update) | async-done | bytes 5242896 | tf_op jit(solution)/shard_map/all_gather | solution.py:569
  193.3 8.9 %fusion.46 = f32[1024,1280]{1,0:T(8,128)S(1)} fusion(bf16[1024,2048]{1,0:T(8,128)(2,1)} %constant_dynamic-update-slice_fusion.18, bf16[2048,1280]{1,0:T(8,128)(2,1)} %all-gather.6.cloned.1.call-done), kind=kOutput, calls=%fused_computation.185 | convolution fusion | flops 5368709120 | bytes 14680064 | tf_op jit(solution)/shard_map/dot_general | solution.py:51
  206.5 6.6 %convolution_convert_fusion.6 = bf16[640,2048]{1,0:T(8,128)(2,1)} fusion(bf16[1024,640]{1,0:T(8,128)(2,1)S(1)} %multiply_convert_fusion.1, bf16[1024,2048]{1,0:T(8,128)(2,1)} %constant_dynamic-update-slice_fusion.9), kind=kOutput, calls=%fused_computation.17 | convolution fusion | flops 2685665280 | bytes 8126464 | tf_op jit(solution)/shard_map/dot_general | solution.py:51
  213.6 35.0 %all-gather.8.cloned.1.call-done = bf16[640,2048]{1,0:T(8,128)(2,1)} async-done(((bf16[160,2048]{1,0:T(8,128)(2,1)}), bf16[640,2048]{1,0:T(8,128)(2,1)}) %all-gather.8.cloned.1.call-update) | async-done | bytes 2621456 | tf_op jit(solution)/shard_map/all_gather | solution.py:569
  248.7 9.4 %fusion.14 = (bf16[1024,640]{1,0:T(8,128)(2,1)S(1)}, bf16[1024,640]{1,0:T(8,128)(2,1)S(1)}) fusion(f32[1024,1280]{1,0:T(8,128)} %copy-done.5, bf16[1024,2048]{1,0:T(8,128)(2,1)} %constant_dynamic-update-slice_fusion.9, bf16[640,2048]{1,0:T(8,128)(2,1)} %all-gather.8.cloned.1.call-done), kind=kOutput, calls=%fused_computation.27 | convolution fusion | flops 2700083200 | bytes 14680064 | tf_op jit(solution)/shard_map/dot_general | solution.py:51
  258.2 8.4 %convolution_convert_fusion.2 = bf16[1024,2048]{1,0:T(8,128)(2,1)S(1)} fusion(bf16[2048,1280]{1,0:T(8,128)(2,1)} %all-gather.6.cloned.1.call-done, bf16[1024,640]{1,0:T(8,128)(2,1)S(1)} %get-tuple-element.95, bf16[1024,640]{1,0:T(8,128)(2,1)S(1)} %get-tuple-element.94), kind=kOutput, calls=%fused_computation.10 | convolution fusion | flops 5376049152 | bytes 12058624 | tf_op jit(solution)/shard_map/dot_general | solution.py:51
  271.6 7.6 %convolution_convert_fusion = bf16[2048,1280]{1,0:T(8,128)(2,1)} fusion(bf16[1024,2048]{1,0:T(8,128)(2,1)S(1)} %copy-done.15, bf16[1024,1280]{1,0:T(8,128)(2,1)S(1)} %pad_maximum_fusion), kind=kOutput, calls=%fused_computation.6 | convolution fusion | flops 5371330560 | bytes 12058624 | tf_op jit(solution)/shard_map/dot_general | solution.py:51
  285.2 4.9 collective-permute-done.38
  293.4 10.3 %collective-permute-done.39 = bf16[128,2048]{1,0:T(8,128)(2,1)S(1)} collective-permute-done((bf16[128,2048]{1,0:T(8,128)(2,1)S(1)}, bf16[128,2048]{1,0:T(8,128)(2,1)S(1)}, u32[]{:S(2)}, u32[]{:S(2)}) %collective-permute-start.39) | collective-permute-done | bytes 524320 | tf_op jit(solution)/shard_map/ppermute | solution.py:55
  312.5 5.6 %convolution_convert_fusion.1 = bf16[1024,2048]{1,0:T(8,128)(2,1)S(1)} fusion(bf16[1024,640]{1,0:T(8,128)(2,1)} %copy-done.10, bf16[640,2048]{1,0:T(8,128)(2,1)} %all-gather.8.cloned.1.call-done), kind=kOutput, calls=%fused_computation.9 | convolution fusion | flops 2686451712 | bytes 8126464 | tf_op jit(solution)/shard_map/dot_general | solution.py:51
  318.1 4.9 collective-permute-done.44
  326.3 3.6 collective-permute-done.48
  338.1 20.0 %attend_backward.2 = (bf16[1024,768]{1,0:T(8,128)(2,1)}, f32[2,32,8,128]{3,2,1,0:T(8,128)}) custom-call(s32[1]{0:T(128)} %bitcast.base_ref, bf16[1024,768]{1,0:T(8,128)(2,1)} %fusion.15.q_ref.k_ref.v_ref, bf16[1024,768]{1,0:T(8,128)(2,1)} %fusion.15.q_ref.k_ref.v_ref, bf16[1024,768]{1,0:T(8,128)(2,1)} %fusion.15.q_ref.k_ref.v_ref, ...), custom_call_target="tpu_custom_call" | custom-call | tf_op jit(solution)/shard_map/attend_backward/pallas_call | solution.py:515
  358.1 3.6 add_convert_fusion.2
  361.7 20.3 %attend_backward.3 = (bf16[1024,768]{1,0:T(8,128)(2,1)}, f32[2,32,8,128]{3,2,1,0:T(8,128)}) custom-call(s32[1]{0:T(128)} %bitcast.base_ref, bf16[1024,768]{1,0:T(8,128)(2,1)} %fusion.15.q_ref.k_ref.v_ref, bf16[1024,768]{1,0:T(8,128)(2,1)} %fusion.15.q_ref.k_ref.v_ref, bf16[1024,768]{1,0:T(8,128)(2,1)} %fusion.15.q_ref.k_ref.v_ref, ...), custom_call_target="tpu_custom_call", output_to_operand_aliasing={{0}: (9, {})} | custom-call | tf_op jit(solution)/shard_map/attend_backward/pallas_call | solution.py:515
  383.3 6.2 %convolution_convert_fusion.5 = bf16[2048,768]{1,0:T(8,128)(2,1)S(1)} fusion(bf16[1024,2048]{1,0:T(8,128)(2,1)} %fusion.2, bf16[1024,768]{1,0:T(8,128)(2,1)} %get-tuple-element.65), kind=kOutput, calls=%fused_computation.15 | convolution fusion | flops 3222798336 | bytes 8912896 | tf_op jit(solution)/shard_map/dot_general | solution.py:51
  394.4 5.8 %convolution_convert_fusion.4 = bf16[1024,2048]{1,0:T(8,128)(2,1)S(1)} fusion(bf16[1024,768]{1,0:T(8,128)(2,1)} %get-tuple-element.65, bf16[2048,1024]{1,0:T(8,128)(2,1)} %all-gather.4.cloned.1.call-done), kind=kOutput, calls=%fused_computation.12 | convolution fusion | flops 3223322624 | bytes 8912896 | tf_op jit(solution)/shard_map/dot_general | solution.py:51
  409.7 5.0 %collective-permute-done.60 = bf16[64,2048]{1,0:T(8,128)(2,1)S(1)} collective-permute-done((bf16[64,2048]{1,0:T(8,128)(2,1)S(1)}, bf16[64,2048]{1,0:T(8,128)(2,1)S(1)}, u32[]{:S(2)}, u32[]{:S(2)}) %collective-permute-start.60) | collective-permute-done | bytes 262176 | tf_op jit(solution)/shard_map/ppermute | solution.py:55
  420.6 4.3 all-to-all-start
  425.0 4.4 convolution_convert_fusion.7
  435.9 20.2 %collective-permute-done.65 = bf16[128,2048]{1,0:T(8,128)(2,1)} collective-permute-done((bf16[128,2048]{1,0:T(8,128)(2,1)}, bf16[128,2048]{1,0:T(8,128)(2,1)}, u32[]{:S(2)}, u32[]{:S(2)}) %collective-permute-start.65) | collective-permute-done | bytes 524320 | tf_op jit(solution)/shard_map/ppermute | solution.py:55
  475.0 9.9 %all-to-all-done.1 = bf16[8,65,768]{2,1,0:T(8,128)(2,1)S(1)} async-done(((bf16[8,65,768]{2,1,0:T(8,128)(2,1)}), bf16[8,65,768]{2,1,0:T(8,128)(2,1)S(1)}, u32[]{:S(2)}, u32[]{:S(2)}) %all-to-all-start.1) | async-done | bytes 798752 | tf_op jit(solution)/shard_map/all_to_all | solution.py:688
  (333 shorter events, 187.1 us)
Async XLA Ops:
  7.2 87.3 %all-gather.4.cloned.1.call-start = ((), (), s32[]{:S(2)}) async-start(), calls=%async_computation.6 | async-start | bytes 5242880 | tf_op jit(solution)/shard_map/all_gather | solution.py:569
  10.9 182.4 %all-gather.6.cloned.1.call-start = ((), (), s32[]{:S(2)}) async-start(), calls=%async_computation.7 | async-start | bytes 6553600 | tf_op jit(solution)/shard_map/all_gather | solution.py:569
  10.9 29.3 %collective-permute-start = (bf16[128,2048]{1,0:T(8,128)(2,1)S(1)}, bf16[128,2048]{1,0:T(8,128)(2,1)S(1)}, u32[]{:S(2)}, u32[]{:S(2)}) collective-permute-start(bf16[128,2048]{1,0:T(8,128)(2,1)S(1)} %copy-done.3), channel_id=1, source_target_pairs={{0,1},{1,0},{2,3},{3,2},{4,5},{5,4},{6,7},{7,6},{8,9},{9,8},{10,11... | collective-permute-start | bytes 1572872 | tf_op jit(solution)/shard_map/ppermute | solution.py:55
  11.5 26.5 %collective-permute-start.1 = (bf16[128,2048]{1,0:T(8,128)(2,1)S(1)}, bf16[128,2048]{1,0:T(8,128)(2,1)S(1)}, u32[]{:S(2)}, u32[]{:S(2)}) collective-permute-start(bf16[128,2048]{1,0:T(8,128)(2,1)S(1)} %copy-done.3), channel_id=1, source_target_pairs={{0,2},{1,3},{2,0},{3,1},{4,6},{5,7},{6,4},{7,5},{8,10},{9,11},{10,... | collective-permute-start | bytes 1572872 | tf_op jit(solution)/shard_map/ppermute | solution.py:55
  14.0 25.5 %collective-permute-start.3 = (bf16[128,2048]{1,0:T(8,128)(2,1)S(1)}, bf16[128,2048]{1,0:T(8,128)(2,1)S(1)}, u32[]{:S(2)}, u32[]{:S(2)}) collective-permute-start(bf16[128,2048]{1,0:T(8,128)(2,1)S(1)} %copy-done.3), channel_id=1, source_target_pairs={{0,4},{1,5},{2,6},{3,7},{4,0},{5,1},{6,2},{7,3},{8,12},{9,13},{10,... | collective-permute-start | bytes 1572872 | tf_op jit(solution)/shard_map/ppermute | solution.py:55
  15.6 17.3 %collective-permute-start.8 = (bf16[2,512]{1,0:T(2,128)(2,1)S(1)}, bf16[2,512]{1,0:T(2,128)(2,1)S(1)}, u32[]{:S(2)}, u32[]{:S(2)}) collective-permute-start(bf16[2,512]{1,0:T(2,128)(2,1)S(1)} %pad_maximum_fusion.14), channel_id=1, source_target_pairs={{0,8},{8,16},{16,24},{24,0},{1,9},{9,17},{17,25},{25,1},{2,10},{10... | collective-permute-start | bytes 6152 | tf_op jit(solution)/shard_map/ppermute | solution.py:117
  17.2 17.1 %collective-permute-start.9 = (bf16[2,512]{1,0:T(2,128)(2,1)S(1)}, bf16[2,512]{1,0:T(2,128)(2,1)S(1)}, u32[]{:S(2)}, u32[]{:S(2)}) collective-permute-start(bf16[2,512]{1,0:T(2,128)(2,1)S(1)} %pad_maximum_fusion.14), channel_id=1, source_target_pairs={{0,16},{8,24},{16,0},{24,8},{1,17},{9,25},{17,1},{25,9},{2,18},{10... | collective-permute-start | bytes 6152 | tf_op jit(solution)/shard_map/ppermute | solution.py:117
  25.5 223.1 %all-gather.8.cloned.1.call-start = ((), (), s32[]{:S(2)}) async-start(), calls=%async_computation.8 | async-start | bytes 3276800 | tf_op jit(solution)/shard_map/all_gather | solution.py:569
  51.9 17.1 %collective-permute-start.11 = (bf16[128,2048]{1,0:T(8,128)(2,1)S(1)}, bf16[128,2048]{1,0:T(8,128)(2,1)S(1)}, u32[]{:S(2)}, u32[]{:S(2)}) collective-permute-start(bf16[128,2048]{1,0:T(8,128)(2,1)S(1)} %copy-done.8), channel_id=1, source_target_pairs={{0,1},{1,0},{2,3},{3,2},{4,5},{5,4},{6,7},{7,6},{8,9},{9,8},{10,11... | collective-permute-start | bytes 1572872 | tf_op jit(solution)/shard_map/ppermute | solution.py:55
  52.4 13.8 %collective-permute-start.12 = (bf16[128,2048]{1,0:T(8,128)(2,1)S(1)}, bf16[128,2048]{1,0:T(8,128)(2,1)S(1)}, u32[]{:S(2)}, u32[]{:S(2)}) collective-permute-start(bf16[128,2048]{1,0:T(8,128)(2,1)S(1)} %copy-done.8), channel_id=1, source_target_pairs={{0,2},{1,3},{2,0},{3,1},{4,6},{5,7},{6,4},{7,5},{8,10},{9,11},{10,... | collective-permute-start | bytes 1572872 | tf_op jit(solution)/shard_map/ppermute | solution.py:55
  52.5 14.4 %collective-permute-start.14 = (bf16[128,2048]{1,0:T(8,128)(2,1)S(1)}, bf16[128,2048]{1,0:T(8,128)(2,1)S(1)}, u32[]{:S(2)}, u32[]{:S(2)}) collective-permute-start(bf16[128,2048]{1,0:T(8,128)(2,1)S(1)} %copy-done.8), channel_id=1, source_target_pairs={{0,4},{1,5},{2,6},{3,7},{4,0},{5,1},{6,2},{7,3},{8,12},{9,13},{10,... | collective-permute-start | bytes 1572872 | tf_op jit(solution)/shard_map/ppermute | solution.py:55
  142.1 13.3 %collective-permute-start.23 = (bf16[128,2048]{1,0:T(8,128)(2,1)S(1)}, bf16[128,2048]{1,0:T(8,128)(2,1)S(1)}, u32[]{:S(2)}, u32[]{:S(2)}) collective-permute-start(bf16[128,2048]{1,0:T(8,128)(2,1)S(1)} %pad_maximum_fusion.4), channel_id=1, source_target_pairs={{0,2},{1,3},{2,0},{3,1},{4,6},{5,7},{6,4},{7,5},{8,10},{9,11},{10,... | collective-permute-start | bytes 1572872 | tf_op jit(solution)/shard_map/ppermute | solution.py:55
  144.1 13.7 %collective-permute-start.26 = (bf16[128,2048]{1,0:T(8,128)(2,1)S(1)}, bf16[128,2048]{1,0:T(8,128)(2,1)S(1)}, u32[]{:S(2)}, u32[]{:S(2)}) collective-permute-start(bf16[128,2048]{1,0:T(8,128)(2,1)S(1)} %pad_maximum_fusion.5), channel_id=1, source_target_pairs={{0,4},{1,5},{2,6},{3,7},{4,0},{5,1},{6,2},{7,3},{8,12},{9,13},{10,... | collective-permute-start | bytes 1572872 | tf_op jit(solution)/shard_map/ppermute | solution.py:55
  159.5 13.2 %collective-permute-start.28 = (bf16[128,2048]{1,0:T(8,128)(2,1)}, bf16[128,2048]{1,0:T(8,128)(2,1)}, u32[]{:S(2)}, u32[]{:S(2)}) collective-permute-start(bf16[128,2048]{1,0:T(8,128)(2,1)} %get-tuple-element.91), channel_id=1, source_target_pairs={{0,2},{1,3},{2,0},{3,1},{4,6},{5,7},{6,4},{7,5},{8,10},{9,11},{10,... | collective-permute-start | bytes 1572872 | tf_op jit(solution)/shard_map/ppermute | solution.py:55
  161.4 15.8 %collective-permute-start.27 = (bf16[128,2048]{1,0:T(8,128)(2,1)}, bf16[128,2048]{1,0:T(8,128)(2,1)}, u32[]{:S(2)}, u32[]{:S(2)}) collective-permute-start(bf16[128,2048]{1,0:T(8,128)(2,1)} %get-tuple-element.91), channel_id=1, source_target_pairs={{0,1},{1,0},{2,3},{3,2},{4,5},{5,4},{6,7},{7,6},{8,9},{9,8},{10,11... | collective-permute-start | bytes 1572872 | tf_op jit(solution)/shard_map/ppermute | solution.py:55
  163.4 147.1 %reduce-scatter.5.cloned.1.call-start = ((), (), s32[]{:S(2)}) async-start(), calls=%async_computation.9 | async-start | bytes 3276800 | tf_op jit(solution)/shard_map/reduce_scatter | solution.py:572
  213.2 204.4 %reduce-scatter.7.cloned.1.call-start = ((), (), s32[]{:S(2)}) async-start(), calls=%async_computation.10 | async-start | bytes 6553600 | tf_op jit(solution)/shard_map/reduce_scatter | solution.py:572
  279.3 185.6 %reduce-scatter.9.cloned.1.call-start = ((), (), s32[]{:S(2)}) async-start(), calls=%async_computation.11 | async-start | bytes 3993600 | tf_op jit(solution)/shard_map/reduce_scatter | solution.py:572
  290.2 13.4 %collective-permute-start.39 = (bf16[128,2048]{1,0:T(8,128)(2,1)S(1)}, bf16[128,2048]{1,0:T(8,128)(2,1)S(1)}, u32[]{:S(2)}, u32[]{:S(2)}) collective-permute-start(bf16[128,2048]{1,0:T(8,128)(2,1)S(1)} %pad_maximum_fusion.7), channel_id=1, source_target_pairs={{0,2},{1,3},{2,0},{3,1},{4,6},{5,7},{6,4},{7,5},{8,10},{9,11},{10,... | collective-permute-start | bytes 1572872 | tf_op jit(solution)/shard_map/ppermute | solution.py:55
  292.9 13.3 %collective-permute-start.42 = (bf16[128,2048]{1,0:T(8,128)(2,1)S(1)}, bf16[128,2048]{1,0:T(8,128)(2,1)S(1)}, u32[]{:S(2)}, u32[]{:S(2)}) collective-permute-start(bf16[128,2048]{1,0:T(8,128)(2,1)S(1)} %pad_maximum_fusion.8), channel_id=1, source_target_pairs={{0,4},{1,5},{2,6},{3,7},{4,0},{5,1},{6,2},{7,3},{8,12},{9,13},{10,... | collective-permute-start | bytes 1572872 | tf_op jit(solution)/shard_map/ppermute | solution.py:55
  312.5 13.7 %collective-permute-start.43 = (bf16[128,2048]{1,0:T(8,128)(2,1)}, bf16[128,2048]{1,0:T(8,128)(2,1)S(1)}, u32[]{:S(2)}, u32[]{:S(2)}) collective-permute-start(bf16[128,2048]{1,0:T(8,128)(2,1)} %get-tuple-element.57), channel_id=1, source_target_pairs={{0,1},{1,0},{2,3},{3,2},{4,5},{5,4},{6,7},{7,6},{8,9},{9,8},{10,11... | collective-permute-start | bytes 1572872 | tf_op jit(solution)/shard_map/ppermute | solution.py:55
  335.0 23.1 %collective-permute-start.51 = (bf16[128,2048]{1,0:T(8,128)(2,1)}, bf16[128,2048]{1,0:T(8,128)(2,1)}, u32[]{:S(2)}, u32[]{:S(2)}) collective-permute-start(bf16[128,2048]{1,0:T(8,128)(2,1)} %get-tuple-element.111), channel_id=1, source_target_pairs={{0,1},{1,0},{2,3},{3,2},{4,5},{5,4},{6,7},{7,6},{8,9},{9,8},{10,11... | collective-permute-start | bytes 1572872 | tf_op jit(solution)/shard_map/ppermute | solution.py:55
  335.1 23.0 %collective-permute-start.52 = (bf16[128,2048]{1,0:T(8,128)(2,1)}, bf16[128,2048]{1,0:T(8,128)(2,1)}, u32[]{:S(2)}, u32[]{:S(2)}) collective-permute-start(bf16[128,2048]{1,0:T(8,128)(2,1)} %get-tuple-element.110), channel_id=1, source_target_pairs={{0,1},{1,0},{2,3},{3,2},{4,5},{5,4},{6,7},{7,6},{8,9},{9,8},{10,11... | collective-permute-start | bytes 1572872 | tf_op jit(solution)/shard_map/ppermute | solution.py:55
  335.5 22.6 %collective-permute-start.53 = (bf16[128,2048]{1,0:T(8,128)(2,1)S(1)}, bf16[128,2048]{1,0:T(8,128)(2,1)}, u32[]{:S(2)}, u32[]{:S(2)}) collective-permute-start(bf16[128,2048]{1,0:T(8,128)(2,1)S(1)} %get-tuple-element.109), channel_id=1, source_target_pairs={{0,1},{1,0},{2,3},{3,2},{4,5},{5,4},{6,7},{7,6},{8,9},{9,8},{10,11... | collective-permute-start | bytes 1572872 | tf_op jit(solution)/shard_map/ppermute | solution.py:55
  335.6 22.5 %collective-permute-start.54 = (bf16[128,2048]{1,0:T(8,128)(2,1)S(1)}, bf16[128,2048]{1,0:T(8,128)(2,1)}, u32[]{:S(2)}, u32[]{:S(2)}) collective-permute-start(bf16[128,2048]{1,0:T(8,128)(2,1)S(1)} %get-tuple-element.108), channel_id=1, source_target_pairs={{0,1},{1,0},{2,3},{3,2},{4,5},{5,4},{6,7},{7,6},{8,9},{9,8},{10,11... | collective-permute-start | bytes 1572872 | tf_op jit(solution)/shard_map/ppermute | solution.py:55
  417.6 15.2 %collective-permute-start.63 = (bf16[128,2048]{1,0:T(8,128)(2,1)}, bf16[128,2048]{1,0:T(8,128)(2,1)}, u32[]{:S(2)}, u32[]{:S(2)}) collective-permute-start(bf16[128,2048]{1,0:T(8,128)(2,1)} %pad_maximum_fusion.10), channel_id=1, source_target_pairs={{0,2},{1,3},{2,0},{3,1},{4,6},{5,7},{6,4},{7,5},{8,10},{9,11},{10,... | collective-permute-start | bytes 1572872 | tf_op jit(solution)/shard_map/ppermute | solution.py:55
  418.4 15.9 %collective-permute-start.64 = (bf16[128,2048]{1,0:T(8,128)(2,1)}, bf16[128,2048]{1,0:T(8,128)(2,1)}, u32[]{:S(2)}, u32[]{:S(2)}) collective-permute-start(bf16[128,2048]{1,0:T(8,128)(2,1)} %pad_maximum_fusion.11), channel_id=1, source_target_pairs={{0,4},{1,5},{2,6},{3,7},{4,0},{5,1},{6,2},{7,3},{8,12},{9,13},{10,... | collective-permute-start | bytes 1572872 | tf_op jit(solution)/shard_map/ppermute | solution.py:55
  420.6 38.7 %all-to-all-start = ((bf16[8,64,1280]{2,1,0:T(8,128)(2,1)}), bf16[8,64,1280]{2,1,0:T(8,128)(2,1)}, u32[]{:S(2)}, u32[]{:S(2)}) async-start(bf16[8,64,1280]{2,1,0:T(8,128)(2,1)} %bitcast.71), calls=%async_computation.2 | async-start | bytes 2621440 | tf_op jit(solution)/shard_map/all_to_all | solution.py:576
  424.9 66.0 %reduce-scatter.11.cloned.1.call-start = ((), (), s32[]{:S(2)}) async-start(), calls=%async_computation.12 | async-start | bytes 1310720 | tf_op jit(solution)/shard_map/reduce_scatter | solution.py:572
  429.4 26.7 %collective-permute-start.65 = (bf16[128,2048]{1,0:T(8,128)(2,1)}, bf16[128,2048]{1,0:T(8,128)(2,1)}, u32[]{:S(2)}, u32[]{:S(2)}) collective-permute-start(bf16[128,2048]{1,0:T(8,128)(2,1)} %pad_maximum_fusion.12), channel_id=1, source_target_pairs={{0,2},{1,3},{2,0},{3,1},{4,6},{5,7},{6,4},{7,5},{8,10},{9,11},{10,... | collective-permute-start | bytes 1572872 | tf_op jit(solution)/shard_map/ppermute | solution.py:55
  431.2 25.4 %collective-permute-start.66 = (bf16[128,2048]{1,0:T(8,128)(2,1)S(1)}, bf16[128,2048]{1,0:T(8,128)(2,1)}, u32[]{:S(2)}, u32[]{:S(2)}) collective-permute-start(bf16[128,2048]{1,0:T(8,128)(2,1)S(1)} %pad_maximum_fusion.13), channel_id=1, source_target_pairs={{0,4},{1,5},{2,6},{3,7},{4,0},{5,1},{6,2},{7,3},{8,12},{9,13},{10,... | collective-permute-start | bytes 1572872 | tf_op jit(solution)/shard_map/ppermute | solution.py:55
  467.8 17.1 %all-to-all-start.1 = ((bf16[8,65,768]{2,1,0:T(8,128)(2,1)}), bf16[8,65,768]{2,1,0:T(8,128)(2,1)S(1)}, u32[]{:S(2)}, u32[]{:S(2)}) async-start(bf16[8,65,768]{2,1,0:T(8,128)(2,1)} %pad_maximum_fusion.1), calls=%async_computation.4 | async-start | bytes 1769472 | tf_op jit(solution)/shard_map/all_to_all | solution.py:688
  (66 other events, 490.9 us)
Sparse Core Ops, SparseCore 0:
  11.0 83.4 all-gather.3
  96.7 96.5 all-gather.5
  195.4 53.1 all-gather.7
  250.8 50.8 reduce-scatter.4
  303.9 93.4 reduce-scatter.6
  399.5 61.6 reduce-scatter.8
  463.6 27.2 reduce-scatter.10
